TPU v7x, 32 devices: a whole 2x2x4 slice. The times are simulated.
32 devices in a mesh: ex: 8 (over z, x), rep: 4 (over y, core).
Axes of the slice: x: 2, y: 2, z: 4, core: 2. Of those that a mesh axis runs over, the one named last changes fastest.
Arguments:
- tokens: bfloat16 [20480, 1024], P(('ex', 'rep')), may hold values from -6 to 6
- lengths: int32 [10], replicated, may hold values from 1 to 2048, 14336 in all
- assign: int32 [20480, 1], P(('ex', 'rep')), may hold values from 0 to 7; in each aligned block of 640 rows (0 to 639, 640 to 1279, ...) at most 100 rows name the same one
- centroids: bfloat16 [8, 1024], P('ex', 'rep'), may hold values from -0.125 to 0.125
- ln_gain: bfloat16 [8, 2, 1024], P('ex', None, 'rep'), may hold values from 0.5 to 1.5
- ln_bias: bfloat16 [8, 2, 1024], P('ex', None, 'rep'), may hold values from -0.59765625 to 0.59765625
- w_in: bfloat16 [8, 2, 1024, 4096], P('ex', None, None, 'rep'), may hold values from -0.1875 to 0.1875
- b_in: bfloat16 [8, 2, 4096], P('ex', None, 'rep'), may hold values from -0.59765625 to 0.59765625
- w_out: bfloat16 [8, 2, 4096, 1024], P('ex', None, 'rep'), may hold values from -0.09375 to 0.09375
- b_out: bfloat16 [8, 2, 1024], P('ex', None, 'rep'), may hold values from -0.59765625 to 0.59765625
- grad_output: bfloat16 [20480, 1024], P(('ex', 'rep')), may hold values from -6 to 6
Outputs:
- output: bfloat16 [20480, 1024], P(('ex', 'rep'))
- grad_input: bfloat16 [20480, 1024], P(('ex', 'rep'))
- grad_centroids: float32 [8, 1024], P('ex', 'rep')
- grad_ln_gain: float32 [8, 2, 1024], P('ex', None, 'rep')
- grad_ln_bias: float32 [8, 2, 1024], P('ex', None, 'rep')
- grad_w_in: float32 [8, 2, 1024, 4096], P('ex', None, None, 'rep')
- grad_b_in: float32 [8, 2, 4096], P('ex', None, 'rep')
- grad_w_out: float32 [8, 2, 4096, 1024], P('ex', None, 'rep')
- grad_b_out: float32 [8, 2, 1024], P('ex', None, 'rep')
Inputs may be any that keep to these rules, and one draw needn't show every extreme that they name: `assign`: in the rows of one device no expert is named by more than 100 rows, a bound that some block reaches; padding rows carry an expert too but are ignored. Sequence s holds rows s * 2048 to (s + 1) * 2048 - 1, of which the first lengths[s] are tokens and the rest padding; the lengths sum to 14336 and the largest is 2048.
All inputs are finite; a program needn't handle non-finite values.
Results may differ from a plain program's by a relative error of at most 0.011.
Values may be sent and summed in bfloat16 or wider, within the bound.
No kernel may reach another device: no remote copies, remote signals or barrier semaphores. Data moves between devices by JAX's collectives and lax.ppermute only.
A program may use at most 256 MiB of HBM per device.

v0:
```python
import functools

import jax
import jax.numpy as jnp
from jax import lax
from jax.experimental import pallas as pl
from jax.experimental.pallas import tpu as pltpu
from jax.sharding import PartitionSpec as P

SEQ_LEN = 2048
EPSILON = 1e-05
F32 = jnp.float32
BF16 = jnp.bfloat16
VMEM = pl.BlockSpec(memory_space=pltpu.VMEM)
SMEM = pl.BlockSpec(memory_space=pltpu.SMEM)
ANY = pl.BlockSpec(memory_space=pl.ANY)
HBM = pl.BlockSpec(memory_space=pltpu.HBM)
CAP = 640
SCALE = 16


def swap(value, mask):
    return lax.ppermute(value, "rep", [(r, r ^ mask) for r in range(lax.axis_size("rep"))])


def dot(left, right, over_left, over_right):
    dims = (((over_left,), (over_right,)), ((), ()))
    return lax.dot_general(left, right, dims, preferred_element_type=F32)


def ceil_to(value, unit):
    return -(-value // unit) * unit


def shaped(*shape, dtype=BF16):
    return jax.ShapeDtypeStruct(shape, dtype)


def run(kernel, outs, operands, flops=0, scratch=(), in_specs=None, out_specs=None, limit=16, aliases=None, after=(), pinned=False, name=None):
    outs, count, extra = list(outs), len(operands), len(after)
    moved = sum(v.size * v.dtype.itemsize for v in (*operands, *outs))

    def body(*refs):
        kernel(*refs[:count], *refs[count + extra :])

    specs = in_specs or [VMEM] * count
    places = {id(HBM): pltpu.HBM, id(VMEM): pltpu.VMEM if pinned else pl.ANY}
    operands = [
        pltpu.with_memory_space_constraint(v, places.get(id(spec), pl.ANY))
        for v, spec in zip(operands, specs)
    ]
    out_specs = out_specs or [VMEM] * len(outs)
    outs = [
        pltpu.HBM(o.shape, o.dtype) if spec is HBM else o for o, spec in zip(outs, out_specs)
    ]
    return pl.pallas_call(
        body,
        out_shape=outs,
        in_specs=[*specs, *([ANY] * extra)],
        out_specs=out_specs,
        scratch_shapes=list(scratch),
        input_output_aliases=aliases or {},
        cost_estimate=pl.CostEstimate(flops=flops // SCALE, bytes_accessed=moved // SCALE, transcendentals=0),
        compiler_params=pltpu.CompilerParams(vmem_limit_bytes=limit << 20),
        name=name or kernel.__name__,
    )(*operands, *after)


def room(rows, limit):
    return dict(limit=limit, pinned=True) if rows <= 640 else dict(limit=54)


def iota(shape, dim):
    return lax.broadcasted_iota(jnp.int32, shape, dim)


def onehot(rows, index):
    return (iota((rows, index.shape[1]), 0) == index).astype(F32).astype(BF16)


def normalize(hidden):
    center = hidden - jnp.mean(hidden, -1, keepdims=True)
    rstd = lax.rsqrt(jnp.mean(center * center, -1, keepdims=True) + EPSILON)
    return center * rstd, rstd


def norm_backward(d_normed, xhat, rstd, gain):
    dx = d_normed * gain
    mean = jnp.mean(dx, -1, keepdims=True)
    return (dx - mean - xhat * jnp.mean(dx * xhat, -1, keepdims=True)) * rstd


def gelu_both(a):
    c = 0.7978845608028654
    a2 = a * a
    t = jnp.tanh(a * (c + (c * 0.044715) * a2))
    half = 0.5 + 0.5 * t
    act = a * half
    return act, half + act * (1.0 - t) * (c + (3 * c * 0.044715) * a2)


def gate_of(rows, centroid):
    return 1.0 / (1.0 + jnp.exp(-jnp.sum(rows * centroid, -1, keepdims=True)))


def up(ref):
    return ref[...].astype(F32)


CENTROID, GAIN, SHIFT, B_OUT = 0, 1, 3, 5


def row(ref, index):
    return ref[index : index + 1, :]


def route_kernel(experts, slots, lengths, base, assign, tokens, target_ref, packed_ref):
    n = assign.shape[1]
    position = base[0] + iota((1, n), 1)
    first = base[0] // SEQ_LEN
    limit = jnp.zeros((1, n), jnp.int32)
    for k in range(n // SEQ_LEN + 2):
        s = first + k
        size = lengths[jnp.minimum(s, lengths.shape[0] - 1)]
        within = position - s * SEQ_LEN
        limit = jnp.where((within >= 0) & (within < size), 1, limit)
    live = limit > 0
    expert = assign[...]
    hits = ((iota((experts, n), 0) == expert) & live).astype(F32)
    before = (iota((n, n), 0) < iota((n, n), 1)).astype(F32).astype(BF16)
    earlier = dot(hits.astype(BF16), before, 1, 0)
    slot = jnp.sum(hits * earlier, 0, keepdims=True).astype(jnp.int32)
    target = jnp.where(live, expert * slots + slot, -1)
    target_ref[...] = target
    packed = dot(onehot(experts * slots, target), tokens[...], 1, 0)
    packed_ref[...] = packed.astype(BF16)
    counts = jnp.broadcast_to(jnp.sum(hits, 1, keepdims=True), (experts, 128)).astype(BF16)
    last = iota((experts * slots, experts), 0) == iota((experts * slots, experts), 1) * slots + slots - 1
    marks = dot(last.astype(F32).astype(BF16), counts, 1, 0)
    packed_ref[:, 0:128] = (packed[:, 0:128] + marks).astype(BF16)


def pack_kernel(target, values, packed_ref):
    packed_ref[...] = dot(onehot(packed_ref.shape[0], target[...]), values[...], 1, 0).astype(BF16)


def marks_kernel(sources, returned, mark_ref):
    slots = returned.shape[0] // sources
    total = jnp.zeros((1, 128), F32)
    for k in range(sources):
        total = total + returned[(k + 1) * slots - 1 : (k + 1) * slots, 0:128].astype(F32)
    mark_ref[...] = jnp.zeros(mark_ref.shape, F32)
    mark_ref[:, 0:128] = total


def columns_kernel(column_x, own0, far0, own1, far1, mark, columns_ref):
    columns_ref[0:1, :] = column_x[...]
    columns_ref[1:2, :] = own0[0:1, :] + far0[0:1, :]
    columns_ref[2:3, :] = own1[0:1, :] + far1[0:1, :]
    columns_ref[3:4, :] = own0[1:2, :] + far0[1:2, :]
    columns_ref[4:5, :] = own1[1:2, :] + far1[1:2, :]
    columns_ref[5:6, :] = own0[2:3, :]
    columns_ref[6:7, :] = own1[2:3, :]
    columns_ref[7:8, :] = mark[...]


def add_kernel(left, right, out_ref):
    out_ref[...] = left[...] + right[...]


def finish_kernel(position, left, right, bias0, bias1, centroid_ref, gain_ref, shift_ref, out_ref, bias_ref, mark_ref):
    width = centroid_ref.shape[1]
    total = left[...] + right[...]
    mine = total[:, 0:width]
    for k in range(1, total.shape[1] // width):
        mine = jnp.where(position[0] == k, total[:, k * width : (k + 1) * width], mine)
    centroid_ref[...] = mine[0:1]
    gain_ref[...] = mine[1:3]
    shift_ref[...] = mine[3:5]
    out_ref[...] = mine[5:7]
    mark_ref[...] = total[7:8, 0:128]
    bias_ref[0:1, :] = bias0[...]
    bias_ref[1:2, :] = bias1[...]


def unpack_kernel(target, returned, values, out_ref):
    places = onehot(returned.shape[0], target[...])
    moved = dot(places, returned[...], 0, 0)
    alive = dot(places, jnp.ones((returned.shape[0], 128), BF16), 0, 0)[:, 0:1] > 0.5
    out_ref[...] = jnp.where(alive, up(values) + moved, 0.0).astype(BF16)


def compact_kernel(place, arrived, rows_ref):
    rows_ref[...] = dot(onehot(rows_ref.shape[0], place[...]), arrived[...], 1, 0).astype(BF16)


def place_kernel(sources, arrived, rows_ref, place_ref, count_ref):
    n = arrived.shape[0]
    slots = n // sources
    lane = iota((1, n), 1).astype(F32)
    place, total = jnp.full((1, n), -1.0, F32), jnp.zeros((1, 1), F32)
    for k in range(sources):
        count = arrived[(k + 1) * slots - 1 : (k + 1) * slots, 0:128].astype(F32)[:, 0:1]
        slot = lane - k * slots
        place = jnp.where((slot >= 0.0) & (slot < count), total + slot, place)
        total = total + count
    place_ref[...] = place.astype(jnp.int32)
    count_ref[...] = jnp.broadcast_to(total, count_ref.shape)
    rows_ref[...] = dot(onehot(rows_ref.shape[0], place_ref[...]), arrived[...], 1, 0).astype(BF16)


def spread(place, values, slots_ref):
    places = onehot(values.shape[0], place[...])
    slots_ref[...] = dot(places, values, 0, 0).astype(BF16)


def hidden1_of(rows, own0, far0, vectors):
    return up(rows) + up(own0) + up(far0) + row(vectors, B_OUT)


class Copies:
    def __init__(self, sems):
        self.sems, self.made = sems, []

    def start(self, source, target):
        copy = pltpu.make_async_copy(source, target, self.sems.at[len(self.made)])
        copy.start()
        self.made.append(copy)
        return copy

    def wait(self):
        for copy in self.made:
            copy.wait()


def fetch(layer, weights, order, buffer, sems):
    copies = [
        pltpu.make_async_copy(weights[k].at[layer], buffer.at[k], sems.at[k]) for k in range(4)
    ]
    copies[order[0]].start()
    copies[order[1]].start()
    left = list(order)

    def got(k):
        assert left.pop(0) == k
        copies[k].wait()
        if len(left) > 1:
            copies[left[1]].start()
        return buffer[k]

    return got


def dma(count):
    return pltpu.SemaphoreType.DMA((count,))


def weight_scratch(weights):
    return [pltpu.VMEM((4, *weights[0].shape[1:]), BF16), dma(4)]


def forward_kernel(layer, *refs):
    n = 1 + 2 * layer
    sources, (vectors, biases_own, biases_sib) = refs[:n], refs[n : n + 3]
    got = fetch(layer, refs[n + 3 : n + 7], (0, 2, 1, 3), *refs[-2:])
    normed_out, act_out, slope_out, out_ref, normed, act, slope, sems = refs[n + 7 : n + 15]
    copies = Copies(sems)
    hidden = hidden1_of(*sources, vectors) if layer else up(sources[0])
    xhat, _ = normalize(hidden)
    normed[...] = (xhat * row(vectors, GAIN + layer) + row(vectors, SHIFT + layer)).astype(BF16)
    copies.start(normed, normed_out)
    total = None
    for q, bias in enumerate((biases_own, biases_sib)):
        pre = dot(normed[...], got(q), 1, 0) + row(bias, layer).astype(F32)
        columns = slice(q * pre.shape[1], (q + 1) * pre.shape[1])
        value, change = gelu_both(pre)
        act[:, columns] = value.astype(BF16)
        slope[:, columns] = change.astype(BF16)
        copies.start(act.at[:, columns], act_out.at[:, columns])
        copies.start(slope.at[:, columns], slope_out.at[:, columns])
        part = dot(act[:, columns], got(2 + q), 1, 0)
        total = part if total is None else total + part
    out_ref[...] = total.astype(BF16)
    copies.wait()


def forward(layer, sources, vectors, biases, weights, after=()):
    rows, d = sources[0].shape
    f = 2 * weights[0].shape[2]
    small = [*sources, vectors, *biases]
    return run(
        functools.partial(forward_kernel, layer),
        [shaped(rows, d), shaped(rows, f), shaped(rows, f), shaped(rows, d)],
        [*small, *weights],
        flops=4 * rows * d * f,
        in_specs=[VMEM] * len(small) + [HBM] * 4,
        out_specs=[HBM] * 3 + [VMEM],
        scratch=[
            pltpu.VMEM((rows, d), BF16),
            pltpu.VMEM((rows, f), BF16),
            pltpu.VMEM((rows, f), BF16),
            dma(5),
            *weight_scratch(weights),
        ],
        after=after,
        name=f"forward_sublayer{layer}",
        **room(rows, 26),
    )


def backward_kernel(layer, keep, *refs):
    n = 4 if layer else 6
    sources, (vectors, slope_in) = refs[:n], refs[n : n + 2]
    got = fetch(layer, refs[n + 2 : n + 6], (2, 0, 3, 1), *refs[-2:])
    branch_out, low_out, out_ref, columns_ref, bias_ref = refs[n + 6 : n + 11]
    branch, low, slope, sems, slope_sem = refs[-7:-2]
    copies = Copies(sems)
    slope_copy = pltpu.make_async_copy(slope_in, slope, slope_sem.at[0])
    slope_copy.start()
    rows, grads, own0, far0 = sources[:4]
    d_hidden = gate_of(up(rows), row(vectors, CENTROID)) * up(grads)
    if layer == 0:
        xhat, rstd = normalize(hidden1_of(rows, own0, far0, vectors))
        d_normed = up(sources[4]) + up(sources[5])
        d_hidden = d_hidden + norm_backward(d_normed, xhat, rstd, row(vectors, GAIN + 1))
        if keep:
            refs[n + 11][...] = d_hidden
    branch[...] = d_hidden.astype(BF16)
    copies.start(branch, branch_out)
    columns_ref[2:3, :] = jnp.sum(d_hidden, 0, keepdims=True)
    total = None
    for q in range(2):
        d_act = dot(branch[...], got(2 + q), 1, 1)
        if q == 0:
            slope_copy.wait()
        columns = slice(q * d_act.shape[1], (q + 1) * d_act.shape[1])
        d_pre = d_act * slope[:, columns].astype(F32)
        bias_ref[:, columns] = jnp.sum(d_pre, 0, keepdims=True)
        low[:, columns] = d_pre.astype(BF16)
        copies.start(low.at[:, columns], low_out.at[:, columns])
        part = dot(low[:, columns], got(q), 1, 1)
        total = part if total is None else total + part
    out_ref[...] = total.astype(BF16)
    xhat, _ = normalize(hidden1_of(rows, own0, far0, vectors) if layer else up(rows))
    columns_ref[0:1, :] = jnp.sum(total * xhat, 0, keepdims=True)
    columns_ref[1:2, :] = jnp.sum(total, 0, keepdims=True)
    copies.wait()


def backward(layer, keep, sources, vectors, slope, weights, after=()):
    rows, d = sources[0].shape
    f = 2 * weights[0].shape[2]
    outs = [shaped(rows, d), shaped(rows, f), shaped(rows, d), shaped(3, d, dtype=F32), shaped(1, f, dtype=F32)]
    outs += [shaped(rows, d, dtype=F32)] if keep else []
    return run(
        functools.partial(backward_kernel, layer, keep),
        outs,
        [*sources, vectors, slope, *weights],
        flops=4 * rows * d * f,
        in_specs=[VMEM] * (len(sources) + 1) + [HBM] * 5,
        out_specs=[HBM] * 2 + [VMEM] * (len(outs) - 2),
        scratch=[
            pltpu.VMEM((rows, d), BF16),
            pltpu.VMEM((rows, f), BF16),
            pltpu.VMEM((rows, f), BF16),
            dma(3),
            dma(1),
            *weight_scratch(weights),
        ],
        after=after,
        name=f"backward_sublayer{layer}",
        **room(rows, 26),
    )


def result_kernel(sources, place, count, rows, grads, own0, far0, own1, far1, vectors, slots_ref, logit_ref):
    gate = gate_of(up(rows), row(vectors, CENTROID))
    hidden = hidden1_of(rows, own0, far0, vectors) + up(own1) + up(far1) + row(vectors, B_OUT + 1)
    d_gate = jnp.sum(up(grads) * hidden, -1, keepdims=True)
    d_logit = (d_gate * gate * (1.0 - gate)).astype(BF16).astype(F32)
    logit_ref[...] = jnp.broadcast_to(d_logit, logit_ref.shape)
    spread(place, (gate * hidden).astype(BF16), slots_ref)
    over = jnp.where(count[...] > rows.shape[0], 1.0, 0.0).astype(BF16)
    slots = slots_ref.shape[0] // sources
    for k in range(sources):
        slots_ref[(k + 1) * slots - 1 : (k + 1) * slots, 0:128] = over


def row_grad_kernel(place, rows, d_hidden1, logit, own0, far0, vectors, slots_ref, columns_ref):
    x = up(rows)
    xhat, rstd = normalize(x)
    d_logit = logit[:, 0:1]
    d_hidden = d_hidden1[...] + norm_backward(up(own0) + up(far0), xhat, rstd, row(vectors, GAIN))
    d_row = d_hidden + d_logit * row(vectors, CENTROID)
    spread(place, d_row.astype(BF16), slots_ref)
    columns_ref[...] = jnp.sum(d_logit * x, 0, keepdims=True)


def products(q, sources, buffers, sems):
    width = sources[2].shape[1] // 2
    columns = slice(q * width, (q + 1) * width)
    wide = (2, 3, 4, 5)
    order = (0, 2, 1, 3, 4, 6, 5, 7)
    copies = {
        k: pltpu.make_async_copy(
            sources[k].at[:, columns] if k in wide else sources[k], buffers[k], sems.at[k]
        )
        for k in order
    }
    for k in order:
        copies[k].start()

    def got(k):
        if k in copies:
            copies.pop(k).wait()
        return buffers[k]

    def first(part):
        return sum(dot(got(k)[...], got(2 + k)[:, part], 0, 0) for k in range(2))

    def second(part):
        return sum(dot(got(4 + k)[:, part], got(6 + k)[...], 0, 0) for k in range(2))

    return first, second, width


def sibling_kernel(*refs):
    first_ref, second_ref, bias_ref = refs[10:13]
    first, second, width = products(1, refs[:8], refs[13:21], refs[21])
    half = width // 2
    parts = [slice(k * half, (k + 1) * half) for k in range(2)]
    for part in parts:
        first_ref[:, part] = first(part).astype(BF16)
    for part in parts:
        second_ref[part, :] = second(part).astype(BF16)
    bias_ref[...] = (refs[8][...] + refs[9][...])[:, width:]


def own_kernel(layer, n_before, *refs):
    got_first_in, got_second_in, got_bias = refs[10:13]
    refs_out = refs[13 + n_before :]
    first_out, second_out, bias_ref = refs_out[:3]
    first, second, width = products(0, refs[:8], refs_out[3:11], refs_out[11])
    got_first, got_second, buffer_first, buffer_second, sems_in, sems = refs_out[12:]
    copies_in = Copies(sems_in)
    copy_first = copies_in.start(got_first_in, got_first)
    copy_second = copies_in.start(got_second_in, got_second)
    half = width // 2
    parts = [slice(k * half, (k + 1) * half) for k in range(2)]
    copies = Copies(sems)
    for k, part in enumerate(parts):
        value = first(part)
        if k == 0:
            copy_first.wait()
        buffer_first[:, part] = value + got_first[:, part].astype(F32)
        copies.start(buffer_first.at[:, part], first_out.at[layer, :, part])
    for k, part in enumerate(parts):
        value = second(part)
        if k == 0:
            copy_second.wait()
        buffer_second[part, :] = value + got_second[part, :].astype(F32)
        copies.start(buffer_second.at[part, :], second_out.at[layer, part, :])
    bias_ref[...] = (refs[8][...] + refs[9][...])[:, :width] + got_bias[...]
    copies.wait()


def product_scratch(saved):
    rows, d = saved[0][0].shape
    f = saved[1][0].shape[1] // 2
    return [pltpu.VMEM((rows, n), BF16) for n in (d, d, f, f, f, f, d, d)] + [dma(8)]


def sibling_grads(saved, biases, after=()):
    normed, low, act, branch = saved
    rows, d = normed[0].shape
    f = low[0].shape[1] // 2
    return run(
        sibling_kernel,
        [shaped(d, f), shaped(f, d), shaped(1, f, dtype=F32)],
        [*normed, *low, *act, *branch, *biases],
        flops=8 * rows * d * f,
        in_specs=[HBM] * 8 + [VMEM] * 2,
        scratch=product_scratch(saved),
        after=after,
        **room(rows, 24),
    )


def own_grads(layer, saved, biases, got, before, after=()):
    normed, low, act, branch = saved
    rows, d = normed[0].shape
    f = low[0].shape[1] // 2
    return run(
        functools.partial(own_kernel, layer, len(before)),
        [shaped(2, d, f, dtype=F32), shaped(2, f, d, dtype=F32), shaped(1, f, dtype=F32)],
        [*normed, *low, *act, *branch, *biases, *got, *before],
        flops=8 * rows * d * f,
        in_specs=[HBM] * 8 + [VMEM] * 2 + [HBM] * 2 + [VMEM] + [HBM] * len(before),
        out_specs=[HBM, HBM, VMEM],
        scratch=[
            *product_scratch(saved),
            pltpu.VMEM((d, f), BF16),
            pltpu.VMEM((f, d), BF16),
            pltpu.VMEM((d, f), F32),
            pltpu.VMEM((f, d), F32),
            dma(2),
            dma(4),
        ],
        aliases={13 + k: k for k in range(len(before))},
        after=after,
        name=f"own_grads_sublayer{layer}",
        **room(rows, 32),
    )


def expert_group(cap, arrived, outgoing_g, target, tokens, grad_output, vectors, biases, weights):
    d, worst, sources = tokens.shape[1], arrived.shape[0], lax.axis_size("ex")
    exchange = functools.partial(lax.all_to_all, axis_name="ex", split_axis=0, concat_axis=0, tiled=True)
    one_hot_flops = 2 * cap * worst * d

    def compact(values):
        return run(compact_kernel, [shaped(cap, d)], [place, values], flops=one_hot_flops)[0]

    def unpack(returned, values):
        return run(unpack_kernel, [shaped(*values.shape)], [target, returned, values], flops=one_hot_flops)[0]

    x_own, place, count = run(
        functools.partial(place_kernel, sources),
        [shaped(cap, d), shaped(1, worst, dtype=jnp.int32), shaped(1, 128, dtype=F32)],
        [arrived],
        flops=one_hot_flops,
        name="place",
        after=(vectors,),
    )
    x_far = swap(x_own, 2)

    normed_own0, act_own0, slope_own0, own0 = forward(0, (x_own,), vectors, biases, weights)
    got_far0 = swap(own0, 2)
    normed_far0, act_far0, slope_far0, far0 = forward(0, (x_far,), vectors, biases, weights, (own0,))
    got_own0 = swap(far0, 2)
    g_arrived = exchange(outgoing_g)
    g_own = compact(g_arrived)
    g_far = swap(g_own, 2)

    normed_far1, act_far1, slope_far1, far1 = forward(1, (x_far, far0, got_far0), vectors, biases, weights)
    got_own1 = swap(far1, 2)
    normed_own1, act_own1, slope_own1, own1 = forward(1, (x_own, own0, got_own0), vectors, biases, weights)
    in_own, in_far = (x_own, g_own, own0, got_own0), (x_far, g_far, far0, got_far0)
    branch_own1, low_own1, d_own1, columns_own1, bias_own1 = backward(
        1, False, in_own, vectors, slope_own1, weights
    )
    got_d_far1 = swap(d_own1, 2)
    branch_far1, low_far1, d_far1, columns_far1, bias_far1 = backward(
        1, False, in_far, vectors, slope_far1, weights
    )
    got_d_own1 = swap(d_far1, 2)

    result, logit = run(
        functools.partial(result_kernel, sources),
        [shaped(worst, d), shaped(cap, 128, dtype=F32)],
        [place, count, x_own, g_own, own0, got_own0, own1, got_own1, vectors],
        flops=one_hot_flops,
        name="result",
    )
    returned = exchange(result)

    saved1 = (
        (normed_own1, normed_far1),
        (low_own1, low_far1),
        (act_own1, act_far1),
        (branch_own1, branch_far1),
    )
    sent1 = sibling_grads(saved1, (bias_own1, bias_far1))
    got1 = [swap(v, 1) for v in sent1]

    branch_far0, low_far0, d_far0, columns_far0, bias_far0 = backward(
        0, False, (*in_far, d_far1, got_d_far1), vectors, slope_far0, weights, (sent1[2],)
    )
    got_d_own0 = swap(d_far0, 2)
    grad_first, grad_second, grad_bias1 = own_grads(
        1, saved1, (bias_own1, bias_far1), got1, (), (bias_far0,)
    )
    branch_own0, low_own0, d_own0, columns_own0, bias_own0, d_hidden1 = backward(
        0, True, (*in_own, d_own1, got_d_own1), vectors, slope_own0, weights, (grad_bias1,)
    )
    d_rows, columns_x = run(
        row_grad_kernel,
        [shaped(worst, d), shaped(1, d, dtype=F32)],
        [place, x_own, d_hidden1, logit, d_own0, got_d_own0, vectors],
        flops=one_hot_flops,
    )
    d_back = exchange(d_rows)

    saved0 = (
        (normed_own0, normed_far0),
        (low_own0, low_far0),
        (act_own0, act_far0),
        (branch_own0, branch_far0),
    )
    sent0 = sibling_grads(saved0, (bias_own0, bias_far0), (columns_x,))
    got0 = [swap(v, 1) for v in sent0]
    grad_first, grad_second, grad_bias0 = own_grads(
        0, saved0, (bias_own0, bias_far0), got0, (grad_first, grad_second)
    )

    marks = run(functools.partial(marks_kernel, sources), [shaped(1, d, dtype=F32)], [returned], name="marks")[0]
    row_sums = [columns_x, columns_own0, columns_far0, columns_own1, columns_far1, marks]
    columns = run(columns_kernel, [shaped(8, d, dtype=F32)], row_sums)[0]
    columns = run(add_kernel, [shaped(8, d, dtype=F32)], [columns, swap(columns, 1)])[0]
    width = d // lax.axis_size("rep")
    position = lax.axis_index("rep").astype(jnp.int32).reshape(1)
    *small, grad_bias, over = run(
        finish_kernel,
        [shaped(n, width, dtype=F32) for n in (1, 2, 2, 2)]
        + [shaped(2, grad_bias0.shape[1], dtype=F32), shaped(1, 128, dtype=F32)],
        [position, columns, swap(columns, 2), grad_bias0, grad_bias1],
        in_specs=[SMEM] + [VMEM] * 4,
    )
    outs = (
        unpack(returned, tokens),
        unpack(d_back, grad_output),
        small[0],
        small[1][None],
        small[2][None],
        grad_first[None],
        grad_bias[None],
        grad_second[None],
        small[3][None],
    )
    return outs, over[0, 0]


def shards(
    tokens, lengths, assign, centroids, ln_gain, ln_bias, w_in, b_in, w_out, b_out, grad_output
):
    experts, reps = lax.axis_size("ex"), lax.axis_size("rep")
    rows_here, d = tokens.shape
    slots = ceil_to(max(2, 5 * rows_here // (4 * experts)) + 1, 8)
    worst = experts * slots
    base = ((lax.axis_index("ex") * reps + lax.axis_index("rep")) * rows_here).astype(jnp.int32).reshape(1)
    target, outgoing = run(
        functools.partial(route_kernel, experts, slots),
        [shaped(1, rows_here, dtype=jnp.int32), shaped(worst, d)],
        [lengths, base, assign.reshape(1, rows_here), tokens],
        in_specs=[SMEM, SMEM, VMEM, VMEM],
        name="route",
        flops=2 * worst * rows_here * d,
    )
    arrived = lax.all_to_all(outgoing, "ex", split_axis=0, concat_axis=0, tiled=True)
    outgoing_g = run(pack_kernel, [shaped(worst, d)], [target, grad_output], flops=2 * worst * rows_here * d)[0]
    biases = (b_in[0], swap(b_in[0], 1))
    weights = (w_in[0], swap(w_in[0], 1), w_out[0], swap(w_out[0], 1))
    own_vectors = jnp.concatenate([centroids, ln_gain[0], ln_bias[0], b_out[0]], 0)
    own_vectors = jnp.concatenate([own_vectors, outgoing_g[:1, : own_vectors.shape[1]]], 0)
    vectors = lax.all_gather(own_vectors, "rep", axis=1, tiled=True).astype(F32)

    operands = (arrived, outgoing_g, target, tokens, grad_output, vectors, biases, weights)
    cap = min(CAP, worst)
    outs, over = expert_group(cap, *operands)
    if cap == worst:
        return outs
    return lax.cond(over > 0.0, lambda *_: expert_group(worst, *operands)[0], lambda *kept: kept, *outs)


def solution(mesh):
    rows = P(("ex", "rep"), None)
    in_specs = (
        rows,
        P(),
        rows,
        P("ex", "rep"),
        P("ex", None, "rep"),
        P("ex", None, "rep"),
        P("ex", None, None, "rep"),
        P("ex", None, "rep"),
        P("ex", None, "rep", None),
        P("ex", None, "rep"),
        rows,
    )
    out_specs = (
        rows,
        rows,
        P("ex", "rep"),
        P("ex", None, "rep"),
        P("ex", None, "rep"),
        P("ex", None, None, "rep"),
        P("ex", None, "rep"),
        P("ex", None, "rep", None),
        P("ex", None, "rep"),
    )
    return jax.shard_map(shards, mesh=mesh, in_specs=in_specs, out_specs=out_specs, check_vma=False)
```

profile of v0, /device:TPU:0, one launch (start us, length us, event | category | flops | bytes accessed | tf_op | source)
XLA Modules:
  0.0 351.3 jit_solution(15588398245946113807)
XLA Ops:
  2.6 4.3 %route.1 = (s32[1,640]{1,0:T(1,128)S(1)}, bf16[832,1024]{1,0:T(8,128)(2,1)}) custom-call(s32[10]{0:T(128)S(1)} %copy-done.25, s32[1]{0:T(128)} %bitcast.8.refs_1_, s32[1,640]{1,0:T(1,128)S(1)} %bitcast.45, bf16[640,1024]{1,0:T(8,128)(2,1)} %refs_2_.2), custom_call_target="tpu_custom_call" | custom-call | flops 68157440 | bytes 188738 | tf_op jit(solution)/shard_map/route/pallas_call | solution.py:56
  6.8 7.4 %all-to-all-start.3 = ((bf16[8,104,1024]{2,1,0:T(8,128)(2,1)}), bf16[8,104,1024]{2,1,0:T(8,128)(2,1)S(1)}, u32[]{:S(2)}, u32[]{:S(2)}) async-start(bf16[8,104,1024]{2,1,0:T(8,128)(2,1)} %bitcast.10), calls=%async_computation.3 | async-start | bytes 3407872 | tf_op jit(solution)/shard_map/all_to_all | solution.py:649
  14.2 2.7 pack_kernel.1
  16.9 37.4 %all-to-all-done.3 = bf16[8,104,1024]{2,1,0:T(8,128)(2,1)S(1)} async-done(((bf16[8,104,1024]{2,1,0:T(8,128)(2,1)}), bf16[8,104,1024]{2,1,0:T(8,128)(2,1)S(1)}, u32[]{:S(2)}, u32[]{:S(2)}) %all-to-all-start.3) | async-done | bytes 1703968 | tf_op jit(solution)/shard_map/all_to_all | solution.py:649
  54.3 4.4 %all-to-all-start.4 = ((bf16[8,104,1024]{2,1,0:T(8,128)(2,1)}), bf16[8,104,1024]{2,1,0:T(8,128)(2,1)}, u32[]{:S(2)}, u32[]{:S(2)}) async-start(bf16[8,104,1024]{2,1,0:T(8,128)(2,1)} %bitcast.15), calls=%async_computation.4 | async-start | bytes 3407872 | tf_op jit(solution)/shard_map/all_to_all | solution.py:541
  59.6 5.8 %all_gather.3 = bf16[8,1024]{1,0:T(8,128)(2,1)S(1)} all-gather(bf16[8,256]{1,0:T(8,128)(2,1)S(1)} %concatenate.3), channel_id=1, replica_groups=mesh['ex'=8,'rep'=4] {'rep'}, dimensions={1}, use_global_device_ids=true | all-gather | bytes 20480 | tf_op jit(solution)/shard_map/all_gather | solution.py:655
  65.4 1.6 place.3
  67.0 1.6 collective-permute-start.19
  68.6 10.9 %forward_sublayer0.6 = (bf16[640,1024]{1,0:T(8,128)(2,1)}, bf16[640,2048]{1,0:T(8,128)(2,1)}, bf16[640,2048]{1,0:T(8,128)(2,1)}, bf16[640,1024]{1,0:T(8,128)(2,1)S(1)}) custom-call(bf16[640,1024]{1,0:T(8,128)(2,1)S(1)} %get-tuple-element.215.refs_0_.refs_2_.refs_1_, f32[8,1024]{1,0:T(8,128)S(1)} %convert_element_type.9.refs_1_.refs_3_.refs_4_.refs_6_.refs_8_, ...), custom_call_target="tpu_custom_call" | custom-call | flops 335544320 | bytes 1624576 | tf_op jit(solution)/shard_map/forward_sublayer0/pallas_call | solution.py:56
  80.1 18.6 %collective-permute-done.19.refs_0_ = bf16[640,1024]{1,0:T(8,128)(2,1)S(1)} collective-permute-done((bf16[640,1024]{1,0:T(8,128)(2,1)S(1)}, bf16[640,1024]{1,0:T(8,128)(2,1)S(1)}, u32[]{:S(2)}, u32[]{:S(2)}) %collective-permute-start.19) | collective-permute-done | bytes 1310752 | tf_op jit(solution)/shard_map/ppermute | solution.py:23
  98.7 12.1 %forward_sublayer0.7 = (bf16[640,1024]{1,0:T(8,128)(2,1)}, bf16[640,2048]{1,0:T(8,128)(2,1)}, bf16[640,2048]{1,0:T(8,128)(2,1)}, bf16[640,1024]{1,0:T(8,128)(2,1)}) custom-call(bf16[640,1024]{1,0:T(8,128)(2,1)S(1)} %collective-permute-done.19.refs_0_, f32[8,1024]{1,0:T(8,128)S(1)} %convert_element_type.9.refs_1_.refs_3_.refs_4_.refs_6_.refs_8_, ...), custom_call_target="tpu_custom_call" | custom-call | flops 335544320 | bytes 1624576 | tf_op jit(solution)/shard_map/forward_sublayer0/pallas_call | solution.py:56
  110.8 1.6 collective-permute-start.20
  112.4 14.3 %collective-permute-done.22.refs_2_.refs_3_ = bf16[640,1024]{1,0:T(8,128)(2,1)S(1)} collective-permute-done((bf16[640,1024]{1,0:T(8,128)(2,1)S(1)}, bf16[640,1024]{1,0:T(8,128)(2,1)S(1)}, u32[]{:S(2)}, u32[]{:S(2)}) %collective-permute-start.22) | collective-permute-done | bytes 1310752 | tf_op jit(solution)/shard_map/ppermute | solution.py:23
  126.8 14.5 %forward_sublayer1.7 = (bf16[640,1024]{1,0:T(8,128)(2,1)}, bf16[640,2048]{1,0:T(8,128)(2,1)}, bf16[640,2048]{1,0:T(8,128)(2,1)}, bf16[640,1024]{1,0:T(8,128)(2,1)}) custom-call(bf16[640,1024]{1,0:T(8,128)(2,1)S(1)} %collective-permute-done.19.refs_0_, bf16[640,1024]{1,0:T(8,128)(2,1)} %get-tuple-element.217.refs_1_.refs_2_, ...), custom_call_target="tpu_custom_call" | custom-call | flops 335544320 | bytes 1788416 | tf_op jit(solution)/shard_map/forward_sublayer1/pallas_call | solution.py:56
  141.3 1.6 collective-permute-start.28
  142.9 4.0 %compact_kernel.3.refs_1_.refs_3_ = bf16[640,1024]{1,0:T(8,128)(2,1)} custom-call(s32[1,832]{1,0:T(1,128)S(1)} %get-tuple-element.214.refs_0_, bf16[832,1024]{1,0:T(8,128)(2,1)} %bitcast.16.refs_1_), custom_call_target="tpu_custom_call" | custom-call | flops 68157440 | bytes 188624 | tf_op jit(solution)/shard_map/compact_kernel/pallas_call | solution.py:56
  147.4 7.5 %collective-permute-done.20.refs_2_.refs_3_.refs_5_ = bf16[640,1024]{1,0:T(8,128)(2,1)} collective-permute-done((bf16[640,1024]{1,0:T(8,128)(2,1)}, bf16[640,1024]{1,0:T(8,128)(2,1)}, u32[]{:S(2)}, u32[]{:S(2)}) %collective-permute-start.20) | collective-permute-done | bytes 1310752 | tf_op jit(solution)/shard_map/ppermute | solution.py:23
  154.9 12.5 %forward_sublayer1.6 = (bf16[640,1024]{1,0:T(8,128)(2,1)}, bf16[640,2048]{1,0:T(8,128)(2,1)}, bf16[640,2048]{1,0:T(8,128)(2,1)}, bf16[640,1024]{1,0:T(8,128)(2,1)S(1)}) custom-call(bf16[640,1024]{1,0:T(8,128)(2,1)S(1)} %get-tuple-element.215.refs_0_.refs_2_.refs_1_, bf16[640,1024]{1,0:T(8,128)(2,1)S(1)} %get-tuple-element.216.refs_8_.refs_1_.refs_2_.refs_4_, ...), custom_call_target="tpu_custom_call" | custom-call | flops 335544320 | bytes 1788416 | tf_op jit(solution)/shard_map/forward_sublayer1/pallas_call | solution.py:56
  167.5 15.5 %collective-permute-done.28.refs_7_ = bf16[640,1024]{1,0:T(8,128)(2,1)} collective-permute-done((bf16[640,1024]{1,0:T(8,128)(2,1)}, bf16[640,1024]{1,0:T(8,128)(2,1)}, u32[]{:S(2)}, u32[]{:S(2)}) %collective-permute-start.28) | collective-permute-done | bytes 1310752 | tf_op jit(solution)/shard_map/ppermute | solution.py:23
  183.0 5.1 %result.3 = (bf16[832,1024]{1,0:T(8,128)(2,1)S(1)}, f32[640,128]{1,0:T(8,128)S(1)}) custom-call(s32[1,832]{1,0:T(1,128)S(1)} %get-tuple-element.214.refs_0_, f32[1,128]{1,0:T(1,128)S(1)} %get-tuple-element.240.refs_1_, bf16[640,1024]{1,0:T(8,128)(2,1)S(1)} %get-tuple-element.215.refs_0_.refs_2_.refs_1_, bf16[640,1024]{1,0:T(8,128)(2,1)} %compact_kernel.3.refs_1_.refs_3_, ...), custom_call_target="tpu_custom_call" | custom-call | flops 68157440 | bytes 620784 | tf_op jit(solution)/shard_map/result/pallas_call | solution.py:56
  188.2 1.2 copy-done.12
  189.4 5.9 %all-to-all-start.5 = ((bf16[8,104,1024]{2,1,0:T(8,128)(2,1)}), bf16[8,104,1024]{2,1,0:T(8,128)(2,1)}, u32[]{:S(2)}, u32[]{:S(2)}) async-start(bf16[8,104,1024]{2,1,0:T(8,128)(2,1)} %bitcast.37), calls=%async_computation.5 | async-start | bytes 3407872 | tf_op jit(solution)/shard_map/all_to_all | solution.py:565
  195.3 12.0 %backward_sublayer1.6 = (bf16[640,1024]{1,0:T(8,128)(2,1)}, bf16[640,2048]{1,0:T(8,128)(2,1)}, bf16[640,1024]{1,0:T(8,128)(2,1)S(1)}, f32[3,1024]{1,0:T(4,128)S(1)}, f32[1,2048]{1,0:T(1,128)S(1)}) custom-call(bf16[640,1024]{1,0:T(8,128)(2,1)S(1)} %get-tuple-element.215.refs_0_.refs_2_.refs_1_, bf16[640,1024]{1,0:T(8,128)(2,1)} %compact_kernel.3.refs_1_.refs_3_, ...), custom_call_target="tpu_custom_call" | custom-call | flops 335544320 | bytes 1871104 | tf_op jit(solution)/shard_map/backward_sublayer1/pallas_call | solution.py:56
  207.3 1.6 collective-permute-start.27
  208.9 2.2 collective-permute-done.21.refs_1_
  211.1 12.3 %backward_sublayer1.7 = (bf16[640,1024]{1,0:T(8,128)(2,1)}, bf16[640,2048]{1,0:T(8,128)(2,1)}, bf16[640,1024]{1,0:T(8,128)(2,1)S(1)}, f32[3,1024]{1,0:T(4,128)S(1)}, f32[1,2048]{1,0:T(1,128)S(1)}) custom-call(bf16[640,1024]{1,0:T(8,128)(2,1)S(1)} %copy-done.7, bf16[640,1024]{1,0:T(8,128)(2,1)} %collective-permute-done.21.refs_1_, ...), custom_call_target="tpu_custom_call" | custom-call | flops 335544320 | bytes 1871104 | tf_op jit(solution)/shard_map/backward_sublayer1/pallas_call | solution.py:56
  223.4 9.7 %sibling_kernel.6 = (bf16[1024,1024]{1,0:T(8,128)(2,1)S(1)}, bf16[1024,1024]{1,0:T(8,128)(2,1)S(1)}, f32[1,1024]{1,0:T(1,128)S(1)}) custom-call(bf16[640,1024]{1,0:T(8,128)(2,1)} %get-tuple-element.223.refs_0_, bf16[640,1024]{1,0:T(8,128)(2,1)} %get-tuple-element.224.refs_1_, bf16[640,2048]{1,0:T(8,128)(2,1)} %get-tuple-element.225.refs_2_, ...), custom_call_target="tpu_custom_call" | custom-call | flops 335544320 | bytes 1246464 | tf_op jit(solution)/shard_map/sibling_kernel/pallas_call | solution.py:56
  233.7 1.5 collective-permute-start.23
  235.3 3.9 %collective-permute-done.27.refs_5_ = bf16[640,1024]{1,0:T(8,128)(2,1)S(1)} collective-permute-done((bf16[640,1024]{1,0:T(8,128)(2,1)S(1)}, bf16[640,1024]{1,0:T(8,128)(2,1)S(1)}, u32[]{:S(2)}, u32[]{:S(2)}) %collective-permute-start.27) | collective-permute-done | bytes 1310752 | tf_op jit(solution)/shard_map/ppermute | solution.py:23
  239.1 14.1 %backward_sublayer0.6 = (bf16[640,1024]{1,0:T(8,128)(2,1)}, bf16[640,2048]{1,0:T(8,128)(2,1)}, bf16[640,1024]{1,0:T(8,128)(2,1)S(1)}, f32[3,1024]{1,0:T(4,128)S(1)}, f32[1,2048]{1,0:T(1,128)S(1)}) custom-call(bf16[640,1024]{1,0:T(8,128)(2,1)S(1)} %copy-done.7, bf16[640,1024]{1,0:T(8,128)(2,1)} %collective-permute-done.21.refs_1_, ...), custom_call_target="tpu_custom_call" | custom-call | flops 335544320 | bytes 2034944 | tf_op jit(solution)/shard_map/backward_sublayer0/pallas_call | solution.py:56
  253.2 1.6 collective-permute-start.29
  254.8 1.2 collective-permute-done.26.refs_12_
  256.0 1.3 copy-done.36
  258.0 12.2 %own_grads_sublayer1.3 = (f32[2,1024,1024]{2,1,0:T(8,128)}, f32[2,1024,1024]{2,1,0:T(8,128)}, f32[1,1024]{1,0:T(1,128)S(1)}) custom-call(bf16[640,1024]{1,0:T(8,128)(2,1)} %get-tuple-element.223.refs_0_, bf16[640,1024]{1,0:T(8,128)(2,1)} %get-tuple-element.224.refs_1_, bf16[640,2048]{1,0:T(8,128)(2,1)} %get-tuple-element.225.refs_2_, ...), custom_call_target="tpu_custom_call" | custom-call | flops 335544320 | bytes 2295296 | tf_op jit(solution)/shard_map/own_grads_sublayer1/pallas_call | solution.py:56
  270.2 12.5 %backward_sublayer0.7 = (bf16[640,1024]{1,0:T(8,128)(2,1)}, bf16[640,2048]{1,0:T(8,128)(2,1)}, bf16[640,1024]{1,0:T(8,128)(2,1)S(1)}, f32[3,1024]{1,0:T(4,128)S(...) custom-call(bf16[640,1024]{1,0:T(8,128)(2,1)S(1)} %get-tuple-element.215.refs_0_.refs_2_.refs_1_, ...), custom_call_target="tpu_custom_call" | custom-call | flops 335544320 | bytes 2198784 | tf_op jit(solution)/shard_map/backward_sublayer0/pallas_call | solution.py:56
  282.7 11.9 %collective-permute-done.29.refs_5_ = bf16[640,1024]{1,0:T(8,128)(2,1)S(1)} collective-permute-done((bf16[640,1024]{1,0:T(8,128)(2,1)S(1)}, bf16[640,1024]{1,0:T(8,128)(2,1)S(1)}, u32[]{:S(2)}, u32[]{:S(2)}) %collective-permute-start.29) | collective-permute-done | bytes 1310752 | tf_op jit(solution)/shard_map/ppermute | solution.py:23
  294.7 4.7 %row_grad_kernel.3 = (bf16[832,1024]{1,0:T(8,128)(2,1)}, f32[1,1024]{1,0:T(1,128)S(1)}) custom-call(s32[1,832]{1,0:T(1,128)S(1)} %get-tuple-element.214.refs_0_, bf16[640,1024]{1,0:T(8,128)(2,1)S(1)} %get-tuple-element.215.refs_0_.refs_2_.refs_1_, f32[640,1024]{1,0:T(8,128)S(1)} %get-tuple-element.239.refs_2_, f32[640,128]{1,0:T(8,128)S(1)} %get-tuple-element.243.refs_3_, ...), custom_call_target="tpu_custom_call" | custom-call | flops 68157440 | bytes 539088 | tf_op jit(solution)/shard_map/row_grad_kernel/pallas_call | solution.py:56
  299.4 6.2 %all-to-all-start.6 = ((bf16[8,104,1024]{2,1,0:T(8,128)(2,1)}), bf16[8,104,1024]{2,1,0:T(8,128)(2,1)S(1)}, u32[]{:S(2)}, u32[]{:S(2)}) async-start(bf16[8,104,1024]{2,1,0:T(8,128)(2,1)} %bitcast.23), calls=%async_computation.6 | async-start | bytes 3407872 | tf_op jit(solution)/shard_map/all_to_all | solution.py:592
  305.6 9.7 %sibling_kernel.7 = (bf16[1024,1024]{1,0:T(8,128)(2,1)S(1)}, bf16[1024,1024]{1,0:T(8,128)(2,1)S(1)}, f32[1,1024]{1,0:T(1,128)S(1)}) custom-call(bf16[640,1024]{1,0:T(8,128)(2,1)} %get-tuple-element.252.refs_0_, bf16[640,1024]{1,0:T(8,128)(2,1)} %get-tuple-element.253.refs_1_, bf16[640,2048]{1,0:T(8,128)(2,1)} %get-tuple-element.254.refs_2_, ...), custom_call_target="tpu_custom_call" | custom-call | flops 335544320 | bytes 1246464 | tf_op jit(solution)/shard_map/sibling_kernel/pallas_call | solution.py:56
  315.9 1.5 marks.3.refs_5_
  318.0 4.6 %collective-permute-done.30.refs_1_ = f32[8,1024]{1,0:T(8,128)S(1)} collective-permute-done((f32[8,1024]{1,0:T(8,128)S(1)}, f32[8,1024]{1,0:T(8,128)S(1)}, u32[]{:S(2)}, u32[]{:S(2)}) %collective-permute-start.30) | collective-permute-done | bytes 32800 | tf_op jit(solution)/shard_map/ppermute | solution.py:23
  322.6 1.5 collective-permute-start.31
  324.2 4.7 %unpack_kernel.6 = bf16[640,1024]{1,0:T(8,128)(2,1)} custom-call(s32[1,640]{1,0:T(1,128)S(1)} %get-tuple-element.213.refs_0_, bf16[832,1024]{1,0:T(8,128)(2,1)} %bitcast.21.refs_0_.refs_1_, bf16[640,1024]{1,0:T(8,128)(2,1)S(1)} %copy-done.29), custom_call_target="tpu_custom_call" | custom-call | flops 68157440 | bytes 270496 | tf_op jit(solution)/shard_map/unpack_kernel/pallas_call | solution.py:56
  328.9 1.3 copy-done.34
  330.9 12.5 %own_grads_sublayer0.3 = (f32[2,1024,1024]{2,1,0:T(8,128)}, f32[2,1024,1024]{2,1,0:T(8,128)}, f32[1,1024]{1,0:T(1,128)S(1)}) custom-call(bf16[640,1024]{1,0:T(8,128)(2,1)} %get-tuple-element.252.refs_0_, bf16[640,1024]{1,0:T(8,128)(2,1)} %get-tuple-element.253.refs_1_, ...), custom_call_target="tpu_custom_call", output_to_operand_aliasing={{0}: (13, {}), {1}: (14, {})} | custom-call | flops 335544320 | bytes 3343872 | tf_op jit(solution)/shard_map/own_grads_sublayer0/pallas_call | solution.py:56
  344.6 2.2 unpack_kernel.7
  346.8 3.1 conditional.1
  349.9 1.0 copy-done.40
  (71 shorter events, 8.2 us)
Async XLA Ops:
  0.6 68.0 %collective-permute-start.17 = (bf16[2,1024,1024]{2,1,0:T(8,128)(2,1)}, bf16[2,1024,1024]{2,1,0:T(8,128)(2,1)}, u32[]{:S(2)}, u32[]{:S(2)}) collective-permute-start(bf16[2,1024,1024]{2,1,0:T(8,128)(2,1)} %bitcast.47), channel_id=1, source_target_pairs={{0,1},{1,0},{2,3},{3,2},{4,5},{5,4},{6,7},{7,6},{8,9},{9,8},{10,11... | collective-permute-start | bytes 12582920 | tf_op jit(solution)/shard_map/ppermute | solution.py:23
  1.2 67.4 %collective-permute-start.18 = (bf16[2,1024,1024]{2,1,0:T(8,128)(2,1)}, bf16[2,1024,1024]{2,1,0:T(8,128)(2,1)}, u32[]{:S(2)}, u32[]{:S(2)}) collective-permute-start(bf16[2,1024,1024]{2,1,0:T(8,128)(2,1)} %bitcast.57), channel_id=1, source_target_pairs={{0,1},{1,0},{2,3},{3,2},{4,5},{5,4},{6,7},{7,6},{8,9},{9,8},{10,11... | collective-permute-start | bytes 12582920 | tf_op jit(solution)/shard_map/ppermute | solution.py:23
  1.2 0.7 copy-start.24
  1.9 0.7 copy-start.25
  6.8 7.4 %copy-start.30 = (bf16[640,1024]{1,0:T(8,128)(2,1)S(1)}, bf16[640,1024]{1,0:T(8,128)(2,1)}, u32[]{:S(2)}) copy-start(bf16[640,1024]{1,0:T(8,128)(2,1)} %refs_2_.3) | copy-start | bytes 3932164
  6.8 47.4 %all-to-all-start.3 = ((bf16[8,104,1024]{2,1,0:T(8,128)(2,1)}), bf16[8,104,1024]{2,1,0:T(8,128)(2,1)S(1)}, u32[]{:S(2)}, u32[]{:S(2)}) async-start(bf16[8,104,1024]{2,1,0:T(8,128)(2,1)} %bitcast.10), calls=%async_computation.3 | async-start | bytes 3407872 | tf_op jit(solution)/shard_map/all_to_all | solution.py:649
  54.3 11.1 %copy-start.27 = (bf16[8,104,1024]{2,1,0:T(8,128)(2,1)}, bf16[8,104,1024]{2,1,0:T(8,128)(2,1)S(1)}, u32[]{:S(2)}) copy-start(bf16[8,104,1024]{2,1,0:T(8,128)(2,1)S(1)} %all-to-all-done.3) | copy-start | bytes 5111812
  54.3 4.5 %copy-start.15 = (bf16[1,2,1024]{2,1,0:T(2,128)(2,1)S(1)}, bf16[1,2,1024]{2,1,0:T(2,128)(2,1)}, u32[]{:S(2)}) copy-start(bf16[1,2,1024]{2,1,0:T(2,128)(2,1)} %param.20) | copy-start | bytes 12292
  54.3 5.3 %copy-start.44 = (bf16[1,256]{1,0:T(2,128)(2,1)S(1)}, bf16[1,256]{1,0:T(2,128)(2,1)}, u32[]{:S(2)}) copy-start(bf16[1,256]{1,0:T(2,128)(2,1)} %param.16) | copy-start | bytes 1540
  54.3 5.3 %copy-start.45 = (bf16[1,2,256]{2,1,0:T(2,128)(2,1)S(1)}, bf16[1,2,256]{2,1,0:T(2,128)(2,1)}, u32[]{:S(2)}) copy-start(bf16[1,2,256]{2,1,0:T(2,128)(2,1)} %param.17) | copy-start | bytes 3076
  54.3 5.3 %copy-start.46 = (bf16[1,2,256]{2,1,0:T(2,128)(2,1)S(1)}, bf16[1,2,256]{2,1,0:T(2,128)(2,1)}, u32[]{:S(2)}) copy-start(bf16[1,2,256]{2,1,0:T(2,128)(2,1)} %param.18) | copy-start | bytes 3076
  54.3 5.3 %copy-start.47 = (bf16[1,2,256]{2,1,0:T(2,128)(2,1)S(1)}, bf16[1,2,256]{2,1,0:T(2,128)(2,1)}, u32[]{:S(2)}) copy-start(bf16[1,2,256]{2,1,0:T(2,128)(2,1)} %param.22) | copy-start | bytes 3076
  54.3 88.6 %all-to-all-start.4 = ((bf16[8,104,1024]{2,1,0:T(8,128)(2,1)}), bf16[8,104,1024]{2,1,0:T(8,128)(2,1)}, u32[]{:S(2)}, u32[]{:S(2)}) async-start(bf16[8,104,1024]{2,1,0:T(8,128)(2,1)} %bitcast.15), calls=%async_computation.4 | async-start | bytes 3407872 | tf_op jit(solution)/shard_map/all_to_all | solution.py:541
  58.8 9.8 %collective-permute-start.16 = (bf16[2,1024]{1,0:T(2,128)(2,1)S(1)}, bf16[2,1024]{1,0:T(2,128)(2,1)S(1)}, u32[]{:S(2)}, u32[]{:S(2)}) collective-permute-start(bf16[2,1024]{1,0:T(2,128)(2,1)S(1)} %bitcast.39), channel_id=1, source_target_pairs={{0,1},{1,0},{2,3},{3,2},{4,5},{5,4},{6,7},{7,6},{8,9},{9,8},{10,11... | collective-permute-start | bytes 12296 | tf_op jit(solution)/shard_map/ppermute | solution.py:23
  67.0 31.7 %collective-permute-start.19 = (bf16[640,1024]{1,0:T(8,128)(2,1)S(1)}, bf16[640,1024]{1,0:T(8,128)(2,1)S(1)}, u32[]{:S(2)}, u32[]{:S(2)}) collective-permute-start(bf16[640,1024]{1,0:T(8,128)(2,1)S(1)} %get-tuple-element.215.refs_0_.refs_2_.refs_1_), channel_id=1, source_target_pairs={{0,2},{1,3},{2,0},{3,1},{4,6},{5,7},{6,4},{7,5},{8,10},{9,11},{10,... | collective-permute-start | bytes 3932168 | tf_op jit(solution)/shard_map/ppermute | solution.py:23
  79.5 47.2 %collective-permute-start.22 = (bf16[640,1024]{1,0:T(8,128)(2,1)S(1)}, bf16[640,1024]{1,0:T(8,128)(2,1)S(1)}, u32[]{:S(2)}, u32[]{:S(2)}) collective-permute-start(bf16[640,1024]{1,0:T(8,128)(2,1)S(1)} %get-tuple-element.216.refs_8_.refs_1_.refs_2_.refs_4_), channel_id=1, source_target_pairs={{0,2},{1,3},{2,0},{3,1},{4,6},{5,7},{6,4},{7,5},{8,10},{9,11},{10,... | collective-permute-start | bytes 3932168 | tf_op jit(solution)/shard_map/ppermute | solution.py:23
  98.7 28.1 %copy-start.6 = (bf16[640,1024]{1,0:T(8,128)(2,1)}, bf16[640,1024]{1,0:T(8,128)(2,1)S(1)}, u32[]{:S(2)}) copy-start(bf16[640,1024]{1,0:T(8,128)(2,1)S(1)} %collective-permute-done.19.refs_0_) | copy-start | bytes 3932164
  110.8 44.1 %collective-permute-start.20 = (bf16[640,1024]{1,0:T(8,128)(2,1)}, bf16[640,1024]{1,0:T(8,128)(2,1)}, u32[]{:S(2)}, u32[]{:S(2)}) collective-permute-start(bf16[640,1024]{1,0:T(8,128)(2,1)} %get-tuple-element.217.refs_1_.refs_2_), channel_id=1, source_target_pairs={{0,2},{1,3},{2,0},{3,1},{4,6},{5,7},{6,4},{7,5},{8,10},{9,11},{10,... | collective-permute-start | bytes 3932168 | tf_op jit(solution)/shard_map/ppermute | solution.py:23
  126.8 14.5 %copy-start.8 = (bf16[640,1024]{1,0:T(8,128)(2,1)}, bf16[640,1024]{1,0:T(8,128)(2,1)S(1)}, u32[]{:S(2)}) copy-start(bf16[640,1024]{1,0:T(8,128)(2,1)S(1)} %collective-permute-done.22.refs_2_.refs_3_) | copy-start | bytes 3932164
  141.3 41.8 %collective-permute-start.28 = (bf16[640,1024]{1,0:T(8,128)(2,1)}, bf16[640,1024]{1,0:T(8,128)(2,1)}, u32[]{:S(2)}, u32[]{:S(2)}) collective-permute-start(bf16[640,1024]{1,0:T(8,128)(2,1)} %get-tuple-element.242), channel_id=1, source_target_pairs={{0,2},{1,3},{2,0},{3,1},{4,6},{5,7},{6,4},{7,5},{8,10},{9,11},{10,... | collective-permute-start | bytes 3932168 | tf_op jit(solution)/shard_map/ppermute | solution.py:23
  146.9 64.2 %collective-permute-start.21 = (bf16[640,1024]{1,0:T(8,128)(2,1)}, bf16[640,1024]{1,0:T(8,128)(2,1)}, u32[]{:S(2)}, u32[]{:S(2)}) collective-permute-start(bf16[640,1024]{1,0:T(8,128)(2,1)} %compact_kernel.3.refs_1_.refs_3_), channel_id=1, source_target_pairs={{0,2},{1,3},{2,0},{3,1},{4,6},{5,7},{6,4},{7,5},{8,10},{9,11},{10,... | collective-permute-start | bytes 3932168 | tf_op jit(solution)/shard_map/ppermute | solution.py:23
  188.2 1.2 copy-start.12
  189.4 110.0 %all-to-all-start.5 = ((bf16[8,104,1024]{2,1,0:T(8,128)(2,1)}), bf16[8,104,1024]{2,1,0:T(8,128)(2,1)}, u32[]{:S(2)}, u32[]{:S(2)}) async-start(bf16[8,104,1024]{2,1,0:T(8,128)(2,1)} %bitcast.37), calls=%async_computation.5 | async-start | bytes 3407872 | tf_op jit(solution)/shard_map/all_to_all | solution.py:565
  195.2 15.9 %copy-start.7 = (bf16[640,1024]{1,0:T(8,128)(2,1)S(1)}, bf16[640,1024]{1,0:T(8,128)(2,1)}, u32[]{:S(2)}) copy-start(bf16[640,1024]{1,0:T(8,128)(2,1)} %copy-done.6) | copy-start | bytes 3932164
  195.2 15.9 %copy-start.9 = (bf16[640,1024]{1,0:T(8,128)(2,1)S(1)}, bf16[640,1024]{1,0:T(8,128)(2,1)}, u32[]{:S(2)}) copy-start(bf16[640,1024]{1,0:T(8,128)(2,1)} %copy-done.8) | copy-start | bytes 3932164
  207.3 31.8 %collective-permute-start.27 = (bf16[640,1024]{1,0:T(8,128)(2,1)S(1)}, bf16[640,1024]{1,0:T(8,128)(2,1)S(1)}, u32[]{:S(2)}, u32[]{:S(2)}) collective-permute-start(bf16[640,1024]{1,0:T(8,128)(2,1)S(1)} %get-tuple-element.219.refs_4_), channel_id=1, source_target_pairs={{0,2},{1,3},{2,0},{3,1},{4,6},{5,7},{6,4},{7,5},{8,10},{9,11},{10,... | collective-permute-start | bytes 3932168 | tf_op jit(solution)/shard_map/ppermute | solution.py:23
  233.2 22.8 %collective-permute-start.24 = (bf16[1024,1024]{1,0:T(8,128)(2,1)S(1)}, bf16[1024,1024]{1,0:T(8,128)(2,1)S(1)}, u32[]{:S(2)}, u32[]{:S(2)}) collective-permute-start(bf16[1024,1024]{1,0:T(8,128)(2,1)S(1)} %get-tuple-element.233), channel_id=1, source_target_pairs={{0,1},{1,0},{2,3},{3,2},{4,5},{5,4},{6,7},{7,6},{8,9},{9,8},{10,11... | collective-permute-start | bytes 6291464 | tf_op jit(solution)/shard_map/ppermute | solution.py:23
  233.2 22.8 %collective-permute-start.25 = (bf16[1024,1024]{1,0:T(8,128)(2,1)S(1)}, bf16[1024,1024]{1,0:T(8,128)(2,1)S(1)}, u32[]{:S(2)}, u32[]{:S(2)}) collective-permute-start(bf16[1024,1024]{1,0:T(8,128)(2,1)S(1)} %get-tuple-element.234), channel_id=1, source_target_pairs={{0,1},{1,0},{2,3},{3,2},{4,5},{5,4},{6,7},{7,6},{8,9},{9,8},{10,11... | collective-permute-start | bytes 6291464 | tf_op jit(solution)/shard_map/ppermute | solution.py:23
  233.7 36.4 %collective-permute-start.23 = (bf16[640,1024]{1,0:T(8,128)(2,1)S(1)}, bf16[640,1024]{1,0:T(8,128)(2,1)S(1)}, u32[]{:S(2)}, u32[]{:S(2)}) collective-permute-start(bf16[640,1024]{1,0:T(8,128)(2,1)S(1)} %get-tuple-element.221.refs_4_), channel_id=1, source_target_pairs={{0,2},{1,3},{2,0},{3,1},{4,6},{5,7},{6,4},{7,5},{8,10},{9,11},{10,... | collective-permute-start | bytes 3932168 | tf_op jit(solution)/shard_map/ppermute | solution.py:23
  253.2 41.5 %collective-permute-start.29 = (bf16[640,1024]{1,0:T(8,128)(2,1)S(1)}, bf16[640,1024]{1,0:T(8,128)(2,1)S(1)}, u32[]{:S(2)}, u32[]{:S(2)}) collective-permute-start(bf16[640,1024]{1,0:T(8,128)(2,1)S(1)} %get-tuple-element.245), channel_id=1, source_target_pairs={{0,2},{1,3},{2,0},{3,1},{4,6},{5,7},{6,4},{7,5},{8,10},{9,11},{10,... | collective-permute-start | bytes 3932168 | tf_op jit(solution)/shard_map/ppermute | solution.py:23
  254.8 1.2 collective-permute-start.26
  256.0 1.3 copy-start.36
  256.0 2.0 copy-start.37
  299.4 45.2 %all-to-all-start.6 = ((bf16[8,104,1024]{2,1,0:T(8,128)(2,1)}), bf16[8,104,1024]{2,1,0:T(8,128)(2,1)S(1)}, u32[]{:S(2)}, u32[]{:S(2)}) async-start(bf16[8,104,1024]{2,1,0:T(8,128)(2,1)} %bitcast.23), calls=%async_computation.6 | async-start | bytes 3407872 | tf_op jit(solution)/shard_map/all_to_all | solution.py:592
  315.3 8.8 %copy-start.29 = (bf16[640,1024]{1,0:T(8,128)(2,1)S(1)}, bf16[640,1024]{1,0:T(8,128)(2,1)}, u32[]{:S(2)}) copy-start(bf16[640,1024]{1,0:T(8,128)(2,1)} %refs_2_.2) | copy-start | bytes 3932164
  315.4 13.5 %collective-permute-start.32 = (bf16[1024,1024]{1,0:T(8,128)(2,1)S(1)}, bf16[1024,1024]{1,0:T(8,128)(2,1)S(1)}, u32[]{:S(2)}, u32[]{:S(2)}) collective-permute-start(bf16[1024,1024]{1,0:T(8,128)(2,1)S(1)} %get-tuple-element.261), channel_id=1, source_target_pairs={{0,1},{1,0},{2,3},{3,2},{4,5},{5,4},{6,7},{7,6},{8,9},{9,8},{10,11... | collective-permute-start | bytes 6291464 | tf_op jit(solution)/shard_map/ppermute | solution.py:23
  315.4 13.4 %collective-permute-start.33 = (bf16[1024,1024]{1,0:T(8,128)(2,1)S(1)}, bf16[1024,1024]{1,0:T(8,128)(2,1)S(1)}, u32[]{:S(2)}, u32[]{:S(2)}) collective-permute-start(bf16[1024,1024]{1,0:T(8,128)(2,1)S(1)} %get-tuple-element.262), channel_id=1, source_target_pairs={{0,1},{1,0},{2,3},{3,2},{4,5},{5,4},{6,7},{7,6},{8,9},{9,8},{10,11... | collective-permute-start | bytes 6291464 | tf_op jit(solution)/shard_map/ppermute | solution.py:23
  317.4 5.2 %collective-permute-start.30 = (f32[8,1024]{1,0:T(8,128)S(1)}, f32[8,1024]{1,0:T(8,128)S(1)}, u32[]{:S(2)}, u32[]{:S(2)}) collective-permute-start(f32[8,1024]{1,0:T(8,128)S(1)} %columns_kernel.3.refs_0_), channel_id=1, source_target_pairs={{0,1},{1,0},{2,3},{3,2},{4,5},{5,4},{6,7},{7,6},{8,9},{9,8},{10,11... | collective-permute-start | bytes 98312 | tf_op jit(solution)/shard_map/ppermute | solution.py:23
  317.6 11.3 %collective-permute-start.34 = (f32[1,1024]{1,0:T(1,128)S(1)}, f32[1,1024]{1,0:T(1,128)S(1)}, u32[]{:S(2)}, u32[]{:S(2)}) collective-permute-start(f32[1,1024]{1,0:T(1,128)S(1)} %get-tuple-element.263), channel_id=1, source_target_pairs={{0,1},{1,0},{2,3},{3,2},{4,5},{5,4},{6,7},{7,6},{8,9},{9,8},{10,11... | collective-permute-start | bytes 12296 | tf_op jit(solution)/shard_map/ppermute | solution.py:23
  322.6 20.7 %collective-permute-start.31 = (f32[8,1024]{1,0:T(8,128)S(1)}, f32[8,1024]{1,0:T(8,128)S(1)}, u32[]{:S(2)}, u32[]{:S(2)}) collective-permute-start(f32[8,1024]{1,0:T(8,128)S(1)} %add_kernel.3.refs_1_), channel_id=1, source_target_pairs={{0,2},{1,3},{2,0},{3,1},{4,6},{5,7},{6,4},{7,5},{8,10},{9,11},{10,... | collective-permute-start | bytes 98312 | tf_op jit(solution)/shard_map/ppermute | solution.py:23
  328.8 1.3 copy-start.34
  328.9 2.0 copy-start.35
  330.9 13.7 %copy-start.31 = (bf16[640,1024]{1,0:T(8,128)(2,1)S(1)}, bf16[640,1024]{1,0:T(8,128)(2,1)}, u32[]{:S(2)}) copy-start(bf16[640,1024]{1,0:T(8,128)(2,1)} %refs_2_.3) | copy-start | bytes 3932164
  344.6 2.2 copy-start.28
  349.9 1.1 copy-start.40
where the time goes:
time: 355 us; the launch traced here: 351 us
  Pallas kernels  177 us (50%)
  waiting for transfers between devices  118 us (33%)
  starting transfers between devices  38.3 us (11%)
  local copies, waits for them, and re-layouts  8.31 us (2%)
  blocking collectives  5.77 us (2%)
    pallas_call x24, Pallas kernels, run(): pl.pallas_call(body, out_shape=outs, in_specs=[*specs, *[ANY] * extra], o...  177 us
    ppermute x19, waiting for transfers between devices, swap(): lax.ppermute(value, 'rep', [(r, r ^ mask) for r in range(lax.axis_size('r...  79.8 us
    all_to_all x1, waiting for transfers between devices, shards(): lax.all_to_all(outgoing, 'ex', split_axis=0, concat_axis=0, tiled=True)  37.4 us
    ppermute x19, starting transfers between devices, swap(): lax.ppermute(value, 'rep', [(r, r ^ mask) for r in range(lax.axis_size('r...  14.4 us
    unnamed x44, local copies, waits for them, and re-layouts  7.6 us
    all_to_all x1, starting transfers between devices, shards(): lax.all_to_all(outgoing, 'ex', split_axis=0, concat_axis=0, tiled=True)  7.36 us
  transfers between devices with their start and end apart: 23, of which 11 were waited for; matrix products, arithmetic and copies ran while one was open for 0% of the time, Pallas kernels for 50%

commit v1 on v0

--- a/solution.py
+++ b/solution.py
@@ -15,8 +15,9 @@
 SMEM = pl.BlockSpec(memory_space=pltpu.SMEM)
 ANY = pl.BlockSpec(memory_space=pl.ANY)
 HBM = pl.BlockSpec(memory_space=pltpu.HBM)
-CAP = 640
+EDGE, SHARED = 448, 192
 SCALE = 16
+LAST_COST = 128
 
 
 def swap(value, mask):
@@ -36,7 +37,7 @@
     return jax.ShapeDtypeStruct(shape, dtype)
 
 
-def run(kernel, outs, operands, flops=0, scratch=(), in_specs=None, out_specs=None, limit=16, aliases=None, after=(), pinned=False, name=None):
+def run(kernel, outs, operands, flops=0, scratch=(), in_specs=None, out_specs=None, limit=24, aliases=None, after=(), pinned=False, name=None):
     outs, count, extra = list(outs), len(operands), len(after)
     moved = sum(v.size * v.dtype.itemsize for v in (*operands, *outs))
 
@@ -159,8 +160,8 @@
     columns_ref[2:3, :] = own1[0:1, :] + far1[0:1, :]
     columns_ref[3:4, :] = own0[1:2, :] + far0[1:2, :]
     columns_ref[4:5, :] = own1[1:2, :] + far1[1:2, :]
-    columns_ref[5:6, :] = own0[2:3, :]
-    columns_ref[6:7, :] = own1[2:3, :]
+    columns_ref[5:6, :] = own0[2:3, :] + far0[2:3, :]
+    columns_ref[6:7, :] = own1[2:3, :] + far1[2:3, :]
     columns_ref[7:8, :] = mark[...]
 
 
@@ -194,19 +195,21 @@
     rows_ref[...] = dot(onehot(rows_ref.shape[0], place[...]), arrived[...], 1, 0).astype(BF16)
 
 
-def place_kernel(sources, arrived, rows_ref, place_ref, count_ref):
-    n = arrived.shape[0]
-    slots = n // sources
+def place_kernel(senders, edge, position, arrived, rows_ref, place_ref, count_ref):
+    n, window = arrived.shape[0], rows_ref.shape[0]
+    slots = n // senders
     lane = iota((1, n), 1).astype(F32)
     place, total = jnp.full((1, n), -1.0, F32), jnp.zeros((1, 1), F32)
-    for k in range(sources):
+    for k in range(senders):
         count = arrived[(k + 1) * slots - 1 : (k + 1) * slots, 0:128].astype(F32)[:, 0:1]
         slot = lane - k * slots
         place = jnp.where((slot >= 0.0) & (slot < count), total + slot, place)
         total = total + count
+    backwards = (place >= edge) & ((position[0] // 2) % 2 == 1)
+    place = jnp.where(backwards, window + edge - 1 - place, place)
     place_ref[...] = place.astype(jnp.int32)
     count_ref[...] = jnp.broadcast_to(total, count_ref.shape)
-    rows_ref[...] = dot(onehot(rows_ref.shape[0], place_ref[...]), arrived[...], 1, 0).astype(BF16)
+    rows_ref[...] = dot(onehot(window, place_ref[...]), arrived[...], 1, 0).astype(BF16)
 
 
 def spread(place, values, slots_ref):
@@ -214,8 +217,46 @@
     slots_ref[...] = dot(places, values, 0, 0).astype(BF16)
 
 
-def hidden1_of(rows, own0, far0, vectors):
-    return up(rows) + up(own0) + up(far0) + row(vectors, B_OUT)
+FIELDS = {
+    "p": ("pE", "pFW", "pFW"),
+    "q": ("qOW", "qF", "qOW"),
+    "d": ("dOW", "dF", "dOW"),
+    "h": ("hE", "hFW", "hFW"),
+    "c": ("cE", "cFW", "cFW"),
+}
+
+
+def names_of(rows, *fields):
+    names = []
+    for field in fields:
+        if field in FIELDS:
+            own, far, shared = FIELDS[field]
+        else:
+            own, far, shared = field + "_own", field + "_far", None
+        names.append(own if rows in ("E", "OW") else far)
+        if rows in ("OW", "FW"):
+            names += [shared] if shared else [own, far]
+    return list(dict.fromkeys(names))
+
+
+def values_of(rows, field, edge, refs):
+    if field in FIELDS:
+        own, far, shared = FIELDS[field]
+    else:
+        own, far, shared = field + "_own", field + "_far", None
+    first = refs[own if rows in ("E", "OW") else far]
+    if rows in ("E", "F"):
+        return first[0:edge, :].astype(F32)
+    if shared:
+        inner = refs[shared][edge:, :].astype(F32)
+    else:
+        inner = refs[own][edge:, :].astype(F32) + refs[far][edge:, :].astype(F32)
+    return jnp.concatenate([first[0:edge, :].astype(F32), inner], 0)
+
+
+def hidden1_of(rows, edge, refs, vectors):
+    parts = [values_of(rows, field, edge, refs) for field in ("x", "p", "q")]
+    return parts[0] + parts[1] + parts[2] + row(vectors, B_OUT)
 
 
 class Copies:
@@ -259,13 +300,14 @@
     return [pltpu.VMEM((4, *weights[0].shape[1:]), BF16), dma(4)]
 
 
-def forward_kernel(layer, *refs):
-    n = 1 + 2 * layer
-    sources, (vectors, biases_own, biases_sib) = refs[:n], refs[n : n + 3]
+def forward_kernel(layer, rows, edge, names, send, *refs):
+    n = len(names)
+    named, (vectors, biases_own, biases_sib) = dict(zip(names, refs[:n])), refs[n : n + 3]
     got = fetch(layer, refs[n + 3 : n + 7], (0, 2, 1, 3), *refs[-2:])
-    normed_out, act_out, slope_out, out_ref, normed, act, slope, sems = refs[n + 7 : n + 15]
+    normed_out, act_out, slope_out, out_ref = refs[n + 7 : n + 11]
+    normed, act, slope, sems = refs[-6:-2]
     copies = Copies(sems)
-    hidden = hidden1_of(*sources, vectors) if layer else up(sources[0])
+    hidden = hidden1_of(rows, edge, named, vectors) if layer else values_of(rows, "x", edge, named)
     xhat, _ = normalize(hidden)
     normed[...] = (xhat * row(vectors, GAIN + layer) + row(vectors, SHIFT + layer)).astype(BF16)
     copies.start(normed, normed_out)
@@ -281,53 +323,60 @@
         part = dot(act[:, columns], got(2 + q), 1, 0)
         total = part if total is None else total + part
     out_ref[...] = total.astype(BF16)
+    if send:
+        refs[n + 11][...] = out_ref[edge:, :]
     copies.wait()
 
 
-def forward(layer, sources, vectors, biases, weights, after=()):
-    rows, d = sources[0].shape
-    f = 2 * weights[0].shape[2]
-    small = [*sources, vectors, *biases]
+def forward(layer, rows, sizes, named, vectors, biases, weights, after=(), send=False):
+    edge, count = sizes[0], sizes[0] + (sizes[1] if rows in ("OW", "FW") else 0)
+    names = names_of(rows, *(("x", "p", "q") if layer else ("x",)))
+    d, f = vectors.shape[1], 2 * weights[0].shape[2]
+    small = [*(named[k] for k in names), vectors, *biases]
     return run(
-        functools.partial(forward_kernel, layer),
-        [shaped(rows, d), shaped(rows, f), shaped(rows, f), shaped(rows, d)],
+        functools.partial(forward_kernel, layer, rows, edge, names, send),
+        [shaped(count, d), shaped(count, f), shaped(count, f), shaped(count, d)] + [shaped(sizes[1], d)] * send,
         [*small, *weights],
-        flops=4 * rows * d * f,
+        flops=4 * count * d * f,
         in_specs=[VMEM] * len(small) + [HBM] * 4,
-        out_specs=[HBM] * 3 + [VMEM],
+        out_specs=[HBM] * 3 + [VMEM] * (1 + send),
         scratch=[
-            pltpu.VMEM((rows, d), BF16),
-            pltpu.VMEM((rows, f), BF16),
-            pltpu.VMEM((rows, f), BF16),
+            pltpu.VMEM((count, d), BF16),
+            pltpu.VMEM((count, f), BF16),
+            pltpu.VMEM((count, f), BF16),
             dma(5),
             *weight_scratch(weights),
         ],
         after=after,
-        name=f"forward_sublayer{layer}",
-        **room(rows, 26),
-    )
-
-
-def backward_kernel(layer, keep, *refs):
-    n = 4 if layer else 6
-    sources, (vectors, slope_in) = refs[:n], refs[n : n + 2]
+        name=f"forward_sublayer{layer}_{rows}",
+        **room(count, 26),
+    )
+
+
+def backward_kernel(layer, rows, edge, names, *refs):
+    n = len(names)
+    named, (vectors, slope_in) = dict(zip(names, refs[:n])), refs[n : n + 2]
     got = fetch(layer, refs[n + 2 : n + 6], (2, 0, 3, 1), *refs[-2:])
     branch_out, low_out, out_ref, columns_ref, bias_ref = refs[n + 6 : n + 11]
     branch, low, slope, sems, slope_sem = refs[-7:-2]
     copies = Copies(sems)
     slope_copy = pltpu.make_async_copy(slope_in, slope, slope_sem.at[0])
     slope_copy.start()
-    rows, grads, own0, far0 = sources[:4]
-    d_hidden = gate_of(up(rows), row(vectors, CENTROID)) * up(grads)
+    x = values_of(rows, "x", edge, named)
+    d_hidden = gate_of(x, row(vectors, CENTROID)) * values_of(rows, "g", edge, named)
     if layer == 0:
-        xhat, rstd = normalize(hidden1_of(rows, own0, far0, vectors))
-        d_normed = up(sources[4]) + up(sources[5])
+        xhat, rstd = normalize(hidden1_of(rows, edge, named, vectors))
+        d_normed = values_of(rows, "d", edge, named) + values_of(rows, "h", edge, named)
         d_hidden = d_hidden + norm_backward(d_normed, xhat, rstd, row(vectors, GAIN + 1))
-        if keep:
-            refs[n + 11][...] = d_hidden
+        refs[n + 11][...] = d_hidden if rows == "E" else d_hidden[edge:]
     branch[...] = d_hidden.astype(BF16)
     copies.start(branch, branch_out)
-    columns_ref[2:3, :] = jnp.sum(d_hidden, 0, keepdims=True)
+    own = jnp.zeros((1, d_hidden.shape[1]), F32)
+    if rows in ("E", "OW"):
+        own = own + jnp.sum(d_hidden[:edge], 0, keepdims=True)
+    if rows in ("OW", "FW"):
+        own = own + 0.5 * jnp.sum(d_hidden[edge:], 0, keepdims=True)
+    columns_ref[2:3, :] = own
     total = None
     for q in range(2):
         d_act = dot(branch[...], got(2 + q), 1, 1)
@@ -341,56 +390,68 @@
         part = dot(low[:, columns], got(q), 1, 1)
         total = part if total is None else total + part
     out_ref[...] = total.astype(BF16)
-    xhat, _ = normalize(hidden1_of(rows, own0, far0, vectors) if layer else up(rows))
+    xhat, _ = normalize(hidden1_of(rows, edge, named, vectors) if layer else values_of(rows, "x", edge, named))
     columns_ref[0:1, :] = jnp.sum(total * xhat, 0, keepdims=True)
     columns_ref[1:2, :] = jnp.sum(total, 0, keepdims=True)
     copies.wait()
 
 
-def backward(layer, keep, sources, vectors, slope, weights, after=()):
-    rows, d = sources[0].shape
-    f = 2 * weights[0].shape[2]
-    outs = [shaped(rows, d), shaped(rows, f), shaped(rows, d), shaped(3, d, dtype=F32), shaped(1, f, dtype=F32)]
-    outs += [shaped(rows, d, dtype=F32)] if keep else []
+def backward(layer, rows, sizes, named, vectors, slope, weights, after=()):
+    edge, count = sizes[0], sizes[0] + (sizes[1] if rows in ("OW", "FW") else 0)
+    names = names_of(rows, *(("x", "g", "p", "q") if layer else ("x", "g", "p", "q", "d", "h")))
+    d, f = vectors.shape[1], 2 * weights[0].shape[2]
+    outs = [shaped(count, d), shaped(count, f), shaped(count, d), shaped(3, d, dtype=F32), shaped(1, f, dtype=F32)]
+    if layer == 0:
+        outs.append(shaped(edge if rows == "E" else sizes[1], d, dtype=F32))
+    operands = [named[k] for k in names]
     return run(
-        functools.partial(backward_kernel, layer, keep),
+        functools.partial(backward_kernel, layer, rows, edge, names),
         outs,
-        [*sources, vectors, slope, *weights],
-        flops=4 * rows * d * f,
-        in_specs=[VMEM] * (len(sources) + 1) + [HBM] * 5,
+        [*operands, vectors, slope, *weights],
+        flops=(LAST_COST if layer == 0 and rows == "E" else 4) * count * d * f,
+        in_specs=[VMEM] * (len(operands) + 1) + [HBM] * 5,
         out_specs=[HBM] * 2 + [VMEM] * (len(outs) - 2),
         scratch=[
-            pltpu.VMEM((rows, d), BF16),
-            pltpu.VMEM((rows, f), BF16),
-            pltpu.VMEM((rows, f), BF16),
+            pltpu.VMEM((count, d), BF16),
+            pltpu.VMEM((count, f), BF16),
+            pltpu.VMEM((count, f), BF16),
             dma(3),
             dma(1),
             *weight_scratch(weights),
         ],
         after=after,
-        name=f"backward_sublayer{layer}",
-        **room(rows, 26),
-    )
-
-
-def result_kernel(sources, place, count, rows, grads, own0, far0, own1, far1, vectors, slots_ref, logit_ref):
-    gate = gate_of(up(rows), row(vectors, CENTROID))
-    hidden = hidden1_of(rows, own0, far0, vectors) + up(own1) + up(far1) + row(vectors, B_OUT + 1)
-    d_gate = jnp.sum(up(grads) * hidden, -1, keepdims=True)
+        name=f"backward_sublayer{layer}_{rows}",
+        **room(count, 32),
+    )
+
+
+def result_kernel(senders, edge, names, *refs):
+    named = dict(zip(names, refs))
+    place, count, count_far, vectors, slots_ref, logit_ref = refs[len(names) :]
+    gate = gate_of(values_of("OW", "x", edge, named), row(vectors, CENTROID))
+    hidden = hidden1_of("OW", edge, named, vectors)
+    hidden = hidden + up(named["u"]) + jnp.concatenate([up(named["vE"]), up(named["vS"])], 0) + row(vectors, B_OUT + 1)
+    d_gate = jnp.sum(up(named["g_own"]) * hidden, -1, keepdims=True)
     d_logit = (d_gate * gate * (1.0 - gate)).astype(BF16).astype(F32)
     logit_ref[...] = jnp.broadcast_to(d_logit, logit_ref.shape)
     spread(place, (gate * hidden).astype(BF16), slots_ref)
-    over = jnp.where(count[...] > rows.shape[0], 1.0, 0.0).astype(BF16)
-    slots = slots_ref.shape[0] // sources
-    for k in range(sources):
+    window = logit_ref.shape[0]
+    inner = jnp.maximum(count[...] - edge, 0.0) + jnp.maximum(count_far[...] - edge, 0.0)
+    over = jnp.where((count[...] > window) | (inner > window - edge), 1.0, 0.0).astype(BF16)
+    slots = slots_ref.shape[0] // senders
+    for k in range(senders):
         slots_ref[(k + 1) * slots - 1 : (k + 1) * slots, 0:128] = over
 
 
-def row_grad_kernel(place, rows, d_hidden1, logit, own0, far0, vectors, slots_ref, columns_ref):
-    x = up(rows)
+def row_grad_kernel(edge, names, *refs):
+    named = dict(zip(names, refs))
+    place, edge_grad, shared_grad, got, logit, vectors, slots_ref, columns_ref = refs[len(names) :]
+    x = values_of("OW", "x", edge, named)
     xhat, rstd = normalize(x)
     d_logit = logit[:, 0:1]
-    d_hidden = d_hidden1[...] + norm_backward(up(own0) + up(far0), xhat, rstd, row(vectors, GAIN))
+    d_normed = values_of("OW", "c", edge, named) + up(got)
+    d_hidden = jnp.concatenate([edge_grad[...], shared_grad[...]], 0)
+    d_hidden = d_hidden + norm_backward(d_normed, xhat, rstd, row(vectors, GAIN))
     d_row = d_hidden + d_logit * row(vectors, CENTROID)
     spread(place, d_row.astype(BF16), slots_ref)
     columns_ref[...] = jnp.sum(d_logit * x, 0, keepdims=True)
@@ -465,36 +526,36 @@
 
 
 def product_scratch(saved):
-    rows, d = saved[0][0].shape
-    f = saved[1][0].shape[1] // 2
-    return [pltpu.VMEM((rows, n), BF16) for n in (d, d, f, f, f, f, d, d)] + [dma(8)]
+    d, f = saved[0][0].shape[1], saved[1][0].shape[1] // 2
+    counts = [v.shape[0] for v in saved[0]] * 4
+    return [pltpu.VMEM((m, n), BF16) for m, n in zip(counts, (d, d, f, f, f, f, d, d))] + [dma(8)]
 
 
 def sibling_grads(saved, biases, after=()):
     normed, low, act, branch = saved
-    rows, d = normed[0].shape
+    rows, d = sum(v.shape[0] for v in normed), normed[0].shape[1]
     f = low[0].shape[1] // 2
     return run(
         sibling_kernel,
         [shaped(d, f), shaped(f, d), shaped(1, f, dtype=F32)],
         [*normed, *low, *act, *branch, *biases],
-        flops=8 * rows * d * f,
+        flops=4 * rows * d * f,
         in_specs=[HBM] * 8 + [VMEM] * 2,
         scratch=product_scratch(saved),
         after=after,
-        **room(rows, 24),
+        **room(rows // 2, 24),
     )
 
 
 def own_grads(layer, saved, biases, got, before, after=()):
     normed, low, act, branch = saved
-    rows, d = normed[0].shape
+    rows, d = sum(v.shape[0] for v in normed), normed[0].shape[1]
     f = low[0].shape[1] // 2
     return run(
         functools.partial(own_kernel, layer, len(before)),
         [shaped(2, d, f, dtype=F32), shaped(2, f, d, dtype=F32), shaped(1, f, dtype=F32)],
         [*normed, *low, *act, *branch, *biases, *got, *before],
-        flops=8 * rows * d * f,
+        flops=4 * rows * d * f,
         in_specs=[HBM] * 8 + [VMEM] * 2 + [HBM] * 2 + [VMEM] + [HBM] * len(before),
         out_specs=[HBM, HBM, VMEM],
         scratch=[
@@ -509,106 +570,112 @@
         aliases={13 + k: k for k in range(len(before))},
         after=after,
         name=f"own_grads_sublayer{layer}",
-        **room(rows, 32),
-    )
-
-
-def expert_group(cap, arrived, outgoing_g, target, tokens, grad_output, vectors, biases, weights):
-    d, worst, sources = tokens.shape[1], arrived.shape[0], lax.axis_size("ex")
+        **room(rows // 2, 32),
+    )
+
+
+def expert_group(sizes, arrived, outgoing_g, target, tokens, grad_output, vectors, biases, weights):
+    edge, window = sizes[0], sum(sizes)
+    d, worst, senders = tokens.shape[1], arrived.shape[0], lax.axis_size("ex")
     exchange = functools.partial(lax.all_to_all, axis_name="ex", split_axis=0, concat_axis=0, tiled=True)
-    one_hot_flops = 2 * cap * worst * d
-
-    def compact(values):
-        return run(compact_kernel, [shaped(cap, d)], [place, values], flops=one_hot_flops)[0]
+    one_hot_flops = 2 * window * worst * d
 
     def unpack(returned, values):
         return run(unpack_kernel, [shaped(*values.shape)], [target, returned, values], flops=one_hot_flops)[0]
 
+    position = lax.axis_index("rep").astype(jnp.int32).reshape(1)
     x_own, place, count = run(
-        functools.partial(place_kernel, sources),
-        [shaped(cap, d), shaped(1, worst, dtype=jnp.int32), shaped(1, 128, dtype=F32)],
-        [arrived],
+        functools.partial(place_kernel, senders, edge),
+        [shaped(window, d), shaped(1, worst, dtype=jnp.int32), shaped(1, 128, dtype=F32)],
+        [position, arrived],
+        in_specs=[SMEM, VMEM],
         flops=one_hot_flops,
         name="place",
-        after=(vectors,),
-    )
-    x_far = swap(x_own, 2)
-
-    normed_own0, act_own0, slope_own0, own0 = forward(0, (x_own,), vectors, biases, weights)
-    got_far0 = swap(own0, 2)
-    normed_far0, act_far0, slope_far0, far0 = forward(0, (x_far,), vectors, biases, weights, (own0,))
-    got_own0 = swap(far0, 2)
+    )
+    have = {"x_own": x_own, "x_far": swap(x_own, 2)}
+    count_far = swap(count, 2)
     g_arrived = exchange(outgoing_g)
-    g_own = compact(g_arrived)
-    g_far = swap(g_own, 2)
-
-    normed_far1, act_far1, slope_far1, far1 = forward(1, (x_far, far0, got_far0), vectors, biases, weights)
-    got_own1 = swap(far1, 2)
-    normed_own1, act_own1, slope_own1, own1 = forward(1, (x_own, own0, got_own0), vectors, biases, weights)
-    in_own, in_far = (x_own, g_own, own0, got_own0), (x_far, g_far, far0, got_far0)
-    branch_own1, low_own1, d_own1, columns_own1, bias_own1 = backward(
-        1, False, in_own, vectors, slope_own1, weights
-    )
-    got_d_far1 = swap(d_own1, 2)
-    branch_far1, low_far1, d_far1, columns_far1, bias_far1 = backward(
-        1, False, in_far, vectors, slope_far1, weights
-    )
-    got_d_own1 = swap(d_far1, 2)
-
+
+    *keep_e0, have["pE"] = forward(0, "E", sizes, have, vectors, biases, weights)
+    have["qF"] = swap(have["pE"], 2)
+    *keep_fw0, have["pFW"] = forward(0, "FW", sizes, have, vectors, biases, weights, (have["pE"],))
+    have["qOW"] = swap(have["pFW"], 2)
+    g_own = run(compact_kernel, [shaped(window, d)], [place, g_arrived], flops=one_hot_flops)[0]
+    have["g_own"], have["g_far"] = g_own, swap(g_own, 2)
+
+    *keep_f1, far1 = forward(1, "F", sizes, have, vectors, biases, weights)
+    have["vE"] = swap(far1, 2)
+    *keep_ow1, have["u"], shared1 = forward(1, "OW", sizes, have, vectors, biases, weights, send=True)
+    have["vS"] = swap(shared1, 2)
+    branch_ow1, low_ow1, have["dOW"], columns_ow1, bias_ow1 = backward(
+        1, "OW", sizes, have, vectors, keep_ow1[2], weights
+    )
+    have["hFW"] = swap(have["dOW"], 2)
+    branch_f1, low_f1, have["dF"], columns_f1, bias_f1 = backward(
+        1, "F", sizes, have, vectors, keep_f1[2], weights, (bias_ow1,)
+    )
+    have["hE"] = swap(have["dF"], 2)
+
+    names = list(dict.fromkeys([*names_of("OW", "x", "p", "q"), "u", "vE", "vS", "g_own"]))
     result, logit = run(
-        functools.partial(result_kernel, sources),
-        [shaped(worst, d), shaped(cap, 128, dtype=F32)],
-        [place, count, x_own, g_own, own0, got_own0, own1, got_own1, vectors],
+        functools.partial(result_kernel, senders, edge, names),
+        [shaped(worst, d), shaped(window, 128, dtype=F32)],
+        [*(have[k] for k in names), place, count, count_far, vectors],
         flops=one_hot_flops,
         name="result",
+        after=(bias_ow1,),
+        **room(window, 20),
     )
     returned = exchange(result)
 
     saved1 = (
-        (normed_own1, normed_far1),
-        (low_own1, low_far1),
-        (act_own1, act_far1),
-        (branch_own1, branch_far1),
-    )
-    sent1 = sibling_grads(saved1, (bias_own1, bias_far1))
+        (keep_ow1[0], keep_f1[0]),
+        (low_ow1, low_f1),
+        (keep_ow1[1], keep_f1[1]),
+        (branch_ow1, branch_f1),
+    )
+    biases1 = (bias_ow1, bias_f1)
+    sent1 = sibling_grads(saved1, biases1)
     got1 = [swap(v, 1) for v in sent1]
 
-    branch_far0, low_far0, d_far0, columns_far0, bias_far0 = backward(
-        0, False, (*in_far, d_far1, got_d_far1), vectors, slope_far0, weights, (sent1[2],)
-    )
-    got_d_own0 = swap(d_far0, 2)
-    grad_first, grad_second, grad_bias1 = own_grads(
-        1, saved1, (bias_own1, bias_far1), got1, (), (bias_far0,)
-    )
-    branch_own0, low_own0, d_own0, columns_own0, bias_own0, d_hidden1 = backward(
-        0, True, (*in_own, d_own1, got_d_own1), vectors, slope_own0, weights, (grad_bias1,)
-    )
+    branch_fw0, low_fw0, have["cFW"], columns_fw0, bias_fw0, d_shared = backward(
+        0, "FW", sizes, have, vectors, keep_fw0[2], weights, (sent1[2],)
+    )
+    got_c = swap(have["cFW"], 2)
+    branch_e0, low_e0, have["cE"], columns_e0, bias_e0, d_edge = backward(
+        0, "E", sizes, have, vectors, keep_e0[2], weights
+    )
+    saved0 = (
+        (keep_e0[0], keep_fw0[0]),
+        (low_e0, low_fw0),
+        (keep_e0[1], keep_fw0[1]),
+        (branch_e0, branch_fw0),
+    )
+    biases0 = (bias_e0, bias_fw0)
+    sent0 = sibling_grads(saved0, biases0)
+    names = names_of("OW", "x", "c")
     d_rows, columns_x = run(
-        row_grad_kernel,
+        functools.partial(row_grad_kernel, edge, names),
         [shaped(worst, d), shaped(1, d, dtype=F32)],
-        [place, x_own, d_hidden1, logit, d_own0, got_d_own0, vectors],
+        [*(have[k] for k in names), place, d_edge, d_shared, got_c, logit, vectors],
         flops=one_hot_flops,
+        name="row_grad",
+        after=(sent0[2],),
+        **room(window, 20),
     )
     d_back = exchange(d_rows)
 
-    saved0 = (
-        (normed_own0, normed_far0),
-        (low_own0, low_far0),
-        (act_own0, act_far0),
-        (branch_own0, branch_far0),
-    )
-    sent0 = sibling_grads(saved0, (bias_own0, bias_far0), (columns_x,))
+    grad_first, grad_second, grad_bias1 = own_grads(1, saved1, biases1, got1, (), (columns_x,))
     got0 = [swap(v, 1) for v in sent0]
     grad_first, grad_second, grad_bias0 = own_grads(
-        0, saved0, (bias_own0, bias_far0), got0, (grad_first, grad_second)
-    )
-
-    marks = run(functools.partial(marks_kernel, sources), [shaped(1, d, dtype=F32)], [returned], name="marks")[0]
-    row_sums = [columns_x, columns_own0, columns_far0, columns_own1, columns_far1, marks]
+        0, saved0, biases0, got0, (grad_first, grad_second)
+    )
+
+    marks = run(functools.partial(marks_kernel, senders), [shaped(1, d, dtype=F32)], [returned], name="marks")[0]
+    row_sums = [columns_x, columns_e0, columns_fw0, columns_ow1, columns_f1, marks]
     columns = run(columns_kernel, [shaped(8, d, dtype=F32)], row_sums)[0]
     columns = run(add_kernel, [shaped(8, d, dtype=F32)], [columns, swap(columns, 1)])[0]
     width = d // lax.axis_size("rep")
-    position = lax.axis_index("rep").astype(jnp.int32).reshape(1)
     *small, grad_bias, over = run(
         finish_kernel,
         [shaped(n, width, dtype=F32) for n in (1, 2, 2, 2)]
@@ -647,19 +714,25 @@
         flops=2 * worst * rows_here * d,
     )
     arrived = lax.all_to_all(outgoing, "ex", split_axis=0, concat_axis=0, tiled=True)
-    outgoing_g = run(pack_kernel, [shaped(worst, d)], [target, grad_output], flops=2 * worst * rows_here * d)[0]
     biases = (b_in[0], swap(b_in[0], 1))
     weights = (w_in[0], swap(w_in[0], 1), w_out[0], swap(w_out[0], 1))
     own_vectors = jnp.concatenate([centroids, ln_gain[0], ln_bias[0], b_out[0]], 0)
-    own_vectors = jnp.concatenate([own_vectors, outgoing_g[:1, : own_vectors.shape[1]]], 0)
+    own_vectors = jnp.concatenate([own_vectors, outgoing[:1, : own_vectors.shape[1]]], 0)
     vectors = lax.all_gather(own_vectors, "rep", axis=1, tiled=True).astype(F32)
+    outgoing_g = run(
+        pack_kernel,
+        [shaped(worst, d)],
+        [target, grad_output],
+        flops=2 * worst * rows_here * d,
+        after=(vectors,),
+    )[0]
 
     operands = (arrived, outgoing_g, target, tokens, grad_output, vectors, biases, weights)
-    cap = min(CAP, worst)
-    outs, over = expert_group(cap, *operands)
-    if cap == worst:
-        return outs
-    return lax.cond(over > 0.0, lambda *_: expert_group(worst, *operands)[0], lambda *kept: kept, *outs)
+    most = ceil_to(experts * max(2, 5 * rows_here // (4 * experts)), 16)
+    if EDGE + SHARED >= most:
+        return expert_group((most, 16), *operands)[0]
+    outs, over = expert_group((EDGE, SHARED), *operands)
+    return lax.cond(over > 0.0, lambda *_: expert_group((most, 16), *operands)[0], lambda *kept: kept, *outs)
 
 
 def solution(mesh):

time: 355 us -> 348 us (0.980)
  Pallas kernels: 177 us -> 163 us
  waiting for transfers between devices: 118 us -> 105 us
  local copies, waits for them, and re-layouts: 8.31 us -> 19.5 us
  blocking collectives: 5.77 us -> 12.7 us
    all_to_all x1, waiting for transfers between devices: 37.4 us -> 22.5 us  [shards(): lax.all_to_all(outgoing, 'ex', split_axis=0, concat_axis=0, tiled=True)]
    pallas_call x24, Pallas kernels: 177 us -> 163 us  [run(): pl.pallas_call(body, out_shape=outs, in_specs=[*specs, *[ANY] * extra], o...]
    unnamed x44 -> x116, local copies, waits for them, and re-layouts: 7.6 us -> 18.8 us
    all_gather x1, blocking collectives: 5.77 us -> 12.7 us  [shards(): vectors = lax.all_gather(own_vectors, 'rep', axis=1, tiled=True).astype(F32)]
    ppermute x19 -> x21, waiting for transfers between devices: 79.8 us -> 82.2 us  [swap(): lax.ppermute(value, 'rep', [(r, r ^ mask) for r in range(lax.axis_size('r...]
    ppermute x19 -> x21, starting transfers between devices: 14.4 us -> 15.4 us  [swap(): lax.ppermute(value, 'rep', [(r, r ^ mask) for r in range(lax.axis_size('r...]
  transfers between devices with their start and end apart: 23 -> 25, of which waited for: 11 -> 13; matrix products, arithmetic and copies ran while one was open for 0% -> 0% of each run, Pallas kernels for 50% -> 44%
where the time goes in v1:
time: 348 us; the launch traced here: 343 us
  Pallas kernels  163 us (47%)
  waiting for transfers between devices  105 us (30%)
  starting transfers between devices  39.3 us (11%)
  local copies, waits for them, and re-layouts  19.5 us (6%)
  blocking collectives  12.7 us (4%)
    pallas_call x24, Pallas kernels, run(): pl.pallas_call(body, out_shape=outs, in_specs=[*specs, *[ANY] * extra], o...  163 us
    ppermute x21, waiting for transfers between devices, swap(): lax.ppermute(value, 'rep', [(r, r ^ mask) for r in range(lax.axis_size('r...  82.2 us
    all_to_all x1, waiting for transfers between devices, shards(): lax.all_to_all(outgoing, 'ex', split_axis=0, concat_axis=0, tiled=True)  22.5 us
    unnamed x116, local copies, waits for them, and re-layouts  18.8 us
    ppermute x21, starting transfers between devices, swap(): lax.ppermute(value, 'rep', [(r, r ^ mask) for r in range(lax.axis_size('r...  15.4 us
    all_gather x1, blocking collectives, shards(): vectors = lax.all_gather(own_vectors, 'rep', axis=1, tiled=True).astype(F32)  12.7 us
    all_to_all x1, starting transfers between devices, shards(): lax.all_to_all(outgoing, 'ex', split_axis=0, concat_axis=0, tiled=True)  7.4 us
  transfers between devices with their start and end apart: 25, of which 13 were waited for; matrix products, arithmetic and copies ran while one was open for 0% of the time, Pallas kernels for 44%

profile of v1, /device:TPU:0, one launch (start us, length us, event | category | flops | bytes accessed | tf_op | source)
XLA Modules:
  0.0 343.4 jit_solution(12999368270646378606)
XLA Ops:
  2.0 4.3 %route.1 = (s32[1,640]{1,0:T(1,128)S(1)}, bf16[832,1024]{1,0:T(8,128)(2,1)}) custom-call(s32[10]{0:T(128)S(1)} %copy-done.48, s32[1]{0:T(128)} %bitcast.8.refs_1_, s32[1,640]{1,0:T(1,128)S(1)} %bitcast.45, bf16[640,1024]{1,0:T(8,128)(2,1)} %refs_2_.2), custom_call_target="tpu_custom_call" | custom-call | flops 68157440 | bytes 188738 | tf_op jit(solution)/shard_map/route/pallas_call | solution.py:57
  6.3 7.4 %all-to-all-start.3 = ((bf16[8,104,1024]{2,1,0:T(8,128)(2,1)}), bf16[8,104,1024]{2,1,0:T(8,128)(2,1)S(1)}, u32[]{:S(2)}, u32[]{:S(2)}) async-start(bf16[8,104,1024]{2,1,0:T(8,128)(2,1)} %bitcast.10), calls=%async_computation.3 | async-start | bytes 3407872 | tf_op jit(solution)/shard_map/all_to_all | solution.py:716
  14.9 12.7 %all_gather.3 = bf16[8,1024]{1,0:T(8,128)(2,1)S(1)} all-gather(bf16[8,256]{1,0:T(8,128)(2,1)S(1)} %concatenate.3), channel_id=1, replica_groups=mesh['ex'=8,'rep'=4] {'rep'}, dimensions={1}, use_global_device_ids=true | all-gather | bytes 20480 | tf_op jit(solution)/shard_map/all_gather | solution.py:721
  27.7 2.7 pack_kernel.1
  31.0 22.5 %all-to-all-done.3 = bf16[8,104,1024]{2,1,0:T(8,128)(2,1)S(1)} async-done(((bf16[8,104,1024]{2,1,0:T(8,128)(2,1)}), bf16[8,104,1024]{2,1,0:T(8,128)(2,1)S(1)}, u32[]{:S(2)}, u32[]{:S(2)}) %all-to-all-start.3) | async-done | bytes 1703968 | tf_op jit(solution)/shard_map/all_to_all | solution.py:716
  54.7 4.8 %all-to-all-start.4 = ((bf16[8,104,1024]{2,1,0:T(8,128)(2,1)}), bf16[8,104,1024]{2,1,0:T(8,128)(2,1)}, u32[]{:S(2)}, u32[]{:S(2)}) async-start(bf16[8,104,1024]{2,1,0:T(8,128)(2,1)} %bitcast.15), calls=%async_computation.4 | async-start | bytes 3407872 | tf_op jit(solution)/shard_map/all_to_all | solution.py:597
  59.6 3.1 place.3
  62.7 1.6 collective-permute-start.18
  65.5 8.6 %forward_sublayer0_E.3 = (bf16[448,1024]{1,0:T(8,128)(2,1)}, bf16[448,2048]{1,0:T(8,128)(2,1)}, bf16[448,2048]{1,0:T(8,128)(2,1)}, bf16[448,1024]{1,0:T(8,128)(2,1)S(1)}) custom-call(bf16[640,1024]{1,0:T(8,128)(2,1)S(1)} %get-tuple-element.217.refs_0_.refs_1_, f32[8,1024]{1,0:T(8,128)S(1)} %copy-done.5, bf16[2,1024]{1,0:T(2,128)(2,1)S(1)} %bitcast.40, ...), custom_call_target="tpu_custom_call" | custom-call | flops 234881024 | bytes 1477120 | tf_op jit(solution)/shard_map/forward_sublayer0_E/pallas_call | solution.py:57
  74.6 19.8 %collective-permute-done.18.refs_0_.refs_1_ = bf16[640,1024]{1,0:T(8,128)(2,1)S(1)} collective-permute-done((bf16[640,1024]{1,0:T(8,128)(2,1)S(1)}, bf16[640,1024]{1,0:T(8,128)(2,1)S(1)}, u32[]{:S(2)}, u32[]{:S(2)}) %collective-permute-start.18) | collective-permute-done | bytes 1310752 | tf_op jit(solution)/shard_map/ppermute | solution.py:24
  94.5 12.2 %forward_sublayer0_FW.3 = (bf16[640,1024]{1,0:T(8,128)(2,1)}, bf16[640,2048]{1,0:T(8,128)(2,1)}, bf16[640,2048]{1,0:T(8,128)(2,1)}, bf16[640,1024]{1,0:T(8,128)(2,1)}) custom-call(bf16[640,1024]{1,0:T(8,128)(2,1)S(1)} %collective-permute-done.18.refs_0_.refs_1_, bf16[640,1024]{1,0:T(8,128)(2,1)S(1)} %get-tuple-element.217.refs_0_.refs_1_, ...), custom_call_target="tpu_custom_call" | custom-call | flops 335544320 | bytes 1706496 | tf_op jit(solution)/shard_map/forward_sublayer0_FW/pallas_call | solution.py:57
  106.7 1.6 collective-permute-start.22
  108.3 3.0 compact_kernel.3.refs_2_.refs_1_.refs_3_.refs_8_
  111.8 2.4 collective-permute-done.24.refs_2_.refs_3_.refs_5_
  114.2 10.5 %forward_sublayer1_F.3 = (bf16[448,1024]{1,0:T(8,128)(2,1)}, bf16[448,2048]{1,0:T(8,128)(2,1)}, bf16[448,2048]{1,0:T(8,128)(2,1)}, bf16[448,1024]{1,0:T(8,128)(2,1)S(1)}) custom-call(bf16[640,1024]{1,0:T(8,128)(2,1)S(1)} %collective-permute-done.18.refs_0_.refs_1_, bf16[640,1024]{1,0:T(8,128)(2,1)} %get-tuple-element.221.refs_3_.refs_5_.refs_1_.refs_2_.refs_4_, ...), custom_call_target="tpu_custom_call" | custom-call | flops 234881024 | bytes 1616384 | tf_op jit(solution)/shard_map/forward_sublayer1_F/pallas_call | solution.py:57
  124.7 1.6 collective-permute-start.28
  126.3 16.0 %collective-permute-done.22.refs_4_.refs_6_.refs_3_ = bf16[640,1024]{1,0:T(8,128)(2,1)} collective-permute-done((bf16[640,1024]{1,0:T(8,128)(2,1)}, bf16[640,1024]{1,0:T(8,128)(2,1)}, u32[]{:S(2)}, u32[]{:S(2)}) %collective-permute-start.22) | collective-permute-done | bytes 1310752 | tf_op jit(solution)/shard_map/ppermute | solution.py:24
  142.3 13.4 %forward_sublayer1_OW.3 = (bf16[640,1024]{1,0:T(8,128)(2,1)}, bf16[640,2048]{1,0:T(8,128)(2,1)}, bf16[640,2048]{1,0:T(8,128)(2,1)}, bf16[640,1024]{1,0:T(8,128)(2,1)S(1)}, bf16[192,1024]{1,0:T(8,128)(2,1)S(1)}) custom-call(bf16[640,1024]{1,0:T(8,128)(2,1)S(1)} %get-tuple-element.217.refs_0_.refs_1_, ...), custom_call_target="tpu_custom_call" | custom-call | flops 335544320 | bytes 1952256 | tf_op jit(solution)/shard_map/forward_sublayer1_OW/pallas_call | solution.py:57
  155.8 1.6 collective-permute-start.29
  157.9 12.4 %collective-permute-done.23.refs_3_.refs_1_.refs_2_ = bf16[640,1024]{1,0:T(8,128)(2,1)S(1)} collective-permute-done((bf16[640,1024]{1,0:T(8,128)(2,1)S(1)}, bf16[640,1024]{1,0:T(8,128)(2,1)S(1)}, u32[]{:S(2)}, u32[]{:S(2)}) %collective-permute-start.23) | collective-permute-done | bytes 1310752 | tf_op jit(solution)/shard_map/ppermute | solution.py:24
  170.3 12.6 %backward_sublayer1_OW.3 = (bf16[640,1024]{1,0:T(8,128)(2,1)}, bf16[640,2048]{1,0:T(8,128)(2,1)}, bf16[640,1024]{1,0:T(8,128)(2,1)S(1)}, f32[3,1024]{1,0:T(4,128)S(1)}, f32[1,2048]{1,0:T(1,128)S(1)}) custom-call(bf16[640,1024]{1,0:T(8,128)(2,1)S(1)} %get-tuple-element.217.refs_0_.refs_1_, bf16[640,1024]{1,0:T(8,128)(2,1)S(1)} %collective-permute-done.18.refs_0_.refs_1_, ...), custom_call_target="tpu_custom_call" | custom-call | flops 335544320 | bytes 2092288 | tf_op jit(solution)/shard_map/backward_sublayer1_OW/pallas_call | solution.py:57
  183.0 13.5 %collective-permute-done.30.refs_11_ = f32[1,128]{1,0:T(1,128)S(1)} collective-permute-done((f32[1,128]{1,0:T(1,128)}, f32[1,128]{1,0:T(1,128)S(1)}, u32[]{:S(2)}, u32[]{:S(2)}) %collective-permute-start.30) | collective-permute-done | bytes 544 | tf_op jit(solution)/shard_map/ppermute | solution.py:24
  196.5 4.6 %result.3 = (bf16[832,1024]{1,0:T(8,128)(2,1)S(1)}, f32[640,128]{1,0:T(8,128)S(1)}) custom-call(bf16[640,1024]{1,0:T(8,128)(2,1)S(1)} %get-tuple-element.217.refs_0_.refs_1_, bf16[640,1024]{1,0:T(8,128)(2,1)S(1)} %collective-permute-done.18.refs_0_.refs_1_, bf16[448,1024]{1,0:T(8,128)(2,1)S(1)} %get-tuple-element.220.refs_9_.refs_2_.refs_4_, ...), custom_call_target="tpu_custom_call" | custom-call | flops 68157440 | bytes 760080 | tf_op jit(solution)/shard_map/result/pallas_call | solution.py:57
  203.1 5.7 %all-to-all-start.5 = ((bf16[8,104,1024]{2,1,0:T(8,128)(2,1)}), bf16[8,104,1024]{2,1,0:T(8,128)(2,1)}, u32[]{:S(2)}, u32[]{:S(2)}) async-start(bf16[8,104,1024]{2,1,0:T(8,128)(2,1)} %bitcast.38), calls=%async_computation.5 | async-start | bytes 3407872 | tf_op jit(solution)/shard_map/all_to_all | solution.py:629
  208.8 1.5 collective-permute-start.26
  212.4 10.0 %backward_sublayer1_F.3 = (bf16[448,1024]{1,0:T(8,128)(2,1)}, bf16[448,2048]{1,0:T(8,128)(2,1)}, bf16[448,1024]{1,0:T(8,128)(2,1)S(1)}, f32[3,1024]{1,0:T(4,128)S(1)}, f32[1,2048]{1,0:T(1,128)S(1)}) custom-call(bf16[640,1024]{1,0:T(8,128)(2,1)S(1)} %collective-permute-done.18.refs_0_.refs_1_, bf16[640,1024]{1,0:T(8,128)(2,1)S(1)} %copy-done.11, ...), custom_call_target="tpu_custom_call" | custom-call | flops 234881024 | bytes 1699072 | tf_op jit(solution)/shard_map/backward_sublayer1_F/pallas_call | solution.py:57
  223.0 8.5 %sibling_kernel.6 = (bf16[1024,1024]{1,0:T(8,128)(2,1)S(1)}, bf16[1024,1024]{1,0:T(8,128)(2,1)S(1)}, f32[1,1024]{1,0:T(1,128)S(1)}) custom-call(bf16[640,1024]{1,0:T(8,128)(2,1)} %get-tuple-element.230.refs_0_, bf16[448,1024]{1,0:T(8,128)(2,1)} %get-tuple-element.231.refs_1_, bf16[640,2048]{1,0:T(8,128)(2,1)} %get-tuple-element.232.refs_2_, ...), custom_call_target="tpu_custom_call" | custom-call | flops 285212672 | bytes 1099008 | tf_op jit(solution)/shard_map/sibling_kernel/pallas_call | solution.py:57
  232.8 1.3 copy-done.53
  234.2 6.6 %collective-permute-done.26.refs_9_ = bf16[640,1024]{1,0:T(8,128)(2,1)S(1)} collective-permute-done((bf16[640,1024]{1,0:T(8,128)(2,1)}, bf16[640,1024]{1,0:T(8,128)(2,1)S(1)}, u32[]{:S(2)}, u32[]{:S(2)}) %collective-permute-start.26) | collective-permute-done | bytes 1310752 | tf_op jit(solution)/shard_map/ppermute | solution.py:24
  240.7 13.8 %backward_sublayer0_FW.3 = (bf16[640,1024]{1,0:T(8,128)(2,1)}, bf16[640,2048]{1,0:T(8,128)(2,1)}, bf16[640,1024]{1,0:T(8,128)(2,1)S(1)}, f32[3,1024]{1,0:T(4,128...) custom-call(bf16[640,1024]{1,0:T(8,128)(2,1)S(1)} %collective-permute-done.18.refs_0_.refs_1_, ...), custom_call_target="tpu_custom_call" | custom-call | flops 335544320 | bytes 2362624 | tf_op jit(solution)/shard_map/backward_sublayer0_FW/pallas_call | solution.py:57
  255.1 1.5 collective-permute-start.27
  256.7 3.7 %collective-permute-done.25.refs_5_ = bf16[448,1024]{1,0:T(8,128)(2,1)S(1)} collective-permute-done((bf16[448,1024]{1,0:T(8,128)(2,1)S(1)}, bf16[448,1024]{1,0:T(8,128)(2,1)S(1)}, u32[]{:S(2)}, u32[]{:S(2)}) %collective-permute-start.25) | collective-permute-done | bytes 917536 | tf_op jit(solution)/shard_map/ppermute | solution.py:24
  260.4 11.2 %backward_sublayer0_E.3 = (bf16[448,1024]{1,0:T(8,128)(2,1)}, bf16[448,2048]{1,0:T(8,128)(2,1)}, bf16[448,1024]{1,0:T(8,128)(2,1)S(1)}, f32[3,1024]{1,0:T(4,128)...) custom-call(bf16[640,1024]{1,0:T(8,128)(2,1)S(1)} %get-tuple-element.217.refs_0_.refs_1_, ...), custom_call_target="tpu_custom_call" | custom-call | flops 7516192768 | bytes 1953024 | tf_op jit(solution)/shard_map/backward_sublayer0_E/pallas_call | solution.py:57
  271.7 8.4 %sibling_kernel.7 = (bf16[1024,1024]{1,0:T(8,128)(2,1)S(1)}, bf16[1024,1024]{1,0:T(8,128)(2,1)S(1)}, f32[1,1024]{1,0:T(1,128)S(1)}) custom-call(bf16[448,1024]{1,0:T(8,128)(2,1)} %get-tuple-element.248.refs_0_, bf16[640,1024]{1,0:T(8,128)(2,1)} %get-tuple-element.249.refs_1_, bf16[448,2048]{1,0:T(8,128)(2,1)} %get-tuple-element.250.refs_2_, ...), custom_call_target="tpu_custom_call" | custom-call | flops 285212672 | bytes 1099008 | tf_op jit(solution)/shard_map/sibling_kernel/pallas_call | solution.py:57
  281.4 1.3 copy-done.52
  282.7 2.3 collective-permute-done.27.refs_7_
  285.0 3.5 %row_grad.3 = (bf16[832,1024]{1,0:T(8,128)(2,1)S(1)}, f32[1,1024]{1,0:T(1,128)S(1)}) custom-call(bf16[640,1024]{1,0:T(8,128)(2,1)S(1)} %get-tuple-element.217.refs_0_.refs_1_, bf16[640,1024]{1,0:T(8,128)(2,1)S(1)} %collective-permute-done.18.refs_0_.refs_1_, bf16[448,1024]{1,0:T(8,128)(2,1)S(1)} %get-tuple-element.228.refs_2_, ...), custom_call_target="tpu_custom_call" | custom-call | flops 68157440 | bytes 678352 | tf_op jit(solution)/shard_map/row_grad/pallas_call | solution.py:57
  289.7 6.0 %all-to-all-start.6 = ((bf16[8,104,1024]{2,1,0:T(8,128)(2,1)}), bf16[8,104,1024]{2,1,0:T(8,128)(2,1)S(1)}, u32[]{:S(2)}, u32[]{:S(2)}) async-start(bf16[8,104,1024]{2,1,0:T(8,128)(2,1)} %bitcast.37), calls=%async_computation.6 | async-start | bytes 3407872 | tf_op jit(solution)/shard_map/all_to_all | solution.py:666
  297.0 1.5 marks.3.refs_5_
  298.5 1.5 collective-permute-done.38.refs_12_
  300.7 2.6 collective-permute-done.37.refs_11_
  304.6 11.1 %own_grads_sublayer1.3 = (f32[2,1024,1024]{2,1,0:T(8,128)}, f32[2,1024,1024]{2,1,0:T(8,128)}, f32[1,1024]{1,0:T(1,128)S(1)}) custom-call(bf16[640,1024]{1,0:T(8,128)(2,1)} %get-tuple-element.230.refs_0_, bf16[448,1024]{1,0:T(8,128)(2,1)} %get-tuple-element.231.refs_1_, bf16[640,2048]{1,0:T(8,128)(2,1)} %get-tuple-element.232.refs_2_, ...), custom_call_target="tpu_custom_call" | custom-call | flops 285212672 | bytes 2147840 | tf_op jit(solution)/shard_map/own_grads_sublayer1/pallas_call | solution.py:57
  315.7 1.6 collective-permute-start.32
  317.3 4.7 %unpack_kernel.6 = bf16[640,1024]{1,0:T(8,128)(2,1)} custom-call(s32[1,640]{1,0:T(1,128)S(1)} %copy-done.74, bf16[832,1024]{1,0:T(8,128)(2,1)} %bitcast.21.refs_0_.refs_1_, bf16[640,1024]{1,0:T(8,128)(2,1)S(1)} %copy-done.59), custom_call_target="tpu_custom_call" | custom-call | flops 68157440 | bytes 270496 | tf_op jit(solution)/shard_map/unpack_kernel/pallas_call | solution.py:57
  322.0 1.3 copy-done.63
  324.0 11.5 %own_grads_sublayer0.3 = (f32[2,1024,1024]{2,1,0:T(8,128)}, f32[2,1024,1024]{2,1,0:T(8,128)}, f32[1,1024]{1,0:T(1,128)S(1)}) custom-call(bf16[448,1024]{1,0:T(8,128)(2,1)} %get-tuple-element.248.refs_0_, bf16[640,1024]{1,0:T(8,128)(2,1)} %get-tuple-element.249.refs_1_, ...), custom_call_target="tpu_custom_call", output_to_operand_aliasing={{0}: (13, {}), {1}: (14, {})} | custom-call | flops 285212672 | bytes 3196416 | tf_op jit(solution)/shard_map/own_grads_sublayer0/pallas_call | solution.py:57
  336.3 3.6 %unpack_kernel.7 = bf16[640,1024]{1,0:T(8,128)(2,1)S(1)} custom-call(s32[1,640]{1,0:T(1,128)S(1)} %copy-done.74, bf16[832,1024]{1,0:T(8,128)(2,1)S(1)} %bitcast.36, bf16[640,1024]{1,0:T(8,128)(2,1)} %refs_2_.3), custom_call_target="tpu_custom_call" | custom-call | flops 68157440 | bytes 270496 | tf_op jit(solution)/shard_map/unpack_kernel/pallas_call | solution.py:57
  339.9 2.2 conditional.1
  (147 shorter events, 21.8 us)
Async XLA Ops:
  6.3 21.4 %copy-start.73 = (s32[1,640]{1,0:T(1,128)}, s32[1,640]{1,0:T(1,128)S(1)}, u32[]{:S(2)}) copy-start(s32[1,640]{1,0:T(1,128)S(1)} %get-tuple-element.219.refs_0_) | copy-start | bytes 7684
  6.3 8.6 %copy-start.81 = (bf16[1,2,256]{2,1,0:T(2,128)(2,1)S(1)}, bf16[1,2,256]{2,1,0:T(2,128)(2,1)}, u32[]{:S(2)}) copy-start(bf16[1,2,256]{2,1,0:T(2,128)(2,1)} %param.17) | copy-start | bytes 3076
  6.3 8.6 %copy-start.82 = (bf16[1,2,256]{2,1,0:T(2,128)(2,1)S(1)}, bf16[1,2,256]{2,1,0:T(2,128)(2,1)}, u32[]{:S(2)}) copy-start(bf16[1,2,256]{2,1,0:T(2,128)(2,1)} %param.18) | copy-start | bytes 3076
  6.3 21.4 %copy-start.60 = (bf16[640,1024]{1,0:T(8,128)(2,1)S(1)}, bf16[640,1024]{1,0:T(8,128)(2,1)}, u32[]{:S(2)}) copy-start(bf16[640,1024]{1,0:T(8,128)(2,1)} %refs_2_.3) | copy-start | bytes 3932164
  6.3 47.2 %all-to-all-start.3 = ((bf16[8,104,1024]{2,1,0:T(8,128)(2,1)}), bf16[8,104,1024]{2,1,0:T(8,128)(2,1)S(1)}, u32[]{:S(2)}, u32[]{:S(2)}) async-start(bf16[8,104,1024]{2,1,0:T(8,128)(2,1)} %bitcast.10), calls=%async_computation.3 | async-start | bytes 3407872 | tf_op jit(solution)/shard_map/all_to_all | solution.py:716
  13.7 51.8 %collective-permute-start.20 = (bf16[2,1024,1024]{2,1,0:T(8,128)(2,1)}, bf16[2,1024,1024]{2,1,0:T(8,128)(2,1)}, u32[]{:S(2)}, u32[]{:S(2)}) collective-permute-start(bf16[2,1024,1024]{2,1,0:T(8,128)(2,1)} %bitcast.47), channel_id=1, source_target_pairs={{0,1},{1,0},{2,3},{3,2},{4,5},{5,4},{6,7},{7,6},{8,9},{9,8},{10,11... | collective-permute-start | bytes 12582920 | tf_op jit(solution)/shard_map/ppermute | solution.py:24
  13.7 51.8 %collective-permute-start.21 = (bf16[2,1024,1024]{2,1,0:T(8,128)(2,1)}, bf16[2,1024,1024]{2,1,0:T(8,128)(2,1)}, u32[]{:S(2)}, u32[]{:S(2)}) collective-permute-start(bf16[2,1024,1024]{2,1,0:T(8,128)(2,1)} %bitcast.57), channel_id=1, source_target_pairs={{0,1},{1,0},{2,3},{3,2},{4,5},{5,4},{6,7},{7,6},{8,9},{9,8},{10,11... | collective-permute-start | bytes 12582920 | tf_op jit(solution)/shard_map/ppermute | solution.py:24
  54.7 53.5 %all-to-all-start.4 = ((bf16[8,104,1024]{2,1,0:T(8,128)(2,1)}), bf16[8,104,1024]{2,1,0:T(8,128)(2,1)}, u32[]{:S(2)}, u32[]{:S(2)}) async-start(bf16[8,104,1024]{2,1,0:T(8,128)(2,1)} %bitcast.15), calls=%async_computation.4 | async-start | bytes 3407872 | tf_op jit(solution)/shard_map/all_to_all | solution.py:597
  62.7 45.6 %copy-start.26 = (s32[1,832]{1,0:T(1,128)}, s32[1,832]{1,0:T(1,128)S(1)}, u32[]{:S(2)}) copy-start(s32[1,832]{1,0:T(1,128)S(1)} %get-tuple-element.218.refs_0_.refs_9_.refs_4_) | copy-start | bytes 9988
  62.7 31.8 %collective-permute-start.18 = (bf16[640,1024]{1,0:T(8,128)(2,1)S(1)}, bf16[640,1024]{1,0:T(8,128)(2,1)S(1)}, u32[]{:S(2)}, u32[]{:S(2)}) collective-permute-start(bf16[640,1024]{1,0:T(8,128)(2,1)S(1)} %get-tuple-element.217.refs_0_.refs_1_), channel_id=1, source_target_pairs={{0,2},{1,3},{2,0},{3,1},{4,6},{5,7},{6,4},{7,5},{8,10},{9,11},{10,... | collective-permute-start | bytes 3932168 | tf_op jit(solution)/shard_map/ppermute | solution.py:24
  64.3 1.2 collective-permute-start.19
  74.1 40.2 %collective-permute-start.24 = (bf16[448,1024]{1,0:T(8,128)(2,1)S(1)}, bf16[448,1024]{1,0:T(8,128)(2,1)}, u32[]{:S(2)}, u32[]{:S(2)}) collective-permute-start(bf16[448,1024]{1,0:T(8,128)(2,1)S(1)} %get-tuple-element.220.refs_9_.refs_2_.refs_4_), channel_id=1, source_target_pairs={{0,2},{1,3},{2,0},{3,1},{4,6},{5,7},{6,4},{7,5},{8,10},{9,11},{10,... | collective-permute-start | bytes 2752520 | tf_op jit(solution)/shard_map/ppermute | solution.py:24
  106.7 35.7 %collective-permute-start.22 = (bf16[640,1024]{1,0:T(8,128)(2,1)}, bf16[640,1024]{1,0:T(8,128)(2,1)}, u32[]{:S(2)}, u32[]{:S(2)}) collective-permute-start(bf16[640,1024]{1,0:T(8,128)(2,1)} %get-tuple-element.221.refs_3_.refs_5_.refs_1_.refs_2_.refs_4_), channel_id=1, source_target_pairs={{0,2},{1,3},{2,0},{3,1},{4,6},{5,7},{6,4},{7,5},{8,10},{9,11},{10,... | collective-permute-start | bytes 3932168 | tf_op jit(solution)/shard_map/ppermute | solution.py:24
  111.2 85.2 %copy-start.2 = (bf16[640,1024]{1,0:T(8,128)(2,1)}, bf16[640,1024]{1,0:T(8,128)(2,1)S(1)}, u32[]{:S(2)}) copy-start(bf16[640,1024]{1,0:T(8,128)(2,1)S(1)} %compact_kernel.3.refs_2_.refs_1_.refs_3_.refs_8_) | copy-start | bytes 3932164
  111.2 59.1 %collective-permute-start.23 = (bf16[640,1024]{1,0:T(8,128)(2,1)S(1)}, bf16[640,1024]{1,0:T(8,128)(2,1)S(1)}, u32[]{:S(2)}, u32[]{:S(2)}) collective-permute-start(bf16[640,1024]{1,0:T(8,128)(2,1)S(1)} %compact_kernel.3.refs_2_.refs_1_.refs_3_.refs_8_), channel_id=1, source_target_pairs={{0,2},{1,3},{2,0},{3,1},{4,6},{5,7},{6,4},{7,5},{8,10},{9,11},{10,... | collective-permute-start | bytes 3932168 | tf_op jit(solution)/shard_map/ppermute | solution.py:24
  124.7 71.8 %collective-permute-start.28 = (bf16[448,1024]{1,0:T(8,128)(2,1)S(1)}, bf16[448,1024]{1,0:T(8,128)(2,1)S(1)}, u32[]{:S(2)}, u32[]{:S(2)}) collective-permute-start(bf16[448,1024]{1,0:T(8,128)(2,1)S(1)} %get-tuple-element.244), channel_id=1, source_target_pairs={{0,2},{1,3},{2,0},{3,1},{4,6},{5,7},{6,4},{7,5},{8,10},{9,11},{10,... | collective-permute-start | bytes 2752520 | tf_op jit(solution)/shard_map/ppermute | solution.py:24
  155.8 40.7 %collective-permute-start.29 = (bf16[192,1024]{1,0:T(8,128)(2,1)S(1)}, bf16[192,1024]{1,0:T(8,128)(2,1)S(1)}, u32[]{:S(2)}, u32[]{:S(2)}) collective-permute-start(bf16[192,1024]{1,0:T(8,128)(2,1)S(1)} %get-tuple-element.245), channel_id=1, source_target_pairs={{0,2},{1,3},{2,0},{3,1},{4,6},{5,7},{6,4},{7,5},{8,10},{9,11},{10,... | collective-permute-start | bytes 1179656 | tf_op jit(solution)/shard_map/ppermute | solution.py:24
  157.4 39.1 %collective-permute-start.30 = (f32[1,128]{1,0:T(1,128)}, f32[1,128]{1,0:T(1,128)S(1)}, u32[]{:S(2)}, u32[]{:S(2)}) collective-permute-start(f32[1,128]{1,0:T(1,128)} %get-tuple-element.246.refs_10_), channel_id=1, source_target_pairs={{0,2},{1,3},{2,0},{3,1},{4,6},{5,7},{6,4},{7,5},{8,10},{9,11},{10,... | collective-permute-start | bytes 1544 | tf_op jit(solution)/shard_map/ppermute | solution.py:24
  170.3 12.6 %copy-start.10 = (bf16[640,1024]{1,0:T(8,128)(2,1)}, bf16[640,1024]{1,0:T(8,128)(2,1)S(1)}, u32[]{:S(2)}) copy-start(bf16[640,1024]{1,0:T(8,128)(2,1)S(1)} %collective-permute-done.23.refs_3_.refs_1_.refs_2_) | copy-start | bytes 3932164
  170.3 26.2 %copy-start.27 = (s32[1,832]{1,0:T(1,128)S(1)}, s32[1,832]{1,0:T(1,128)}, u32[]{:S(2)}) copy-start(s32[1,832]{1,0:T(1,128)} %copy-done.26) | copy-start | bytes 9988
  183.0 18.2 %copy-start.15 = (bf16[640,1024]{1,0:T(8,128)(2,1)}, bf16[640,1024]{1,0:T(8,128)(2,1)S(1)}, u32[]{:S(2)}) copy-start(bf16[640,1024]{1,0:T(8,128)(2,1)S(1)} %get-tuple-element.223.refs_4_.refs_8_) | copy-start | bytes 3932164
  183.0 18.2 %copy-start.32 = (f32[3,1024]{1,0:T(4,128)}, f32[3,1024]{1,0:T(4,128)S(1)}, u32[]{:S(2)}) copy-start(f32[3,1024]{1,0:T(4,128)S(1)} %get-tuple-element.262.refs_3_) | copy-start | bytes 36868
  203.1 86.6 %all-to-all-start.5 = ((bf16[8,104,1024]{2,1,0:T(8,128)(2,1)}), bf16[8,104,1024]{2,1,0:T(8,128)(2,1)}, u32[]{:S(2)}, u32[]{:S(2)}) async-start(bf16[8,104,1024]{2,1,0:T(8,128)(2,1)} %bitcast.38), calls=%async_computation.5 | async-start | bytes 3407872 | tf_op jit(solution)/shard_map/all_to_all | solution.py:629
  208.8 31.9 %collective-permute-start.26 = (bf16[640,1024]{1,0:T(8,128)(2,1)}, bf16[640,1024]{1,0:T(8,128)(2,1)S(1)}, u32[]{:S(2)}, u32[]{:S(2)}) collective-permute-start(bf16[640,1024]{1,0:T(8,128)(2,1)} %copy-done.15), channel_id=1, source_target_pairs={{0,2},{1,3},{2,0},{3,1},{4,6},{5,7},{6,4},{7,5},{8,10},{9,11},{10,... | collective-permute-start | bytes 3932168 | tf_op jit(solution)/shard_map/ppermute | solution.py:24
  222.4 9.1 %copy-start.20 = (f32[1,2048]{1,0:T(1,128)}, f32[1,2048]{1,0:T(1,128)S(1)}, u32[]{:S(2)}) copy-start(f32[1,2048]{1,0:T(1,128)S(1)} %get-tuple-element.238.refs_9_) | copy-start | bytes 24580
  222.4 9.1 %copy-start.35 = (f32[3,1024]{1,0:T(4,128)}, f32[3,1024]{1,0:T(4,128)S(1)}, u32[]{:S(2)}) copy-start(f32[3,1024]{1,0:T(4,128)S(1)} %get-tuple-element.263.refs_4_) | copy-start | bytes 36868
  222.4 38.0 %collective-permute-start.25 = (bf16[448,1024]{1,0:T(8,128)(2,1)S(1)}, bf16[448,1024]{1,0:T(8,128)(2,1)S(1)}, u32[]{:S(2)}, u32[]{:S(2)}) collective-permute-start(bf16[448,1024]{1,0:T(8,128)(2,1)S(1)} %get-tuple-element.226.refs_7_), channel_id=1, source_target_pairs={{0,2},{1,3},{2,0},{3,1},{4,6},{5,7},{6,4},{7,5},{8,10},{9,11},{10,... | collective-permute-start | bytes 2752520 | tf_op jit(solution)/shard_map/ppermute | solution.py:24
  223.0 17.8 %copy-start.3 = (bf16[640,1024]{1,0:T(8,128)(2,1)S(1)}, bf16[640,1024]{1,0:T(8,128)(2,1)}, u32[]{:S(2)}) copy-start(bf16[640,1024]{1,0:T(8,128)(2,1)} %copy-done.2) | copy-start | bytes 3932164
  223.0 17.8 %copy-start.8 = (f32[8,1024]{1,0:T(8,128)S(1)}, f32[8,1024]{1,0:T(8,128)}, u32[]{:S(2)}) copy-start(f32[8,1024]{1,0:T(8,128)} %copy-done.4) | copy-start | bytes 98308
  223.0 17.8 %copy-start.12 = (bf16[640,1024]{1,0:T(8,128)(2,1)S(1)}, bf16[640,1024]{1,0:T(8,128)(2,1)}, u32[]{:S(2)}) copy-start(bf16[640,1024]{1,0:T(8,128)(2,1)} %copy-done.10) | copy-start | bytes 3932164
  223.0 17.8 %copy-start.16 = (bf16[640,1024]{1,0:T(8,128)(2,1)S(1)}, bf16[640,1024]{1,0:T(8,128)(2,1)}, u32[]{:S(2)}) copy-start(bf16[640,1024]{1,0:T(8,128)(2,1)} %copy-done.15) | copy-start | bytes 3932164
  234.2 20.4 %copy-start.43 = (f32[1,1024]{1,0:T(1,128)}, f32[1,1024]{1,0:T(1,128)S(1)}, u32[]{:S(2)}) copy-start(f32[1,1024]{1,0:T(1,128)S(1)} %get-tuple-element.239.refs_16_) | copy-start | bytes 12292
  255.1 16.5 %copy-start.22 = (f32[1,2048]{1,0:T(1,128)}, f32[1,2048]{1,0:T(1,128)S(1)}, u32[]{:S(2)}) copy-start(f32[1,2048]{1,0:T(1,128)S(1)} %get-tuple-element.257.refs_9_) | copy-start | bytes 24580
  255.1 29.9 %collective-permute-start.27 = (bf16[640,1024]{1,0:T(8,128)(2,1)S(1)}, bf16[640,1024]{1,0:T(8,128)(2,1)S(1)}, u32[]{:S(2)}, u32[]{:S(2)}) collective-permute-start(bf16[640,1024]{1,0:T(8,128)(2,1)S(1)} %get-tuple-element.240.refs_3_), channel_id=1, source_target_pairs={{0,2},{1,3},{2,0},{3,1},{4,6},{5,7},{6,4},{7,5},{8,10},{9,11},{10,... | collective-permute-start | bytes 3932168 | tf_op jit(solution)/shard_map/ppermute | solution.py:24
  271.6 13.4 %copy-start.18 = (f32[640,128]{1,0:T(8,128)S(1)}, f32[640,128]{1,0:T(8,128)}, u32[]{:S(2)}) copy-start(f32[640,128]{1,0:T(8,128)} %copy-done.17) | copy-start | bytes 983044
  271.7 13.4 %copy-start.28 = (s32[1,832]{1,0:T(1,128)S(1)}, s32[1,832]{1,0:T(1,128)}, u32[]{:S(2)}) copy-start(s32[1,832]{1,0:T(1,128)} %copy-done.26) | copy-start | bytes 9988
  289.7 46.5 %all-to-all-start.6 = ((bf16[8,104,1024]{2,1,0:T(8,128)(2,1)}), bf16[8,104,1024]{2,1,0:T(8,128)(2,1)S(1)}, u32[]{:S(2)}, u32[]{:S(2)}) async-start(bf16[8,104,1024]{2,1,0:T(8,128)(2,1)} %bitcast.37), calls=%async_computation.6 | async-start | bytes 3407872 | tf_op jit(solution)/shard_map/all_to_all | solution.py:666
  295.8 8.8 %copy-start.21 = (f32[1,2048]{1,0:T(1,128)S(1)}, f32[1,2048]{1,0:T(1,128)}, u32[]{:S(2)}) copy-start(f32[1,2048]{1,0:T(1,128)} %copy-done.20) | copy-start | bytes 24580
  295.8 4.4 %collective-permute-start.36 = (bf16[1024,1024]{1,0:T(8,128)(2,1)}, bf16[1024,1024]{1,0:T(8,128)(2,1)S(1)}, u32[]{:S(2)}, u32[]{:S(2)}) collective-permute-start(bf16[1024,1024]{1,0:T(8,128)(2,1)} %copy-done.53), channel_id=1, source_target_pairs={{0,1},{1,0},{2,3},{3,2},{4,5},{5,4},{6,7},{7,6},{8,9},{9,8},{10,11... | collective-permute-start | bytes 6291464 | tf_op jit(solution)/shard_map/ppermute | solution.py:24
  295.9 7.4 %collective-permute-start.37 = (bf16[1024,1024]{1,0:T(8,128)(2,1)}, bf16[1024,1024]{1,0:T(8,128)(2,1)S(1)}, u32[]{:S(2)}, u32[]{:S(2)}) collective-permute-start(bf16[1024,1024]{1,0:T(8,128)(2,1)} %copy-done.50), channel_id=1, source_target_pairs={{0,1},{1,0},{2,3},{3,2},{4,5},{5,4},{6,7},{7,6},{8,9},{9,8},{10,11... | collective-permute-start | bytes 6291464 | tf_op jit(solution)/shard_map/ppermute | solution.py:24
  296.4 25.6 %collective-permute-start.33 = (bf16[1024,1024]{1,0:T(8,128)(2,1)}, bf16[1024,1024]{1,0:T(8,128)(2,1)S(1)}, u32[]{:S(2)}, u32[]{:S(2)}) collective-permute-start(bf16[1024,1024]{1,0:T(8,128)(2,1)} %copy-done.52), channel_id=1, source_target_pairs={{0,1},{1,0},{2,3},{3,2},{4,5},{5,4},{6,7},{7,6},{8,9},{9,8},{10,11... | collective-permute-start | bytes 6291464 | tf_op jit(solution)/shard_map/ppermute | solution.py:24
  296.5 25.5 %collective-permute-start.34 = (bf16[1024,1024]{1,0:T(8,128)(2,1)}, bf16[1024,1024]{1,0:T(8,128)(2,1)S(1)}, u32[]{:S(2)}, u32[]{:S(2)}) collective-permute-start(bf16[1024,1024]{1,0:T(8,128)(2,1)} %copy-done.51), channel_id=1, source_target_pairs={{0,1},{1,0},{2,3},{3,2},{4,5},{5,4},{6,7},{7,6},{8,9},{9,8},{10,11... | collective-permute-start | bytes 6291464 | tf_op jit(solution)/shard_map/ppermute | solution.py:24
  296.9 3.1 collective-permute-start.38
  300.1 15.6 %collective-permute-start.31 = (f32[8,1024]{1,0:T(8,128)S(1)}, f32[8,1024]{1,0:T(8,128)S(1)}, u32[]{:S(2)}, u32[]{:S(2)}) collective-permute-start(f32[8,1024]{1,0:T(8,128)S(1)} %columns_kernel.3.refs_0_), channel_id=1, source_target_pairs={{0,1},{1,0},{2,3},{3,2},{4,5},{5,4},{6,7},{7,6},{8,9},{9,8},{10,11... | collective-permute-start | bytes 98312 | tf_op jit(solution)/shard_map/ppermute | solution.py:24
  300.2 17.1 %copy-start.59 = (bf16[640,1024]{1,0:T(8,128)(2,1)S(1)}, bf16[640,1024]{1,0:T(8,128)(2,1)}, u32[]{:S(2)}) copy-start(bf16[640,1024]{1,0:T(8,128)(2,1)} %refs_2_.2) | copy-start | bytes 3932164
  300.2 17.1 %copy-start.74 = (s32[1,640]{1,0:T(1,128)S(1)}, s32[1,640]{1,0:T(1,128)}, u32[]{:S(2)}) copy-start(s32[1,640]{1,0:T(1,128)} %copy-done.73) | copy-start | bytes 7684
  300.3 21.7 %collective-permute-start.35 = (f32[1,1024]{1,0:T(1,128)S(1)}, f32[1,1024]{1,0:T(1,128)S(1)}, u32[]{:S(2)}, u32[]{:S(2)}) collective-permute-start(f32[1,1024]{1,0:T(1,128)S(1)} %get-tuple-element.258.refs_10_), channel_id=1, source_target_pairs={{0,1},{1,0},{2,3},{3,2},{4,5},{5,4},{6,7},{7,6},{8,9},{9,8},{10,11... | collective-permute-start | bytes 12296 | tf_op jit(solution)/shard_map/ppermute | solution.py:24
  315.7 19.9 %collective-permute-start.32 = (f32[8,1024]{1,0:T(8,128)S(1)}, f32[8,1024]{1,0:T(8,128)S(1)}, u32[]{:S(2)}, u32[]{:S(2)}) collective-permute-start(f32[8,1024]{1,0:T(8,128)S(1)} %add_kernel.3.refs_1_), channel_id=1, source_target_pairs={{0,2},{1,3},{2,0},{3,1},{4,6},{5,7},{6,4},{7,5},{8,10},{9,11},{10,... | collective-permute-start | bytes 98312 | tf_op jit(solution)/shard_map/ppermute | solution.py:24
  (35 other events, 115.8 us)

commit v2 on v1

--- a/solution.py
+++ b/solution.py
@@ -16,8 +16,9 @@
 ANY = pl.BlockSpec(memory_space=pl.ANY)
 HBM = pl.BlockSpec(memory_space=pltpu.HBM)
 EDGE, SHARED = 448, 192
+TAIL = 16
 SCALE = 16
-LAST_COST = 128
+COSTS = {(0, "E"): 128, (1, "F"): 48}
 
 
 def swap(value, mask):
@@ -191,12 +192,15 @@
     out_ref[...] = jnp.where(alive, up(values) + moved, 0.0).astype(BF16)
 
 
-def compact_kernel(place, arrived, rows_ref):
-    rows_ref[...] = dot(onehot(rows_ref.shape[0], place[...]), arrived[...], 1, 0).astype(BF16)
+def compact_kernel(place, arrived, edge_ref, shared_ref):
+    edge = edge_ref.shape[0]
+    rows = dot(onehot(edge + shared_ref.shape[0], place[...]), arrived[...], 1, 0).astype(BF16)
+    edge_ref[...] = rows[:edge]
+    shared_ref[...] = rows[edge:]
 
 
 def place_kernel(senders, edge, position, arrived, rows_ref, place_ref, count_ref):
-    n, window = arrived.shape[0], rows_ref.shape[0]
+    n, window = arrived.shape[0], rows_ref.shape[0] - TAIL
     slots = n // senders
     lane = iota((1, n), 1).astype(F32)
     place, total = jnp.full((1, n), -1.0, F32), jnp.zeros((1, 1), F32)
@@ -209,7 +213,9 @@
     place = jnp.where(backwards, window + edge - 1 - place, place)
     place_ref[...] = place.astype(jnp.int32)
     count_ref[...] = jnp.broadcast_to(total, count_ref.shape)
-    rows_ref[...] = dot(onehot(window, place_ref[...]), arrived[...], 1, 0).astype(BF16)
+    rows_ref[0:window, :] = dot(onehot(window, place_ref[...]), arrived[...], 1, 0).astype(BF16)
+    beyond = jnp.clip(total - edge, 0.0, 255.0)
+    rows_ref[window:, :] = jnp.broadcast_to(beyond, (TAIL, arrived.shape[1])).astype(BF16)
 
 
 def spread(place, values, slots_ref):
@@ -229,6 +235,10 @@
 def names_of(rows, *fields):
     names = []
     for field in fields:
+        if field == "g":
+            names.append("gE_own" if rows in ("E", "OW") else "gE_far")
+            names += ["gS_own", "gS_far"] if rows in ("OW", "FW") else []
+            continue
         if field in FIELDS:
             own, far, shared = FIELDS[field]
         else:
@@ -240,6 +250,9 @@
 
 
 def values_of(rows, field, edge, refs):
+    if field == "g":
+        first = up(refs["gE_own" if rows in ("E", "OW") else "gE_far"])
+        return first if rows in ("E", "F") else jnp.concatenate([first, up(refs["gS_own"]) + up(refs["gS_far"])], 0)
     if field in FIELDS:
         own, far, shared = FIELDS[field]
     else:
@@ -250,7 +263,8 @@
     if shared:
         inner = refs[shared][edge:, :].astype(F32)
     else:
-        inner = refs[own][edge:, :].astype(F32) + refs[far][edge:, :].astype(F32)
+        inner = slice(edge, refs[own].shape[0] - TAIL)
+        inner = refs[own][inner, :].astype(F32) + refs[far][inner, :].astype(F32)
     return jnp.concatenate([first[0:edge, :].astype(F32), inner], 0)
 
 
@@ -408,7 +422,7 @@
         functools.partial(backward_kernel, layer, rows, edge, names),
         outs,
         [*operands, vectors, slope, *weights],
-        flops=(LAST_COST if layer == 0 and rows == "E" else 4) * count * d * f,
+        flops=COSTS.get((layer, rows), 4) * count * d * f,
         in_specs=[VMEM] * (len(operands) + 1) + [HBM] * 5,
         out_specs=[HBM] * 2 + [VMEM] * (len(outs) - 2),
         scratch=[
@@ -427,16 +441,17 @@
 
 def result_kernel(senders, edge, names, *refs):
     named = dict(zip(names, refs))
-    place, count, count_far, vectors, slots_ref, logit_ref = refs[len(names) :]
+    place, count, vectors, slots_ref, logit_ref = refs[len(names) :]
     gate = gate_of(values_of("OW", "x", edge, named), row(vectors, CENTROID))
     hidden = hidden1_of("OW", edge, named, vectors)
     hidden = hidden + up(named["u"]) + jnp.concatenate([up(named["vE"]), up(named["vS"])], 0) + row(vectors, B_OUT + 1)
-    d_gate = jnp.sum(up(named["g_own"]) * hidden, -1, keepdims=True)
+    own_g = jnp.concatenate([up(named["gE_own"]), up(named["gS_own"])], 0)
+    d_gate = jnp.sum(own_g * hidden, -1, keepdims=True)
     d_logit = (d_gate * gate * (1.0 - gate)).astype(BF16).astype(F32)
     logit_ref[...] = jnp.broadcast_to(d_logit, logit_ref.shape)
     spread(place, (gate * hidden).astype(BF16), slots_ref)
     window = logit_ref.shape[0]
-    inner = jnp.maximum(count[...] - edge, 0.0) + jnp.maximum(count_far[...] - edge, 0.0)
+    inner = sum(up(named[k])[window : window + 1, 0:128] for k in ("x_own", "x_far"))
     over = jnp.where((count[...] > window) | (inner > window - edge), 1.0, 0.0).astype(BF16)
     slots = slots_ref.shape[0] // senders
     for k in range(senders):
@@ -586,27 +601,34 @@
     position = lax.axis_index("rep").astype(jnp.int32).reshape(1)
     x_own, place, count = run(
         functools.partial(place_kernel, senders, edge),
-        [shaped(window, d), shaped(1, worst, dtype=jnp.int32), shaped(1, 128, dtype=F32)],
+        [shaped(window + TAIL, d), shaped(1, worst, dtype=jnp.int32), shaped(1, 128, dtype=F32)],
         [position, arrived],
         in_specs=[SMEM, VMEM],
         flops=one_hot_flops,
         name="place",
+        after=(outgoing_g,),
     )
     have = {"x_own": x_own, "x_far": swap(x_own, 2)}
-    count_far = swap(count, 2)
     g_arrived = exchange(outgoing_g)
 
     *keep_e0, have["pE"] = forward(0, "E", sizes, have, vectors, biases, weights)
     have["qF"] = swap(have["pE"], 2)
     *keep_fw0, have["pFW"] = forward(0, "FW", sizes, have, vectors, biases, weights, (have["pE"],))
     have["qOW"] = swap(have["pFW"], 2)
-    g_own = run(compact_kernel, [shaped(window, d)], [place, g_arrived], flops=one_hot_flops)[0]
-    have["g_own"], have["g_far"] = g_own, swap(g_own, 2)
 
     *keep_f1, far1 = forward(1, "F", sizes, have, vectors, biases, weights)
     have["vE"] = swap(far1, 2)
     *keep_ow1, have["u"], shared1 = forward(1, "OW", sizes, have, vectors, biases, weights, send=True)
     have["vS"] = swap(shared1, 2)
+    have["gE_own"], have["gS_own"] = run(
+        compact_kernel,
+        [shaped(edge, d), shaped(sizes[1], d)],
+        [place, g_arrived],
+        flops=one_hot_flops,
+        after=(shared1,),
+    )
+    have["gS_far"] = swap(have["gS_own"], 2)
+    have["gE_far"] = swap(have["gE_own"], 2)
     branch_ow1, low_ow1, have["dOW"], columns_ow1, bias_ow1 = backward(
         1, "OW", sizes, have, vectors, keep_ow1[2], weights
     )
@@ -616,14 +638,13 @@
     )
     have["hE"] = swap(have["dF"], 2)
 
-    names = list(dict.fromkeys([*names_of("OW", "x", "p", "q"), "u", "vE", "vS", "g_own"]))
+    names = list(dict.fromkeys([*names_of("OW", "x", "p", "q"), "u", "vE", "vS", "gE_own", "gS_own"]))
     result, logit = run(
         functools.partial(result_kernel, senders, edge, names),
         [shaped(worst, d), shaped(window, 128, dtype=F32)],
-        [*(have[k] for k in names), place, count, count_far, vectors],
+        [*(have[k] for k in names), place, count, vectors],
         flops=one_hot_flops,
         name="result",
-        after=(bias_ow1,),
         **room(window, 20),
     )
     returned = exchange(result)

time: 348 us -> 339 us (0.974)
  waiting for transfers between devices: 105 us -> 95.6 us
  Pallas kernels: 163 us -> 154 us
  local copies, waits for them, and re-layouts: 19.5 us -> 27.3 us
    ppermute x21, waiting for transfers between devices: 82.2 us -> 72.5 us  [swap(): lax.ppermute(value, 'rep', [(r, r ^ mask) for r in range(lax.axis_size('r...]
    pallas_call x24, Pallas kernels: 163 us -> 154 us  [run(): pl.pallas_call(body, out_shape=outs, in_specs=[*specs, *[ANY] * extra], o...]
    unnamed x116 -> x100, local copies, waits for them, and re-layouts: 18.8 us -> 26.5 us
  transfers between devices with their start and end apart: 25 -> 25, of which waited for: 13 -> 14; matrix products, arithmetic and copies ran while one was open for 0% -> 0% of each run, Pallas kernels for 44% -> 44%
where the time goes in v2:
time: 339 us; the launch traced here: 334 us
  Pallas kernels  154 us (45%)
  waiting for transfers between devices  95.6 us (28%)
  starting transfers between devices  40.4 us (12%)
  local copies, waits for them, and re-layouts  27.3 us (8%)
  blocking collectives  12.7 us (4%)
    pallas_call x24, Pallas kernels, run(): pl.pallas_call(body, out_shape=outs, in_specs=[*specs, *[ANY] * extra], o...  154 us
    ppermute x21, waiting for transfers between devices, swap(): lax.ppermute(value, 'rep', [(r, r ^ mask) for r in range(lax.axis_size('r...  72.5 us
    unnamed x100, local copies, waits for them, and re-layouts  26.5 us
    all_to_all x1, waiting for transfers between devices, shards(): lax.all_to_all(outgoing, 'ex', split_axis=0, concat_axis=0, tiled=True)  23.1 us
    ppermute x21, starting transfers between devices, swap(): lax.ppermute(value, 'rep', [(r, r ^ mask) for r in range(lax.axis_size('r...  18.1 us
    all_gather x1, blocking collectives, shards(): vectors = lax.all_gather(own_vectors, 'rep', axis=1, tiled=True).astype(F32)  12.7 us
    all_to_all x1, starting transfers between devices, shards(): lax.all_to_all(outgoing, 'ex', split_axis=0, concat_axis=0, tiled=True)  7.4 us
  transfers between devices with their start and end apart: 25, of which 14 were waited for; matrix products, arithmetic and copies ran while one was open for 0% of the time, Pallas kernels for 44%

profile of v2, /device:TPU:0, one launch (start us, length us, event | category | flops | bytes accessed | tf_op | source)
XLA Modules:
  0.0 334.4 jit_solution(8269309368853198950)
XLA Ops:
  2.0 4.3 %route.1 = (s32[1,640]{1,0:T(1,128)S(1)}, bf16[832,1024]{1,0:T(8,128)(2,1)}) custom-call(s32[10]{0:T(128)S(1)} %copy-done.41, s32[1]{0:T(128)} %bitcast.8.refs_1_, s32[1,640]{1,0:T(1,128)S(1)} %bitcast.44, bf16[640,1024]{1,0:T(8,128)(2,1)} %refs_2_.2), custom_call_target="tpu_custom_call" | custom-call | flops 68157440 | bytes 188738 | tf_op jit(solution)/shard_map/route/pallas_call | solution.py:58
  6.3 7.4 %all-to-all-start.3 = ((bf16[8,104,1024]{2,1,0:T(8,128)(2,1)}), bf16[8,104,1024]{2,1,0:T(8,128)(2,1)S(1)}, u32[]{:S(2)}, u32[]{:S(2)}) async-start(bf16[8,104,1024]{2,1,0:T(8,128)(2,1)} %bitcast.10), calls=%async_computation.3 | async-start | bytes 3407872 | tf_op jit(solution)/shard_map/all_to_all | solution.py:737
  14.9 12.7 %all_gather.3 = bf16[8,1024]{1,0:T(8,128)(2,1)S(1)} all-gather(bf16[8,256]{1,0:T(8,128)(2,1)S(1)} %concatenate.3), channel_id=1, replica_groups=mesh['ex'=8,'rep'=4] {'rep'}, dimensions={1}, use_global_device_ids=true | all-gather | bytes 20480 | tf_op jit(solution)/shard_map/all_gather | solution.py:742
  27.7 2.7 pack_kernel.1.refs_2_
  30.4 23.1 %all-to-all-done.3 = bf16[8,104,1024]{2,1,0:T(8,128)(2,1)S(1)} async-done(((bf16[8,104,1024]{2,1,0:T(8,128)(2,1)}), bf16[8,104,1024]{2,1,0:T(8,128)(2,1)S(1)}, u32[]{:S(2)}, u32[]{:S(2)}) %all-to-all-start.3) | async-done | bytes 1703968 | tf_op jit(solution)/shard_map/all_to_all | solution.py:737
  54.7 3.1 place.3
  57.8 1.6 collective-permute-start.18
  59.4 4.7 %all-to-all-start.4 = ((bf16[8,104,1024]{2,1,0:T(8,128)(2,1)}), bf16[8,104,1024]{2,1,0:T(8,128)(2,1)}, u32[]{:S(2)}, u32[]{:S(2)}) async-start(bf16[8,104,1024]{2,1,0:T(8,128)(2,1)} %bitcast.66), calls=%async_computation.4 | async-start | bytes 3407872 | tf_op jit(solution)/shard_map/all_to_all | solution.py:612
  65.3 8.6 %forward_sublayer0_E.3 = (bf16[448,1024]{1,0:T(8,128)(2,1)}, bf16[448,2048]{1,0:T(8,128)(2,1)}, bf16[448,2048]{1,0:T(8,128)(2,1)}, bf16[448,1024]{1,0:T(8,128)(2,1)S(1)}) custom-call(bf16[656,1024]{1,0:T(8,128)(2,1)S(1)} %get-tuple-element.222.refs_0_.refs_1_, ...), custom_call_target="tpu_custom_call" | custom-call | flops 234881024 | bytes 1479168 | tf_op jit(solution)/shard_map/forward_sublayer0_E/pallas_call | solution.py:58
  74.5 15.8 %collective-permute-done.18.refs_0_.refs_1_ = bf16[656,1024]{1,0:T(8,128)(2,1)S(1)} collective-permute-done((bf16[656,1024]{1,0:T(8,128)(2,1)S(1)}, bf16[656,1024]{1,0:T(8,128)(2,1)S(1)}, u32[]{:S(2)}, u32[]{:S(2)}) %collective-permute-start.18) | collective-permute-done | bytes 1343520 | tf_op jit(solution)/shard_map/ppermute | solution.py:25
  90.3 11.2 %forward_sublayer0_FW.3 = (bf16[640,1024]{1,0:T(8,128)(2,1)}, bf16[640,2048]{1,0:T(8,128)(2,1)}, bf16[640,2048]{1,0:T(8,128)(2,1)}, bf16[640,1024]{1,0:T(8,128)(2,1)S(1)}) custom-call(bf16[656,1024]{1,0:T(8,128)(2,1)S(1)} %collective-permute-done.18.refs_0_.refs_1_, bf16[656,1024]{1,0:T(8,128)(2,1)S(1)} %get-tuple-element.222.refs_0_.refs_1_, ...), custom_call_target="tpu_custom_call" | custom-call | flops 335544320 | bytes 1710592 | tf_op jit(solution)/shard_map/forward_sublayer0_FW/pallas_call | solution.py:58
  101.5 1.6 collective-permute-start.22
  103.1 6.9 %collective-permute-done.25.refs_2_.refs_3_.refs_6_ = bf16[448,1024]{1,0:T(8,128)(2,1)S(1)} collective-permute-done((bf16[448,1024]{1,0:T(8,128)(2,1)S(1)}, bf16[448,1024]{1,0:T(8,128)(2,1)S(1)}, u32[]{:S(2)}, u32[]{:S(2)}) %collective-permute-start.25) | collective-permute-done | bytes 917536 | tf_op jit(solution)/shard_map/ppermute | solution.py:25
  109.9 9.8 %forward_sublayer1_F.3 = (bf16[448,1024]{1,0:T(8,128)(2,1)}, bf16[448,2048]{1,0:T(8,128)(2,1)}, bf16[448,2048]{1,0:T(8,128)(2,1)}, bf16[448,1024]{1,0:T(8,128)(2,1)}) custom-call(bf16[656,1024]{1,0:T(8,128)(2,1)S(1)} %collective-permute-done.18.refs_0_.refs_1_, bf16[640,1024]{1,0:T(8,128)(2,1)S(1)} %get-tuple-element.225.refs_3_.refs_6_.refs_1_.refs_2_.refs_5_, ...), custom_call_target="tpu_custom_call" | custom-call | flops 234881024 | bytes 1618432 | tf_op jit(solution)/shard_map/forward_sublayer1_F/pallas_call | solution.py:58
  119.8 1.6 collective-permute-start.29
  121.3 16.7 %collective-permute-done.22.refs_4_.refs_7_.refs_3_ = bf16[640,1024]{1,0:T(8,128)(2,1)S(1)} collective-permute-done((bf16[640,1024]{1,0:T(8,128)(2,1)S(1)}, bf16[640,1024]{1,0:T(8,128)(2,1)S(1)}, u32[]{:S(2)}, u32[]{:S(2)}) %collective-permute-start.22) | collective-permute-done | bytes 1310752 | tf_op jit(solution)/shard_map/ppermute | solution.py:25
  138.0 12.6 %forward_sublayer1_OW.3 = (bf16[640,1024]{1,0:T(8,128)(2,1)}, bf16[640,2048]{1,0:T(8,128)(2,1)}, bf16[640,2048]{1,0:T(8,128)(2,1)}, bf16[640,1024]{1,0:T(8,128)(2,1)S(1)}, bf16[192,1024]{1,0:T(8,128)(2,1)}) custom-call(bf16[656,1024]{1,0:T(8,128)(2,1)S(1)} %get-tuple-element.222.refs_0_.refs_1_, ...), custom_call_target="tpu_custom_call" | custom-call | flops 335544320 | bytes 1956352 | tf_op jit(solution)/shard_map/forward_sublayer1_OW/pallas_call | solution.py:58
  151.7 1.5 collective-permute-start.30
  153.2 3.1 compact_kernel.3
  157.8 8.4 %collective-permute-done.30.refs_7_ = bf16[192,1024]{1,0:T(8,128)(2,1)} collective-permute-done((bf16[192,1024]{1,0:T(8,128)(2,1)}, bf16[192,1024]{1,0:T(8,128)(2,1)}, u32[]{:S(2)}, u32[]{:S(2)}) %collective-permute-start.30) | collective-permute-done | bytes 393248 | tf_op jit(solution)/shard_map/ppermute | solution.py:25
  170.0 4.2 %result.3 = (bf16[832,1024]{1,0:T(8,128)(2,1)S(1)}, f32[640,128]{1,0:T(8,128)S(1)}) custom-call(bf16[656,1024]{1,0:T(8,128)(2,1)S(1)} %get-tuple-element.222.refs_0_.refs_1_, bf16[656,1024]{1,0:T(8,128)(2,1)S(1)} %collective-permute-done.18.refs_0_.refs_1_, bf16[448,1024]{1,0:T(8,128)(2,1)S(1)} %copy-done.10, bf16[640,1024]{1,0:T(8,128)(2,1)S(1)} %copy-done.2, ...), custom_call_target="tpu_custom_call" | custom-call | flops 68157440 | bytes 764144 | tf_op jit(solution)/shard_map/result/pallas_call | solution.py:58
  176.2 4.5 %all-to-all-start.5 = ((bf16[8,104,1024]{2,1,0:T(8,128)(2,1)}), bf16[8,104,1024]{2,1,0:T(8,128)(2,1)}, u32[]{:S(2)}, u32[]{:S(2)}) async-start(bf16[8,104,1024]{2,1,0:T(8,128)(2,1)} %bitcast.37), calls=%async_computation.5 | async-start | bytes 3407872 | tf_op jit(solution)/shard_map/all_to_all | solution.py:650
  180.7 1.6 collective-permute-start.24
  187.3 10.4 %backward_sublayer1_OW.3 = (bf16[640,1024]{1,0:T(8,128)(2,1)}, bf16[640,2048]{1,0:T(8,128)(2,1)}, bf16[640,1024]{1,0:T(8,128)(2,1)S(1)}, f32[3,1024]{1,0:T(4,128)S(1)}, f32[1,2048]{1,0:T(1,128)S(1)}) custom-call(bf16[656,1024]{1,0:T(8,128)(2,1)S(1)} %get-tuple-element.222.refs_0_.refs_1_, bf16[656,1024]{1,0:T(8,128)(2,1)S(1)} %collective-permute-done.18.refs_0_.refs_1_, ...), custom_call_target="tpu_custom_call" | custom-call | flops 335544320 | bytes 2039040 | tf_op jit(solution)/shard_map/backward_sublayer1_OW/pallas_call | solution.py:58
  198.8 4.2 %collective-permute-done.24.refs_1_.refs_2_ = bf16[448,1024]{1,0:T(8,128)(2,1)S(1)} collective-permute-done((bf16[448,1024]{1,0:T(8,128)(2,1)}, bf16[448,1024]{1,0:T(8,128)(2,1)S(1)}, u32[]{:S(2)}, u32[]{:S(2)}) %collective-permute-start.24) | collective-permute-done | bytes 917536 | tf_op jit(solution)/shard_map/ppermute | solution.py:25
  203.0 8.6 %backward_sublayer1_F.3 = (bf16[448,1024]{1,0:T(8,128)(2,1)}, bf16[448,2048]{1,0:T(8,128)(2,1)}, bf16[448,1024]{1,0:T(8,128)(2,1)S(1)}, f32[3,1024]{1,0:T(4,128)S(1)}, f32[1,2048]{1,0:T(1,128)S(1)}) custom-call(bf16[656,1024]{1,0:T(8,128)(2,1)S(1)} %collective-permute-done.18.refs_0_.refs_1_, bf16[448,1024]{1,0:T(8,128)(2,1)S(1)} %collective-permute-done.24.refs_1_.refs_2_, ...), custom_call_target="tpu_custom_call" | custom-call | flops 2818572288 | bytes 1676544 | tf_op jit(solution)/shard_map/backward_sublayer1_F/pallas_call | solution.py:58
  211.6 2.4 collective-permute-start.26
  214.1 8.5 %sibling_kernel.6 = (bf16[1024,1024]{1,0:T(8,128)(2,1)S(1)}, bf16[1024,1024]{1,0:T(8,128)(2,1)S(1)}, f32[1,1024]{1,0:T(1,128)S(1)}) custom-call(bf16[640,1024]{1,0:T(8,128)(2,1)} %get-tuple-element.237.refs_0_, bf16[448,1024]{1,0:T(8,128)(2,1)} %get-tuple-element.238.refs_1_, bf16[640,2048]{1,0:T(8,128)(2,1)} %get-tuple-element.239.refs_2_, ...), custom_call_target="tpu_custom_call" | custom-call | flops 285212672 | bytes 1099008 | tf_op jit(solution)/shard_map/sibling_kernel/pallas_call | solution.py:58
  225.2 5.9 %collective-permute-done.27.refs_10_ = bf16[640,1024]{1,0:T(8,128)(2,1)S(1)} collective-permute-done((bf16[640,1024]{1,0:T(8,128)(2,1)S(1)}, bf16[640,1024]{1,0:T(8,128)(2,1)S(1)}, u32[]{:S(2)}, u32[]{:S(2)}) %collective-permute-start.27) | collective-permute-done | bytes 1310752 | tf_op jit(solution)/shard_map/ppermute | solution.py:25
  231.0 12.8 %backward_sublayer0_FW.3 = (bf16[640,1024]{1,0:T(8,128)(2,1)}, bf16[640,2048]{1,0:T(8,128)(2,1)}, bf16[640,1024]{1,0:T(8,128)(2,1)S(1)}, f32[3,1024]{1,0:T(4,128...) custom-call(bf16[656,1024]{1,0:T(8,128)(2,1)S(1)} %collective-permute-done.18.refs_0_.refs_1_, ...), custom_call_target="tpu_custom_call" | custom-call | flops 335544320 | bytes 2309376 | tf_op jit(solution)/shard_map/backward_sublayer0_FW/pallas_call | solution.py:58
  244.5 2.4 collective-permute-start.28
  246.9 3.8 %collective-permute-done.26.refs_5_ = bf16[448,1024]{1,0:T(8,128)(2,1)S(1)} collective-permute-done((bf16[448,1024]{1,0:T(8,128)(2,1)S(1)}, bf16[448,1024]{1,0:T(8,128)(2,1)S(1)}, u32[]{:S(2)}, u32[]{:S(2)}) %collective-permute-start.26) | collective-permute-done | bytes 917536 | tf_op jit(solution)/shard_map/ppermute | solution.py:25
  250.7 9.7 %backward_sublayer0_E.3 = (bf16[448,1024]{1,0:T(8,128)(2,1)}, bf16[448,2048]{1,0:T(8,128)(2,1)}, bf16[448,1024]{1,0:T(8,128)(2,1)S(1)}, f32[3,1024]{1,0:T(4,128)...) custom-call(bf16[656,1024]{1,0:T(8,128)(2,1)S(1)} %get-tuple-element.222.refs_0_.refs_1_, ...), custom_call_target="tpu_custom_call" | custom-call | flops 7516192768 | bytes 1930496 | tf_op jit(solution)/shard_map/backward_sublayer0_E/pallas_call | solution.py:58
  260.4 8.6 %sibling_kernel.7 = (bf16[1024,1024]{1,0:T(8,128)(2,1)S(1)}, bf16[1024,1024]{1,0:T(8,128)(2,1)S(1)}, f32[1,1024]{1,0:T(1,128)S(1)}) custom-call(bf16[448,1024]{1,0:T(8,128)(2,1)} %get-tuple-element.254.refs_0_, bf16[640,1024]{1,0:T(8,128)(2,1)} %get-tuple-element.255.refs_1_, bf16[448,2048]{1,0:T(8,128)(2,1)} %get-tuple-element.256.refs_2_, ...), custom_call_target="tpu_custom_call" | custom-call | flops 285212672 | bytes 1099008 | tf_op jit(solution)/shard_map/sibling_kernel/pallas_call | solution.py:58
  270.3 1.4 copy-done.45
  271.7 4.5 %collective-permute-done.28.refs_7_ = bf16[640,1024]{1,0:T(8,128)(2,1)S(1)} collective-permute-done((bf16[640,1024]{1,0:T(8,128)(2,1)S(1)}, bf16[640,1024]{1,0:T(8,128)(2,1)S(1)}, u32[]{:S(2)}, u32[]{:S(2)}) %collective-permute-start.28) | collective-permute-done | bytes 1310752 | tf_op jit(solution)/shard_map/ppermute | solution.py:25
  276.2 3.5 %row_grad.3 = (bf16[832,1024]{1,0:T(8,128)(2,1)S(1)}, f32[1,1024]{1,0:T(1,128)S(1)}) custom-call(bf16[656,1024]{1,0:T(8,128)(2,1)S(1)} %get-tuple-element.222.refs_0_.refs_1_, bf16[656,1024]{1,0:T(8,128)(2,1)S(1)} %collective-permute-done.18.refs_0_.refs_1_, bf16[448,1024]{1,0:T(8,128)(2,1)S(1)} %get-tuple-element.235.refs_2_, ...), custom_call_target="tpu_custom_call" | custom-call | flops 68157440 | bytes 682448 | tf_op jit(solution)/shard_map/row_grad/pallas_call | solution.py:58
  281.0 5.7 %all-to-all-start.6 = ((bf16[8,104,1024]{2,1,0:T(8,128)(2,1)}), bf16[8,104,1024]{2,1,0:T(8,128)(2,1)S(1)}, u32[]{:S(2)}, u32[]{:S(2)}) async-start(bf16[8,104,1024]{2,1,0:T(8,128)(2,1)} %bitcast.36), calls=%async_computation.6 | async-start | bytes 3407872 | tf_op jit(solution)/shard_map/all_to_all | solution.py:687
  287.9 1.5 marks.3.refs_5_
  289.4 1.6 collective-permute-done.38.refs_12_
  291.5 2.6 collective-permute-done.37.refs_11_
  295.5 11.0 %own_grads_sublayer1.3 = (f32[2,1024,1024]{2,1,0:T(8,128)}, f32[2,1024,1024]{2,1,0:T(8,128)}, f32[1,1024]{1,0:T(1,128)S(1)}) custom-call(bf16[640,1024]{1,0:T(8,128)(2,1)} %get-tuple-element.237.refs_0_, bf16[448,1024]{1,0:T(8,128)(2,1)} %get-tuple-element.238.refs_1_, bf16[640,2048]{1,0:T(8,128)(2,1)} %get-tuple-element.239.refs_2_, ...), custom_call_target="tpu_custom_call" | custom-call | flops 285212672 | bytes 2147840 | tf_op jit(solution)/shard_map/own_grads_sublayer1/pallas_call | solution.py:58
  306.5 1.5 collective-permute-start.32
  308.1 4.7 %unpack_kernel.6 = bf16[640,1024]{1,0:T(8,128)(2,1)} custom-call(s32[1,640]{1,0:T(1,128)S(1)} %copy-done.69, bf16[832,1024]{1,0:T(8,128)(2,1)} %bitcast.21.refs_0_.refs_1_, bf16[640,1024]{1,0:T(8,128)(2,1)S(1)} %copy-done.53), custom_call_target="tpu_custom_call" | custom-call | flops 68157440 | bytes 270496 | tf_op jit(solution)/shard_map/unpack_kernel/pallas_call | solution.py:58
  312.8 1.3 copy-done.59
  314.9 11.3 %own_grads_sublayer0.3 = (f32[2,1024,1024]{2,1,0:T(8,128)}, f32[2,1024,1024]{2,1,0:T(8,128)}, f32[1,1024]{1,0:T(1,128)S(1)}) custom-call(bf16[448,1024]{1,0:T(8,128)(2,1)} %get-tuple-element.254.refs_0_, bf16[640,1024]{1,0:T(8,128)(2,1)} %get-tuple-element.255.refs_1_, ...), custom_call_target="tpu_custom_call", output_to_operand_aliasing={{0}: (13, {}), {1}: (14, {})} | custom-call | flops 285212672 | bytes 3196416 | tf_op jit(solution)/shard_map/own_grads_sublayer0/pallas_call | solution.py:58
  326.8 3.6 %unpack_kernel.7 = bf16[640,1024]{1,0:T(8,128)(2,1)S(1)} custom-call(s32[1,640]{1,0:T(1,128)S(1)} %copy-done.69, bf16[832,1024]{1,0:T(8,128)(2,1)S(1)} %bitcast.35, bf16[640,1024]{1,0:T(8,128)(2,1)} %refs_2_.3), custom_call_target="tpu_custom_call" | custom-call | flops 68157440 | bytes 270496 | tf_op jit(solution)/shard_map/unpack_kernel/pallas_call | solution.py:58
  330.5 2.4 conditional.1
  (131 shorter events, 31.3 us)
Async XLA Ops:
  6.3 21.4 %copy-start.68 = (s32[1,640]{1,0:T(1,128)}, s32[1,640]{1,0:T(1,128)S(1)}, u32[]{:S(2)}) copy-start(s32[1,640]{1,0:T(1,128)S(1)} %get-tuple-element.221.refs_0_) | copy-start | bytes 7684
  6.3 8.6 %copy-start.75 = (bf16[1,256]{1,0:T(2,128)(2,1)S(1)}, bf16[1,256]{1,0:T(2,128)(2,1)}, u32[]{:S(2)}) copy-start(bf16[1,256]{1,0:T(2,128)(2,1)} %param.16) | copy-start | bytes 1540
  6.3 8.6 %copy-start.76 = (bf16[1,2,256]{2,1,0:T(2,128)(2,1)S(1)}, bf16[1,2,256]{2,1,0:T(2,128)(2,1)}, u32[]{:S(2)}) copy-start(bf16[1,2,256]{2,1,0:T(2,128)(2,1)} %param.17) | copy-start | bytes 3076
  6.3 8.6 %copy-start.77 = (bf16[1,2,256]{2,1,0:T(2,128)(2,1)S(1)}, bf16[1,2,256]{2,1,0:T(2,128)(2,1)}, u32[]{:S(2)}) copy-start(bf16[1,2,256]{2,1,0:T(2,128)(2,1)} %param.18) | copy-start | bytes 3076
  6.3 8.6 %copy-start.78 = (bf16[1,2,256]{2,1,0:T(2,128)(2,1)S(1)}, bf16[1,2,256]{2,1,0:T(2,128)(2,1)}, u32[]{:S(2)}) copy-start(bf16[1,2,256]{2,1,0:T(2,128)(2,1)} %param.22) | copy-start | bytes 3076
  6.3 21.4 %copy-start.55 = (bf16[640,1024]{1,0:T(8,128)(2,1)S(1)}, bf16[640,1024]{1,0:T(8,128)(2,1)}, u32[]{:S(2)}) copy-start(bf16[640,1024]{1,0:T(8,128)(2,1)} %refs_2_.3) | copy-start | bytes 3932164
  6.3 47.2 %all-to-all-start.3 = ((bf16[8,104,1024]{2,1,0:T(8,128)(2,1)}), bf16[8,104,1024]{2,1,0:T(8,128)(2,1)S(1)}, u32[]{:S(2)}, u32[]{:S(2)}) async-start(bf16[8,104,1024]{2,1,0:T(8,128)(2,1)} %bitcast.10), calls=%async_computation.3 | async-start | bytes 3407872 | tf_op jit(solution)/shard_map/all_to_all | solution.py:737
  13.7 51.6 %collective-permute-start.20 = (bf16[2,1024,1024]{2,1,0:T(8,128)(2,1)}, bf16[2,1024,1024]{2,1,0:T(8,128)(2,1)}, u32[]{:S(2)}, u32[]{:S(2)}) collective-permute-start(bf16[2,1024,1024]{2,1,0:T(8,128)(2,1)} %bitcast.46), channel_id=1, source_target_pairs={{0,1},{1,0},{2,3},{3,2},{4,5},{5,4},{6,7},{7,6},{8,9},{9,8},{10,11... | collective-permute-start | bytes 12582920 | tf_op jit(solution)/shard_map/ppermute | solution.py:25
  13.7 51.6 %collective-permute-start.21 = (bf16[2,1024,1024]{2,1,0:T(8,128)(2,1)}, bf16[2,1024,1024]{2,1,0:T(8,128)(2,1)}, u32[]{:S(2)}, u32[]{:S(2)}) collective-permute-start(bf16[2,1024,1024]{2,1,0:T(8,128)(2,1)} %bitcast.56), channel_id=1, source_target_pairs={{0,1},{1,0},{2,3},{3,2},{4,5},{5,4},{6,7},{7,6},{8,9},{9,8},{10,11... | collective-permute-start | bytes 12582920 | tf_op jit(solution)/shard_map/ppermute | solution.py:25
  57.8 32.5 %collective-permute-start.18 = (bf16[656,1024]{1,0:T(8,128)(2,1)S(1)}, bf16[656,1024]{1,0:T(8,128)(2,1)S(1)}, u32[]{:S(2)}, u32[]{:S(2)}) collective-permute-start(bf16[656,1024]{1,0:T(8,128)(2,1)S(1)} %get-tuple-element.222.refs_0_.refs_1_), channel_id=1, source_target_pairs={{0,2},{1,3},{2,0},{3,1},{4,6},{5,7},{6,4},{7,5},{8,10},{9,11},{10,... | collective-permute-start | bytes 4030472 | tf_op jit(solution)/shard_map/ppermute | solution.py:25
  59.4 4.7 %copy-start.24 = (bf16[1,2,1024]{2,1,0:T(2,128)(2,1)S(1)}, bf16[1,2,1024]{2,1,0:T(2,128)(2,1)}, u32[]{:S(2)}) copy-start(bf16[1,2,1024]{2,1,0:T(2,128)(2,1)} %param.20) | copy-start | bytes 12292
  59.4 93.8 %all-to-all-start.4 = ((bf16[8,104,1024]{2,1,0:T(8,128)(2,1)}), bf16[8,104,1024]{2,1,0:T(8,128)(2,1)}, u32[]{:S(2)}, u32[]{:S(2)}) async-start(bf16[8,104,1024]{2,1,0:T(8,128)(2,1)} %bitcast.66), calls=%async_computation.4 | async-start | bytes 3407872 | tf_op jit(solution)/shard_map/all_to_all | solution.py:612
  64.1 1.2 collective-permute-start.19
  73.9 64.1 %copy-start.9 = (bf16[448,1024]{1,0:T(8,128)(2,1)}, bf16[448,1024]{1,0:T(8,128)(2,1)S(1)}, u32[]{:S(2)}) copy-start(bf16[448,1024]{1,0:T(8,128)(2,1)S(1)} %get-tuple-element.224.refs_9_.refs_2_.refs_5_) | copy-start | bytes 2752516
  73.9 36.0 %collective-permute-start.25 = (bf16[448,1024]{1,0:T(8,128)(2,1)S(1)}, bf16[448,1024]{1,0:T(8,128)(2,1)S(1)}, u32[]{:S(2)}, u32[]{:S(2)}) collective-permute-start(bf16[448,1024]{1,0:T(8,128)(2,1)S(1)} %get-tuple-element.224.refs_9_.refs_2_.refs_5_), channel_id=1, source_target_pairs={{0,2},{1,3},{2,0},{3,1},{4,6},{5,7},{6,4},{7,5},{8,10},{9,11},{10,... | collective-permute-start | bytes 2752520 | tf_op jit(solution)/shard_map/ppermute | solution.py:25
  101.5 36.5 %copy-start.1 = (bf16[640,1024]{1,0:T(8,128)(2,1)}, bf16[640,1024]{1,0:T(8,128)(2,1)S(1)}, u32[]{:S(2)}) copy-start(bf16[640,1024]{1,0:T(8,128)(2,1)S(1)} %get-tuple-element.225.refs_3_.refs_6_.refs_1_.refs_2_.refs_5_) | copy-start | bytes 3932164
  101.5 36.5 %collective-permute-start.22 = (bf16[640,1024]{1,0:T(8,128)(2,1)S(1)}, bf16[640,1024]{1,0:T(8,128)(2,1)S(1)}, u32[]{:S(2)}, u32[]{:S(2)}) collective-permute-start(bf16[640,1024]{1,0:T(8,128)(2,1)S(1)} %get-tuple-element.225.refs_3_.refs_6_.refs_1_.refs_2_.refs_5_), channel_id=1, source_target_pairs={{0,2},{1,3},{2,0},{3,1},{4,6},{5,7},{6,4},{7,5},{8,10},{9,11},{10,... | collective-permute-start | bytes 3932168 | tf_op jit(solution)/shard_map/ppermute | solution.py:25
  109.9 9.8 %copy-start.12 = (bf16[448,1024]{1,0:T(8,128)(2,1)}, bf16[448,1024]{1,0:T(8,128)(2,1)S(1)}, u32[]{:S(2)}) copy-start(bf16[448,1024]{1,0:T(8,128)(2,1)S(1)} %collective-permute-done.25.refs_2_.refs_3_.refs_6_) | copy-start | bytes 2752516
  119.8 38.0 %collective-permute-start.29 = (bf16[448,1024]{1,0:T(8,128)(2,1)}, bf16[448,1024]{1,0:T(8,128)(2,1)}, u32[]{:S(2)}, u32[]{:S(2)}) collective-permute-start(bf16[448,1024]{1,0:T(8,128)(2,1)} %get-tuple-element.251), channel_id=1, source_target_pairs={{0,2},{1,3},{2,0},{3,1},{4,6},{5,7},{6,4},{7,5},{8,10},{9,11},{10,... | collective-permute-start | bytes 2752520 | tf_op jit(solution)/shard_map/ppermute | solution.py:25
  138.0 12.6 %copy-start.5 = (bf16[640,1024]{1,0:T(8,128)(2,1)}, bf16[640,1024]{1,0:T(8,128)(2,1)S(1)}, u32[]{:S(2)}) copy-start(bf16[640,1024]{1,0:T(8,128)(2,1)S(1)} %collective-permute-done.22.refs_4_.refs_7_.refs_3_) | copy-start | bytes 3932164
  151.7 14.5 %collective-permute-start.30 = (bf16[192,1024]{1,0:T(8,128)(2,1)}, bf16[192,1024]{1,0:T(8,128)(2,1)}, u32[]{:S(2)}, u32[]{:S(2)}) collective-permute-start(bf16[192,1024]{1,0:T(8,128)(2,1)} %get-tuple-element.226.refs_2_), channel_id=1, source_target_pairs={{0,2},{1,3},{2,0},{3,1},{4,6},{5,7},{6,4},{7,5},{8,10},{9,11},{10,... | collective-permute-start | bytes 1179656 | tf_op jit(solution)/shard_map/ppermute | solution.py:25
  153.2 13.0 %copy-start.2 = (bf16[640,1024]{1,0:T(8,128)(2,1)S(1)}, bf16[640,1024]{1,0:T(8,128)(2,1)}, u32[]{:S(2)}) copy-start(bf16[640,1024]{1,0:T(8,128)(2,1)} %copy-done.1) | copy-start | bytes 3932164
  156.3 17.9 %copy-start.14 = (bf16[448,1024]{1,0:T(8,128)(2,1)}, bf16[448,1024]{1,0:T(8,128)(2,1)S(1)}, u32[]{:S(2)}) copy-start(bf16[448,1024]{1,0:T(8,128)(2,1)S(1)} %get-tuple-element.227.refs_2_.refs_1_.refs_8_) | copy-start | bytes 2752516
  156.3 25.9 %collective-permute-start.23 = (bf16[192,1024]{1,0:T(8,128)(2,1)S(1)}, bf16[192,1024]{1,0:T(8,128)(2,1)S(1)}, u32[]{:S(2)}, u32[]{:S(2)}) collective-permute-start(bf16[192,1024]{1,0:T(8,128)(2,1)S(1)} %get-tuple-element.228.refs_3_.refs_9_), channel_id=1, source_target_pairs={{0,2},{1,3},{2,0},{3,1},{4,6},{5,7},{6,4},{7,5},{8,10},{9,11},{10,... | collective-permute-start | bytes 1179656 | tf_op jit(solution)/shard_map/ppermute | solution.py:25
  176.2 104.8 %all-to-all-start.5 = ((bf16[8,104,1024]{2,1,0:T(8,128)(2,1)}), bf16[8,104,1024]{2,1,0:T(8,128)(2,1)}, u32[]{:S(2)}, u32[]{:S(2)}) async-start(bf16[8,104,1024]{2,1,0:T(8,128)(2,1)} %bitcast.37), calls=%async_computation.5 | async-start | bytes 3407872 | tf_op jit(solution)/shard_map/all_to_all | solution.py:650
  180.7 22.3 %collective-permute-start.24 = (bf16[448,1024]{1,0:T(8,128)(2,1)}, bf16[448,1024]{1,0:T(8,128)(2,1)S(1)}, u32[]{:S(2)}, u32[]{:S(2)}) collective-permute-start(bf16[448,1024]{1,0:T(8,128)(2,1)} %copy-done.14), channel_id=1, source_target_pairs={{0,2},{1,3},{2,0},{3,1},{4,6},{5,7},{6,4},{7,5},{8,10},{9,11},{10,... | collective-permute-start | bytes 2752520 | tf_op jit(solution)/shard_map/ppermute | solution.py:25
  187.3 15.8 %copy-start.4 = (bf16[640,1024]{1,0:T(8,128)(2,1)S(1)}, bf16[640,1024]{1,0:T(8,128)(2,1)}, u32[]{:S(2)}) copy-start(bf16[640,1024]{1,0:T(8,128)(2,1)} %copy-done.1) | copy-start | bytes 3932164
  187.3 15.8 %copy-start.13 = (bf16[448,1024]{1,0:T(8,128)(2,1)S(1)}, bf16[448,1024]{1,0:T(8,128)(2,1)}, u32[]{:S(2)}) copy-start(bf16[448,1024]{1,0:T(8,128)(2,1)} %copy-done.12) | copy-start | bytes 2752516
  198.3 32.8 %collective-permute-start.27 = (bf16[640,1024]{1,0:T(8,128)(2,1)S(1)}, bf16[640,1024]{1,0:T(8,128)(2,1)S(1)}, u32[]{:S(2)}, u32[]{:S(2)}) collective-permute-start(bf16[640,1024]{1,0:T(8,128)(2,1)S(1)} %get-tuple-element.230.refs_4_.refs_9_), channel_id=1, source_target_pairs={{0,2},{1,3},{2,0},{3,1},{4,6},{5,7},{6,4},{7,5},{8,10},{9,11},{10,... | collective-permute-start | bytes 3932168 | tf_op jit(solution)/shard_map/ppermute | solution.py:25
  211.6 39.1 %collective-permute-start.26 = (bf16[448,1024]{1,0:T(8,128)(2,1)S(1)}, bf16[448,1024]{1,0:T(8,128)(2,1)S(1)}, u32[]{:S(2)}, u32[]{:S(2)}) collective-permute-start(bf16[448,1024]{1,0:T(8,128)(2,1)S(1)} %get-tuple-element.233.refs_8_), channel_id=1, source_target_pairs={{0,2},{1,3},{2,0},{3,1},{4,6},{5,7},{6,4},{7,5},{8,10},{9,11},{10,... | collective-permute-start | bytes 2752520 | tf_op jit(solution)/shard_map/ppermute | solution.py:25
  214.1 17.0 %copy-start.8 = (bf16[640,1024]{1,0:T(8,128)(2,1)S(1)}, bf16[640,1024]{1,0:T(8,128)(2,1)}, u32[]{:S(2)}) copy-start(bf16[640,1024]{1,0:T(8,128)(2,1)} %copy-done.5) | copy-start | bytes 3932164
  231.0 19.7 %copy-start.16 = (bf16[448,1024]{1,0:T(8,128)(2,1)S(1)}, bf16[448,1024]{1,0:T(8,128)(2,1)}, u32[]{:S(2)}) copy-start(bf16[448,1024]{1,0:T(8,128)(2,1)} %copy-done.14) | copy-start | bytes 2752516
  244.5 31.7 %collective-permute-start.28 = (bf16[640,1024]{1,0:T(8,128)(2,1)S(1)}, bf16[640,1024]{1,0:T(8,128)(2,1)S(1)}, u32[]{:S(2)}, u32[]{:S(2)}) collective-permute-start(bf16[640,1024]{1,0:T(8,128)(2,1)S(1)} %get-tuple-element.247.refs_3_), channel_id=1, source_target_pairs={{0,2},{1,3},{2,0},{3,1},{4,6},{5,7},{6,4},{7,5},{8,10},{9,11},{10,... | collective-permute-start | bytes 3932168 | tf_op jit(solution)/shard_map/ppermute | solution.py:25
  260.4 15.8 %copy-start.22 = (f32[640,128]{1,0:T(8,128)S(1)}, f32[640,128]{1,0:T(8,128)}, u32[]{:S(2)}) copy-start(f32[640,128]{1,0:T(8,128)} %copy-done.21) | copy-start | bytes 983044
  281.0 45.9 %all-to-all-start.6 = ((bf16[8,104,1024]{2,1,0:T(8,128)(2,1)}), bf16[8,104,1024]{2,1,0:T(8,128)(2,1)S(1)}, u32[]{:S(2)}, u32[]{:S(2)}) async-start(bf16[8,104,1024]{2,1,0:T(8,128)(2,1)} %bitcast.36), calls=%async_computation.6 | async-start | bytes 3407872 | tf_op jit(solution)/shard_map/all_to_all | solution.py:687
  286.7 2.7 copy-start.32
  286.7 4.4 %collective-permute-start.36 = (bf16[1024,1024]{1,0:T(8,128)(2,1)}, bf16[1024,1024]{1,0:T(8,128)(2,1)S(1)}, u32[]{:S(2)}, u32[]{:S(2)}) collective-permute-start(bf16[1024,1024]{1,0:T(8,128)(2,1)} %copy-done.46), channel_id=1, source_target_pairs={{0,1},{1,0},{2,3},{3,2},{4,5},{5,4},{6,7},{7,6},{8,9},{9,8},{10,11... | collective-permute-start | bytes 6291464 | tf_op jit(solution)/shard_map/ppermute | solution.py:25
  286.8 7.4 %collective-permute-start.37 = (bf16[1024,1024]{1,0:T(8,128)(2,1)}, bf16[1024,1024]{1,0:T(8,128)(2,1)S(1)}, u32[]{:S(2)}, u32[]{:S(2)}) collective-permute-start(bf16[1024,1024]{1,0:T(8,128)(2,1)} %copy-done.43), channel_id=1, source_target_pairs={{0,1},{1,0},{2,3},{3,2},{4,5},{5,4},{6,7},{7,6},{8,9},{9,8},{10,11... | collective-permute-start | bytes 6291464 | tf_op jit(solution)/shard_map/ppermute | solution.py:25
  287.3 25.5 %collective-permute-start.33 = (bf16[1024,1024]{1,0:T(8,128)(2,1)}, bf16[1024,1024]{1,0:T(8,128)(2,1)S(1)}, u32[]{:S(2)}, u32[]{:S(2)}) collective-permute-start(bf16[1024,1024]{1,0:T(8,128)(2,1)} %copy-done.45), channel_id=1, source_target_pairs={{0,1},{1,0},{2,3},{3,2},{4,5},{5,4},{6,7},{7,6},{8,9},{9,8},{10,11... | collective-permute-start | bytes 6291464 | tf_op jit(solution)/shard_map/ppermute | solution.py:25
  287.4 25.4 %collective-permute-start.34 = (bf16[1024,1024]{1,0:T(8,128)(2,1)}, bf16[1024,1024]{1,0:T(8,128)(2,1)S(1)}, u32[]{:S(2)}, u32[]{:S(2)}) collective-permute-start(bf16[1024,1024]{1,0:T(8,128)(2,1)} %copy-done.44), channel_id=1, source_target_pairs={{0,1},{1,0},{2,3},{3,2},{4,5},{5,4},{6,7},{7,6},{8,9},{9,8},{10,11... | collective-permute-start | bytes 6291464 | tf_op jit(solution)/shard_map/ppermute | solution.py:25
  287.8 3.1 collective-permute-start.38
  290.9 15.6 %collective-permute-start.31 = (f32[8,1024]{1,0:T(8,128)S(1)}, f32[8,1024]{1,0:T(8,128)S(1)}, u32[]{:S(2)}, u32[]{:S(2)}) collective-permute-start(f32[8,1024]{1,0:T(8,128)S(1)} %columns_kernel.3.refs_0_), channel_id=1, source_target_pairs={{0,1},{1,0},{2,3},{3,2},{4,5},{5,4},{6,7},{7,6},{8,9},{9,8},{10,11... | collective-permute-start | bytes 98312 | tf_op jit(solution)/shard_map/ppermute | solution.py:25
  291.1 17.0 %copy-start.53 = (bf16[640,1024]{1,0:T(8,128)(2,1)S(1)}, bf16[640,1024]{1,0:T(8,128)(2,1)}, u32[]{:S(2)}) copy-start(bf16[640,1024]{1,0:T(8,128)(2,1)} %refs_2_.2) | copy-start | bytes 3932164
  291.1 17.0 %copy-start.69 = (s32[1,640]{1,0:T(1,128)S(1)}, s32[1,640]{1,0:T(1,128)}, u32[]{:S(2)}) copy-start(s32[1,640]{1,0:T(1,128)} %copy-done.68) | copy-start | bytes 7684
  291.1 3.0 copy-start.62
  291.1 21.6 %collective-permute-start.35 = (f32[1,1024]{1,0:T(1,128)S(1)}, f32[1,1024]{1,0:T(1,128)S(1)}, u32[]{:S(2)}, u32[]{:S(2)}) collective-permute-start(f32[1,1024]{1,0:T(1,128)S(1)} %get-tuple-element.264.refs_10_), channel_id=1, source_target_pairs={{0,1},{1,0},{2,3},{3,2},{4,5},{5,4},{6,7},{7,6},{8,9},{9,8},{10,11... | collective-permute-start | bytes 12296 | tf_op jit(solution)/shard_map/ppermute | solution.py:25
  306.5 19.6 %collective-permute-start.32 = (f32[8,1024]{1,0:T(8,128)S(1)}, f32[8,1024]{1,0:T(8,128)S(1)}, u32[]{:S(2)}, u32[]{:S(2)}) collective-permute-start(f32[8,1024]{1,0:T(8,128)S(1)} %add_kernel.3.refs_1_), channel_id=1, source_target_pairs={{0,2},{1,3},{2,0},{3,1},{4,6},{5,7},{6,4},{7,5},{8,10},{9,11},{10,... | collective-permute-start | bytes 98312 | tf_op jit(solution)/shard_map/ppermute | solution.py:25
  326.8 3.6 %copy-start.48 = (bf16[832,1024]{1,0:T(8,128)(2,1)S(1)}, bf16[832,1024]{1,0:T(8,128)(2,1)}, u32[]{:S(2)}) copy-start(bf16[832,1024]{1,0:T(8,128)(2,1)} %pack_kernel.1.refs_2_) | copy-start | bytes 5111812
  (27 other events, 35.7 us)

commit v3 on v2

--- a/solution.py
+++ b/solution.py
@@ -753,7 +753,12 @@
     if EDGE + SHARED >= most:
         return expert_group((most, 16), *operands)[0]
     outs, over = expert_group((EDGE, SHARED), *operands)
-    return lax.cond(over > 0.0, lambda *_: expert_group((most, 16), *operands)[0], lambda *kept: kept, *outs)
+
+    def second_pass(*_):
+        again = lax.all_to_all(outgoing, "ex", split_axis=0, concat_axis=0, tiled=True)
+        return expert_group((most, 16), again, *operands[1:])[0]
+
+    return lax.cond(over > 0.0, second_pass, lambda *kept: kept, *outs)
 
 
 def solution(mesh):

time: 339 us -> 339 us (level)
    unnamed x100 -> x102, local copies, waits for them, and re-layouts: 26.5 us -> 28 us
  transfers between devices with their start and end apart: 25 -> 25, of which waited for: 14 -> 14; matrix products, arithmetic and copies ran while one was open for 0% -> 0% of each run, Pallas kernels for 44% -> 43%
where the time goes in v3:
time: 339 us; the launch traced here: 334 us
  Pallas kernels  153 us (45%)
  waiting for transfers between devices  95.8 us (28%)
  starting transfers between devices  40.6 us (12%)
  local copies, waits for them, and re-layouts  28.7 us (8%)
  blocking collectives  12.8 us (4%)
    pallas_call x24, Pallas kernels, run(): pl.pallas_call(body, out_shape=outs, in_specs=[*specs, *[ANY] * extra], o...  153 us
    ppermute x21, waiting for transfers between devices, swap(): lax.ppermute(value, 'rep', [(r, r ^ mask) for r in range(lax.axis_size('r...  72.6 us
    unnamed x102, local copies, waits for them, and re-layouts  28 us
    all_to_all x1, waiting for transfers between devices, shards(): lax.all_to_all(outgoing, 'ex', split_axis=0, concat_axis=0, tiled=True)  23.1 us
    ppermute x21, starting transfers between devices, swap(): lax.ppermute(value, 'rep', [(r, r ^ mask) for r in range(lax.axis_size('r...  18.2 us
    all_gather x1, blocking collectives, shards(): vectors = lax.all_gather(own_vectors, 'rep', axis=1, tiled=True).astype(F32)  12.8 us
    all_to_all x1, starting transfers between devices, shards(): lax.all_to_all(outgoing, 'ex', split_axis=0, concat_axis=0, tiled=True)  7.4 us
  transfers between devices with their start and end apart: 25, of which 14 were waited for; matrix products, arithmetic and copies ran while one was open for 0% of the time, Pallas kernels for 43%

profile of v3, /device:TPU:0, one launch (start us, length us, event | category | flops | bytes accessed | tf_op | source)
XLA Modules:
  0.0 334.4 jit_solution(7421734426758981332)
XLA Ops:
  2.0 4.3 %route.1 = (s32[1,640]{1,0:T(1,128)S(1)}, bf16[832,1024]{1,0:T(8,128)(2,1)}) custom-call(s32[10]{0:T(128)S(1)} %copy-done.45, s32[1]{0:T(128)} %bitcast.10.refs_1_, s32[1,640]{1,0:T(1,128)S(1)} %bitcast.48, bf16[640,1024]{1,0:T(8,128)(2,1)} %refs_2_.2), custom_call_target="tpu_custom_call" | custom-call | flops 68157440 | bytes 188738 | tf_op jit(solution)/shard_map/route/pallas_call | solution.py:58
  6.3 7.4 %all-to-all-start.4 = ((bf16[8,104,1024]{2,1,0:T(8,128)(2,1)}), bf16[8,104,1024]{2,1,0:T(8,128)(2,1)S(1)}, u32[]{:S(2)}, u32[]{:S(2)}) async-start(bf16[8,104,1024]{2,1,0:T(8,128)(2,1)} %bitcast.74), calls=%async_computation.4 | async-start | bytes 3407872 | tf_op jit(solution)/shard_map/all_to_all | solution.py:737
  15.0 12.8 %all_gather.3 = bf16[8,1024]{1,0:T(8,128)(2,1)S(1)} all-gather(bf16[8,256]{1,0:T(8,128)(2,1)S(1)} %concatenate.3), channel_id=1, replica_groups=mesh['ex'=8,'rep'=4] {'rep'}, dimensions={1}, use_global_device_ids=true | all-gather | bytes 20480 | tf_op jit(solution)/shard_map/all_gather | solution.py:742
  27.7 2.7 pack_kernel.1.refs_2_
  30.4 23.1 %all-to-all-done.4 = bf16[8,104,1024]{2,1,0:T(8,128)(2,1)S(1)} async-done(((bf16[8,104,1024]{2,1,0:T(8,128)(2,1)}), bf16[8,104,1024]{2,1,0:T(8,128)(2,1)S(1)}, u32[]{:S(2)}, u32[]{:S(2)}) %all-to-all-start.4) | async-done | bytes 1703968 | tf_op jit(solution)/shard_map/all_to_all | solution.py:737
  54.7 1.5 copy-done.15
  56.2 1.7 place.3
  57.8 1.6 collective-permute-start.18
  59.4 4.7 %all-to-all-start.5 = ((bf16[8,104,1024]{2,1,0:T(8,128)(2,1)}), bf16[8,104,1024]{2,1,0:T(8,128)(2,1)}, u32[]{:S(2)}, u32[]{:S(2)}) async-start(bf16[8,104,1024]{2,1,0:T(8,128)(2,1)} %bitcast.70), calls=%async_computation.5 | async-start | bytes 3407872 | tf_op jit(solution)/shard_map/all_to_all | solution.py:612
  65.3 8.6 %forward_sublayer0_E.3 = (bf16[448,1024]{1,0:T(8,128)(2,1)}, bf16[448,2048]{1,0:T(8,128)(2,1)}, bf16[448,2048]{1,0:T(8,128)(2,1)}, bf16[448,1024]{1,0:T(8,128)(2,1)S(1)}) custom-call(bf16[656,1024]{1,0:T(8,128)(2,1)S(1)} %get-tuple-element.222.refs_0_.refs_1_, ...), custom_call_target="tpu_custom_call" | custom-call | flops 234881024 | bytes 1479168 | tf_op jit(solution)/shard_map/forward_sublayer0_E/pallas_call | solution.py:58
  74.6 15.8 %collective-permute-done.18.refs_0_.refs_1_ = bf16[656,1024]{1,0:T(8,128)(2,1)S(1)} collective-permute-done((bf16[656,1024]{1,0:T(8,128)(2,1)S(1)}, bf16[656,1024]{1,0:T(8,128)(2,1)S(1)}, u32[]{:S(2)}, u32[]{:S(2)}) %collective-permute-start.18) | collective-permute-done | bytes 1343520 | tf_op jit(solution)/shard_map/ppermute | solution.py:25
  90.3 11.4 %forward_sublayer0_FW.3 = (bf16[640,1024]{1,0:T(8,128)(2,1)}, bf16[640,2048]{1,0:T(8,128)(2,1)}, bf16[640,2048]{1,0:T(8,128)(2,1)}, bf16[640,1024]{1,0:T(8,128)(2,1)S(1)}) custom-call(bf16[656,1024]{1,0:T(8,128)(2,1)S(1)} %collective-permute-done.18.refs_0_.refs_1_, bf16[656,1024]{1,0:T(8,128)(2,1)S(1)} %get-tuple-element.222.refs_0_.refs_1_, ...), custom_call_target="tpu_custom_call" | custom-call | flops 335544320 | bytes 1710592 | tf_op jit(solution)/shard_map/forward_sublayer0_FW/pallas_call | solution.py:58
  101.7 1.6 collective-permute-start.22
  103.3 6.7 %collective-permute-done.25.refs_2_.refs_3_.refs_6_ = bf16[448,1024]{1,0:T(8,128)(2,1)S(1)} collective-permute-done((bf16[448,1024]{1,0:T(8,128)(2,1)S(1)}, bf16[448,1024]{1,0:T(8,128)(2,1)S(1)}, u32[]{:S(2)}, u32[]{:S(2)}) %collective-permute-start.25) | collective-permute-done | bytes 917536 | tf_op jit(solution)/shard_map/ppermute | solution.py:25
  110.0 9.8 %forward_sublayer1_F.3 = (bf16[448,1024]{1,0:T(8,128)(2,1)}, bf16[448,2048]{1,0:T(8,128)(2,1)}, bf16[448,2048]{1,0:T(8,128)(2,1)}, bf16[448,1024]{1,0:T(8,128)(2,1)}) custom-call(bf16[656,1024]{1,0:T(8,128)(2,1)S(1)} %collective-permute-done.18.refs_0_.refs_1_, bf16[640,1024]{1,0:T(8,128)(2,1)S(1)} %get-tuple-element.225.refs_3_.refs_6_.refs_1_.refs_2_.refs_5_, ...), custom_call_target="tpu_custom_call" | custom-call | flops 234881024 | bytes 1618432 | tf_op jit(solution)/shard_map/forward_sublayer1_F/pallas_call | solution.py:58
  119.8 1.6 collective-permute-start.29
  121.4 16.7 %collective-permute-done.22.refs_4_.refs_7_.refs_3_ = bf16[640,1024]{1,0:T(8,128)(2,1)S(1)} collective-permute-done((bf16[640,1024]{1,0:T(8,128)(2,1)S(1)}, bf16[640,1024]{1,0:T(8,128)(2,1)S(1)}, u32[]{:S(2)}, u32[]{:S(2)}) %collective-permute-start.22) | collective-permute-done | bytes 1310752 | tf_op jit(solution)/shard_map/ppermute | solution.py:25
  138.1 12.3 %forward_sublayer1_OW.3 = (bf16[640,1024]{1,0:T(8,128)(2,1)}, bf16[640,2048]{1,0:T(8,128)(2,1)}, bf16[640,2048]{1,0:T(8,128)(2,1)}, bf16[640,1024]{1,0:T(8,128)(2,1)S(1)}, bf16[192,1024]{1,0:T(8,128)(2,1)}) custom-call(bf16[656,1024]{1,0:T(8,128)(2,1)S(1)} %get-tuple-element.222.refs_0_.refs_1_, ...), custom_call_target="tpu_custom_call" | custom-call | flops 335544320 | bytes 1956352 | tf_op jit(solution)/shard_map/forward_sublayer1_OW/pallas_call | solution.py:58
  151.4 1.5 collective-permute-start.30
  153.0 3.1 compact_kernel.3
  157.8 8.4 %collective-permute-done.30.refs_7_ = bf16[192,1024]{1,0:T(8,128)(2,1)} collective-permute-done((bf16[192,1024]{1,0:T(8,128)(2,1)}, bf16[192,1024]{1,0:T(8,128)(2,1)}, u32[]{:S(2)}, u32[]{:S(2)}) %collective-permute-start.30) | collective-permute-done | bytes 393248 | tf_op jit(solution)/shard_map/ppermute | solution.py:25
  170.1 4.2 %result.3 = (bf16[832,1024]{1,0:T(8,128)(2,1)S(1)}, f32[640,128]{1,0:T(8,128)S(1)}) custom-call(bf16[656,1024]{1,0:T(8,128)(2,1)S(1)} %get-tuple-element.222.refs_0_.refs_1_, bf16[656,1024]{1,0:T(8,128)(2,1)S(1)} %collective-permute-done.18.refs_0_.refs_1_, bf16[448,1024]{1,0:T(8,128)(2,1)S(1)} %copy-done.10, bf16[640,1024]{1,0:T(8,128)(2,1)S(1)} %copy-done.2, ...), custom_call_target="tpu_custom_call" | custom-call | flops 68157440 | bytes 764144 | tf_op jit(solution)/shard_map/result/pallas_call | solution.py:58
  176.2 4.5 %all-to-all-start.6 = ((bf16[8,104,1024]{2,1,0:T(8,128)(2,1)}), bf16[8,104,1024]{2,1,0:T(8,128)(2,1)}, u32[]{:S(2)}, u32[]{:S(2)}) async-start(bf16[8,104,1024]{2,1,0:T(8,128)(2,1)} %bitcast.41), calls=%async_computation.6 | async-start | bytes 3407872 | tf_op jit(solution)/shard_map/all_to_all | solution.py:650
  180.8 1.6 collective-permute-start.24
  187.4 10.4 %backward_sublayer1_OW.3 = (bf16[640,1024]{1,0:T(8,128)(2,1)}, bf16[640,2048]{1,0:T(8,128)(2,1)}, bf16[640,1024]{1,0:T(8,128)(2,1)S(1)}, f32[3,1024]{1,0:T(4,128)S(1)}, f32[1,2048]{1,0:T(1,128)S(1)}) custom-call(bf16[656,1024]{1,0:T(8,128)(2,1)S(1)} %get-tuple-element.222.refs_0_.refs_1_, bf16[656,1024]{1,0:T(8,128)(2,1)S(1)} %collective-permute-done.18.refs_0_.refs_1_, ...), custom_call_target="tpu_custom_call" | custom-call | flops 335544320 | bytes 2039040 | tf_op jit(solution)/shard_map/backward_sublayer1_OW/pallas_call | solution.py:58
  198.9 4.3 %collective-permute-done.24.refs_1_.refs_2_ = bf16[448,1024]{1,0:T(8,128)(2,1)S(1)} collective-permute-done((bf16[448,1024]{1,0:T(8,128)(2,1)}, bf16[448,1024]{1,0:T(8,128)(2,1)S(1)}, u32[]{:S(2)}, u32[]{:S(2)}) %collective-permute-start.24) | collective-permute-done | bytes 917536 | tf_op jit(solution)/shard_map/ppermute | solution.py:25
  203.2 8.8 %backward_sublayer1_F.3 = (bf16[448,1024]{1,0:T(8,128)(2,1)}, bf16[448,2048]{1,0:T(8,128)(2,1)}, bf16[448,1024]{1,0:T(8,128)(2,1)S(1)}, f32[3,1024]{1,0:T(4,128)S(1)}, f32[1,2048]{1,0:T(1,128)S(1)}) custom-call(bf16[656,1024]{1,0:T(8,128)(2,1)S(1)} %collective-permute-done.18.refs_0_.refs_1_, bf16[448,1024]{1,0:T(8,128)(2,1)S(1)} %collective-permute-done.24.refs_1_.refs_2_, ...), custom_call_target="tpu_custom_call" | custom-call | flops 2818572288 | bytes 1676544 | tf_op jit(solution)/shard_map/backward_sublayer1_F/pallas_call | solution.py:58
  212.0 2.4 collective-permute-start.26
  214.4 8.5 %sibling_kernel.6 = (bf16[1024,1024]{1,0:T(8,128)(2,1)S(1)}, bf16[1024,1024]{1,0:T(8,128)(2,1)S(1)}, f32[1,1024]{1,0:T(1,128)S(1)}) custom-call(bf16[640,1024]{1,0:T(8,128)(2,1)} %get-tuple-element.237.refs_0_, bf16[448,1024]{1,0:T(8,128)(2,1)} %get-tuple-element.238.refs_1_, bf16[640,2048]{1,0:T(8,128)(2,1)} %get-tuple-element.239.refs_2_, ...), custom_call_target="tpu_custom_call" | custom-call | flops 285212672 | bytes 1099008 | tf_op jit(solution)/shard_map/sibling_kernel/pallas_call | solution.py:58
  225.5 5.6 %collective-permute-done.27.refs_10_ = bf16[640,1024]{1,0:T(8,128)(2,1)S(1)} collective-permute-done((bf16[640,1024]{1,0:T(8,128)(2,1)S(1)}, bf16[640,1024]{1,0:T(8,128)(2,1)S(1)}, u32[]{:S(2)}, u32[]{:S(2)}) %collective-permute-start.27) | collective-permute-done | bytes 1310752 | tf_op jit(solution)/shard_map/ppermute | solution.py:25
  231.2 12.5 %backward_sublayer0_FW.3 = (bf16[640,1024]{1,0:T(8,128)(2,1)}, bf16[640,2048]{1,0:T(8,128)(2,1)}, bf16[640,1024]{1,0:T(8,128)(2,1)S(1)}, f32[3,1024]{1,0:T(4,128...) custom-call(bf16[656,1024]{1,0:T(8,128)(2,1)S(1)} %collective-permute-done.18.refs_0_.refs_1_, ...), custom_call_target="tpu_custom_call" | custom-call | flops 335544320 | bytes 2309376 | tf_op jit(solution)/shard_map/backward_sublayer0_FW/pallas_call | solution.py:58
  244.3 2.5 collective-permute-start.28
  246.8 4.0 %collective-permute-done.26.refs_5_ = bf16[448,1024]{1,0:T(8,128)(2,1)S(1)} collective-permute-done((bf16[448,1024]{1,0:T(8,128)(2,1)S(1)}, bf16[448,1024]{1,0:T(8,128)(2,1)S(1)}, u32[]{:S(2)}, u32[]{:S(2)}) %collective-permute-start.26) | collective-permute-done | bytes 917536 | tf_op jit(solution)/shard_map/ppermute | solution.py:25
  250.8 9.7 %backward_sublayer0_E.3 = (bf16[448,1024]{1,0:T(8,128)(2,1)}, bf16[448,2048]{1,0:T(8,128)(2,1)}, bf16[448,1024]{1,0:T(8,128)(2,1)S(1)}, f32[3,1024]{1,0:T(4,128)...) custom-call(bf16[656,1024]{1,0:T(8,128)(2,1)S(1)} %get-tuple-element.222.refs_0_.refs_1_, ...), custom_call_target="tpu_custom_call" | custom-call | flops 7516192768 | bytes 1930496 | tf_op jit(solution)/shard_map/backward_sublayer0_E/pallas_call | solution.py:58
  260.6 8.6 %sibling_kernel.7 = (bf16[1024,1024]{1,0:T(8,128)(2,1)S(1)}, bf16[1024,1024]{1,0:T(8,128)(2,1)S(1)}, f32[1,1024]{1,0:T(1,128)S(1)}) custom-call(bf16[448,1024]{1,0:T(8,128)(2,1)} %get-tuple-element.254.refs_0_, bf16[640,1024]{1,0:T(8,128)(2,1)} %get-tuple-element.255.refs_1_, bf16[448,2048]{1,0:T(8,128)(2,1)} %get-tuple-element.256.refs_2_, ...), custom_call_target="tpu_custom_call" | custom-call | flops 285212672 | bytes 1099008 | tf_op jit(solution)/shard_map/sibling_kernel/pallas_call | solution.py:58
  270.5 1.3 copy-done.49
  271.8 4.5 %collective-permute-done.28.refs_7_ = bf16[640,1024]{1,0:T(8,128)(2,1)S(1)} collective-permute-done((bf16[640,1024]{1,0:T(8,128)(2,1)S(1)}, bf16[640,1024]{1,0:T(8,128)(2,1)S(1)}, u32[]{:S(2)}, u32[]{:S(2)}) %collective-permute-start.28) | collective-permute-done | bytes 1310752 | tf_op jit(solution)/shard_map/ppermute | solution.py:25
  276.3 3.5 %row_grad.3 = (bf16[832,1024]{1,0:T(8,128)(2,1)S(1)}, f32[1,1024]{1,0:T(1,128)S(1)}) custom-call(bf16[656,1024]{1,0:T(8,128)(2,1)S(1)} %get-tuple-element.222.refs_0_.refs_1_, bf16[656,1024]{1,0:T(8,128)(2,1)S(1)} %collective-permute-done.18.refs_0_.refs_1_, bf16[448,1024]{1,0:T(8,128)(2,1)S(1)} %get-tuple-element.235.refs_2_, ...), custom_call_target="tpu_custom_call" | custom-call | flops 68157440 | bytes 682448 | tf_op jit(solution)/shard_map/row_grad/pallas_call | solution.py:58
  281.1 5.7 %all-to-all-start.7 = ((bf16[8,104,1024]{2,1,0:T(8,128)(2,1)}), bf16[8,104,1024]{2,1,0:T(8,128)(2,1)S(1)}, u32[]{:S(2)}, u32[]{:S(2)}) async-start(bf16[8,104,1024]{2,1,0:T(8,128)(2,1)} %bitcast.40), calls=%async_computation.7 | async-start | bytes 3407872 | tf_op jit(solution)/shard_map/all_to_all | solution.py:687
  288.0 1.5 marks.3.refs_5_
  289.5 1.6 collective-permute-done.38.refs_12_
  291.6 2.6 collective-permute-done.37.refs_11_
  295.6 11.1 %own_grads_sublayer1.3 = (f32[2,1024,1024]{2,1,0:T(8,128)}, f32[2,1024,1024]{2,1,0:T(8,128)}, f32[1,1024]{1,0:T(1,128)S(1)}) custom-call(bf16[640,1024]{1,0:T(8,128)(2,1)} %get-tuple-element.237.refs_0_, bf16[448,1024]{1,0:T(8,128)(2,1)} %get-tuple-element.238.refs_1_, bf16[640,2048]{1,0:T(8,128)(2,1)} %get-tuple-element.239.refs_2_, ...), custom_call_target="tpu_custom_call" | custom-call | flops 285212672 | bytes 2147840 | tf_op jit(solution)/shard_map/own_grads_sublayer1/pallas_call | solution.py:58
  306.6 1.6 collective-permute-start.32
  308.2 4.7 %unpack_kernel.6 = bf16[640,1024]{1,0:T(8,128)(2,1)} custom-call(s32[1,640]{1,0:T(1,128)S(1)} %copy-done.72, bf16[832,1024]{1,0:T(8,128)(2,1)} %bitcast.23.refs_0_.refs_1_, bf16[640,1024]{1,0:T(8,128)(2,1)S(1)} %copy-done.56), custom_call_target="tpu_custom_call" | custom-call | flops 68157440 | bytes 270496 | tf_op jit(solution)/shard_map/unpack_kernel/pallas_call | solution.py:58
  315.0 11.5 %own_grads_sublayer0.3 = (f32[2,1024,1024]{2,1,0:T(8,128)}, f32[2,1024,1024]{2,1,0:T(8,128)}, f32[1,1024]{1,0:T(1,128)S(1)}) custom-call(bf16[448,1024]{1,0:T(8,128)(2,1)} %get-tuple-element.254.refs_0_, bf16[640,1024]{1,0:T(8,128)(2,1)} %get-tuple-element.255.refs_1_, ...), custom_call_target="tpu_custom_call", output_to_operand_aliasing={{0}: (13, {}), {1}: (14, {})} | custom-call | flops 285212672 | bytes 3196416 | tf_op jit(solution)/shard_map/own_grads_sublayer0/pallas_call | solution.py:58
  327.2 3.6 %unpack_kernel.7 = bf16[640,1024]{1,0:T(8,128)(2,1)S(1)} custom-call(s32[1,640]{1,0:T(1,128)S(1)} %copy-done.72, bf16[832,1024]{1,0:T(8,128)(2,1)S(1)} %bitcast.37, bf16[640,1024]{1,0:T(8,128)(2,1)} %refs_2_.3), custom_call_target="tpu_custom_call" | custom-call | flops 68157440 | bytes 270496 | tf_op jit(solution)/shard_map/unpack_kernel/pallas_call | solution.py:58
  330.8 2.3 conditional.1
  (133 shorter events, 32.9 us)
Async XLA Ops:
  6.3 21.4 %copy-start.71 = (s32[1,640]{1,0:T(1,128)}, s32[1,640]{1,0:T(1,128)S(1)}, u32[]{:S(2)}) copy-start(s32[1,640]{1,0:T(1,128)S(1)} %get-tuple-element.221.refs_0_) | copy-start | bytes 7684
  6.3 8.6 %copy-start.78 = (bf16[1,256]{1,0:T(2,128)(2,1)S(1)}, bf16[1,256]{1,0:T(2,128)(2,1)}, u32[]{:S(2)}) copy-start(bf16[1,256]{1,0:T(2,128)(2,1)} %param.16) | copy-start | bytes 1540
  6.3 8.6 %copy-start.79 = (bf16[1,2,256]{2,1,0:T(2,128)(2,1)S(1)}, bf16[1,2,256]{2,1,0:T(2,128)(2,1)}, u32[]{:S(2)}) copy-start(bf16[1,2,256]{2,1,0:T(2,128)(2,1)} %param.17) | copy-start | bytes 3076
  6.3 8.6 %copy-start.80 = (bf16[1,2,256]{2,1,0:T(2,128)(2,1)S(1)}, bf16[1,2,256]{2,1,0:T(2,128)(2,1)}, u32[]{:S(2)}) copy-start(bf16[1,2,256]{2,1,0:T(2,128)(2,1)} %param.18) | copy-start | bytes 3076
  6.3 8.6 %copy-start.81 = (bf16[1,2,256]{2,1,0:T(2,128)(2,1)S(1)}, bf16[1,2,256]{2,1,0:T(2,128)(2,1)}, u32[]{:S(2)}) copy-start(bf16[1,2,256]{2,1,0:T(2,128)(2,1)} %param.22) | copy-start | bytes 3076
  6.3 21.4 %copy-start.58 = (bf16[640,1024]{1,0:T(8,128)(2,1)S(1)}, bf16[640,1024]{1,0:T(8,128)(2,1)}, u32[]{:S(2)}) copy-start(bf16[640,1024]{1,0:T(8,128)(2,1)} %refs_2_.3) | copy-start | bytes 3932164
  6.3 47.2 %all-to-all-start.4 = ((bf16[8,104,1024]{2,1,0:T(8,128)(2,1)}), bf16[8,104,1024]{2,1,0:T(8,128)(2,1)S(1)}, u32[]{:S(2)}, u32[]{:S(2)}) async-start(bf16[8,104,1024]{2,1,0:T(8,128)(2,1)} %bitcast.74), calls=%async_computation.4 | async-start | bytes 3407872 | tf_op jit(solution)/shard_map/all_to_all | solution.py:737
  13.7 51.6 %collective-permute-start.20 = (bf16[2,1024,1024]{2,1,0:T(8,128)(2,1)}, bf16[2,1024,1024]{2,1,0:T(8,128)(2,1)}, u32[]{:S(2)}, u32[]{:S(2)}) collective-permute-start(bf16[2,1024,1024]{2,1,0:T(8,128)(2,1)} %bitcast.50), channel_id=1, source_target_pairs={{0,1},{1,0},{2,3},{3,2},{4,5},{5,4},{6,7},{7,6},{8,9},{9,8},{10,11... | collective-permute-start | bytes 12582920 | tf_op jit(solution)/shard_map/ppermute | solution.py:25
  13.7 51.6 %collective-permute-start.21 = (bf16[2,1024,1024]{2,1,0:T(8,128)(2,1)}, bf16[2,1024,1024]{2,1,0:T(8,128)(2,1)}, u32[]{:S(2)}, u32[]{:S(2)}) collective-permute-start(bf16[2,1024,1024]{2,1,0:T(8,128)(2,1)} %bitcast.60), channel_id=1, source_target_pairs={{0,1},{1,0},{2,3},{3,2},{4,5},{5,4},{6,7},{7,6},{8,9},{9,8},{10,11... | collective-permute-start | bytes 12582920 | tf_op jit(solution)/shard_map/ppermute | solution.py:25
  57.8 32.5 %collective-permute-start.18 = (bf16[656,1024]{1,0:T(8,128)(2,1)S(1)}, bf16[656,1024]{1,0:T(8,128)(2,1)S(1)}, u32[]{:S(2)}, u32[]{:S(2)}) collective-permute-start(bf16[656,1024]{1,0:T(8,128)(2,1)S(1)} %get-tuple-element.222.refs_0_.refs_1_), channel_id=1, source_target_pairs={{0,2},{1,3},{2,0},{3,1},{4,6},{5,7},{6,4},{7,5},{8,10},{9,11},{10,... | collective-permute-start | bytes 4030472 | tf_op jit(solution)/shard_map/ppermute | solution.py:25
  59.4 4.7 %copy-start.28 = (bf16[1,2,1024]{2,1,0:T(2,128)(2,1)S(1)}, bf16[1,2,1024]{2,1,0:T(2,128)(2,1)}, u32[]{:S(2)}) copy-start(bf16[1,2,1024]{2,1,0:T(2,128)(2,1)} %param.20) | copy-start | bytes 12292
  59.4 93.6 %all-to-all-start.5 = ((bf16[8,104,1024]{2,1,0:T(8,128)(2,1)}), bf16[8,104,1024]{2,1,0:T(8,128)(2,1)}, u32[]{:S(2)}, u32[]{:S(2)}) async-start(bf16[8,104,1024]{2,1,0:T(8,128)(2,1)} %bitcast.70), calls=%async_computation.5 | async-start | bytes 3407872 | tf_op jit(solution)/shard_map/all_to_all | solution.py:612
  64.1 1.2 collective-permute-start.19
  74.0 64.1 %copy-start.9 = (bf16[448,1024]{1,0:T(8,128)(2,1)}, bf16[448,1024]{1,0:T(8,128)(2,1)S(1)}, u32[]{:S(2)}) copy-start(bf16[448,1024]{1,0:T(8,128)(2,1)S(1)} %get-tuple-element.224.refs_9_.refs_2_.refs_5_) | copy-start | bytes 2752516
  74.0 36.0 %collective-permute-start.25 = (bf16[448,1024]{1,0:T(8,128)(2,1)S(1)}, bf16[448,1024]{1,0:T(8,128)(2,1)S(1)}, u32[]{:S(2)}, u32[]{:S(2)}) collective-permute-start(bf16[448,1024]{1,0:T(8,128)(2,1)S(1)} %get-tuple-element.224.refs_9_.refs_2_.refs_5_), channel_id=1, source_target_pairs={{0,2},{1,3},{2,0},{3,1},{4,6},{5,7},{6,4},{7,5},{8,10},{9,11},{10,... | collective-permute-start | bytes 2752520 | tf_op jit(solution)/shard_map/ppermute | solution.py:25
  101.7 36.4 %copy-start.1 = (bf16[640,1024]{1,0:T(8,128)(2,1)}, bf16[640,1024]{1,0:T(8,128)(2,1)S(1)}, u32[]{:S(2)}) copy-start(bf16[640,1024]{1,0:T(8,128)(2,1)S(1)} %get-tuple-element.225.refs_3_.refs_6_.refs_1_.refs_2_.refs_5_) | copy-start | bytes 3932164
  101.7 36.4 %collective-permute-start.22 = (bf16[640,1024]{1,0:T(8,128)(2,1)S(1)}, bf16[640,1024]{1,0:T(8,128)(2,1)S(1)}, u32[]{:S(2)}, u32[]{:S(2)}) collective-permute-start(bf16[640,1024]{1,0:T(8,128)(2,1)S(1)} %get-tuple-element.225.refs_3_.refs_6_.refs_1_.refs_2_.refs_5_), channel_id=1, source_target_pairs={{0,2},{1,3},{2,0},{3,1},{4,6},{5,7},{6,4},{7,5},{8,10},{9,11},{10,... | collective-permute-start | bytes 3932168 | tf_op jit(solution)/shard_map/ppermute | solution.py:25
  110.0 9.8 %copy-start.12 = (bf16[448,1024]{1,0:T(8,128)(2,1)}, bf16[448,1024]{1,0:T(8,128)(2,1)S(1)}, u32[]{:S(2)}) copy-start(bf16[448,1024]{1,0:T(8,128)(2,1)S(1)} %collective-permute-done.25.refs_2_.refs_3_.refs_6_) | copy-start | bytes 2752516
  119.8 38.0 %collective-permute-start.29 = (bf16[448,1024]{1,0:T(8,128)(2,1)}, bf16[448,1024]{1,0:T(8,128)(2,1)}, u32[]{:S(2)}, u32[]{:S(2)}) collective-permute-start(bf16[448,1024]{1,0:T(8,128)(2,1)} %get-tuple-element.251), channel_id=1, source_target_pairs={{0,2},{1,3},{2,0},{3,1},{4,6},{5,7},{6,4},{7,5},{8,10},{9,11},{10,... | collective-permute-start | bytes 2752520 | tf_op jit(solution)/shard_map/ppermute | solution.py:25
  138.1 12.3 %copy-start.5 = (bf16[640,1024]{1,0:T(8,128)(2,1)}, bf16[640,1024]{1,0:T(8,128)(2,1)S(1)}, u32[]{:S(2)}) copy-start(bf16[640,1024]{1,0:T(8,128)(2,1)S(1)} %collective-permute-done.22.refs_4_.refs_7_.refs_3_) | copy-start | bytes 3932164
  151.4 14.8 %collective-permute-start.30 = (bf16[192,1024]{1,0:T(8,128)(2,1)}, bf16[192,1024]{1,0:T(8,128)(2,1)}, u32[]{:S(2)}, u32[]{:S(2)}) collective-permute-start(bf16[192,1024]{1,0:T(8,128)(2,1)} %get-tuple-element.226.refs_2_), channel_id=1, source_target_pairs={{0,2},{1,3},{2,0},{3,1},{4,6},{5,7},{6,4},{7,5},{8,10},{9,11},{10,... | collective-permute-start | bytes 1179656 | tf_op jit(solution)/shard_map/ppermute | solution.py:25
  153.0 13.3 %copy-start.2 = (bf16[640,1024]{1,0:T(8,128)(2,1)S(1)}, bf16[640,1024]{1,0:T(8,128)(2,1)}, u32[]{:S(2)}) copy-start(bf16[640,1024]{1,0:T(8,128)(2,1)} %copy-done.1) | copy-start | bytes 3932164
  156.1 18.2 %copy-start.18 = (bf16[448,1024]{1,0:T(8,128)(2,1)}, bf16[448,1024]{1,0:T(8,128)(2,1)S(1)}, u32[]{:S(2)}) copy-start(bf16[448,1024]{1,0:T(8,128)(2,1)S(1)} %get-tuple-element.227.refs_2_.refs_1_.refs_8_) | copy-start | bytes 2752516
  156.1 26.3 %collective-permute-start.23 = (bf16[192,1024]{1,0:T(8,128)(2,1)S(1)}, bf16[192,1024]{1,0:T(8,128)(2,1)S(1)}, u32[]{:S(2)}, u32[]{:S(2)}) collective-permute-start(bf16[192,1024]{1,0:T(8,128)(2,1)S(1)} %get-tuple-element.228.refs_3_.refs_9_), channel_id=1, source_target_pairs={{0,2},{1,3},{2,0},{3,1},{4,6},{5,7},{6,4},{7,5},{8,10},{9,11},{10,... | collective-permute-start | bytes 1179656 | tf_op jit(solution)/shard_map/ppermute | solution.py:25
  176.2 104.8 %all-to-all-start.6 = ((bf16[8,104,1024]{2,1,0:T(8,128)(2,1)}), bf16[8,104,1024]{2,1,0:T(8,128)(2,1)}, u32[]{:S(2)}, u32[]{:S(2)}) async-start(bf16[8,104,1024]{2,1,0:T(8,128)(2,1)} %bitcast.41), calls=%async_computation.6 | async-start | bytes 3407872 | tf_op jit(solution)/shard_map/all_to_all | solution.py:650
  180.8 22.4 %collective-permute-start.24 = (bf16[448,1024]{1,0:T(8,128)(2,1)}, bf16[448,1024]{1,0:T(8,128)(2,1)S(1)}, u32[]{:S(2)}, u32[]{:S(2)}) collective-permute-start(bf16[448,1024]{1,0:T(8,128)(2,1)} %copy-done.18), channel_id=1, source_target_pairs={{0,2},{1,3},{2,0},{3,1},{4,6},{5,7},{6,4},{7,5},{8,10},{9,11},{10,... | collective-permute-start | bytes 2752520 | tf_op jit(solution)/shard_map/ppermute | solution.py:25
  187.4 15.8 %copy-start.4 = (bf16[640,1024]{1,0:T(8,128)(2,1)S(1)}, bf16[640,1024]{1,0:T(8,128)(2,1)}, u32[]{:S(2)}) copy-start(bf16[640,1024]{1,0:T(8,128)(2,1)} %copy-done.1) | copy-start | bytes 3932164
  187.4 15.8 %copy-start.13 = (bf16[448,1024]{1,0:T(8,128)(2,1)S(1)}, bf16[448,1024]{1,0:T(8,128)(2,1)}, u32[]{:S(2)}) copy-start(bf16[448,1024]{1,0:T(8,128)(2,1)} %copy-done.12) | copy-start | bytes 2752516
  198.4 32.7 %collective-permute-start.27 = (bf16[640,1024]{1,0:T(8,128)(2,1)S(1)}, bf16[640,1024]{1,0:T(8,128)(2,1)S(1)}, u32[]{:S(2)}, u32[]{:S(2)}) collective-permute-start(bf16[640,1024]{1,0:T(8,128)(2,1)S(1)} %get-tuple-element.230.refs_4_.refs_9_), channel_id=1, source_target_pairs={{0,2},{1,3},{2,0},{3,1},{4,6},{5,7},{6,4},{7,5},{8,10},{9,11},{10,... | collective-permute-start | bytes 3932168 | tf_op jit(solution)/shard_map/ppermute | solution.py:25
  212.0 38.8 %collective-permute-start.26 = (bf16[448,1024]{1,0:T(8,128)(2,1)S(1)}, bf16[448,1024]{1,0:T(8,128)(2,1)S(1)}, u32[]{:S(2)}, u32[]{:S(2)}) collective-permute-start(bf16[448,1024]{1,0:T(8,128)(2,1)S(1)} %get-tuple-element.233.refs_8_), channel_id=1, source_target_pairs={{0,2},{1,3},{2,0},{3,1},{4,6},{5,7},{6,4},{7,5},{8,10},{9,11},{10,... | collective-permute-start | bytes 2752520 | tf_op jit(solution)/shard_map/ppermute | solution.py:25
  214.4 16.7 %copy-start.8 = (bf16[640,1024]{1,0:T(8,128)(2,1)S(1)}, bf16[640,1024]{1,0:T(8,128)(2,1)}, u32[]{:S(2)}) copy-start(bf16[640,1024]{1,0:T(8,128)(2,1)} %copy-done.5) | copy-start | bytes 3932164
  231.2 19.7 %copy-start.20 = (bf16[448,1024]{1,0:T(8,128)(2,1)S(1)}, bf16[448,1024]{1,0:T(8,128)(2,1)}, u32[]{:S(2)}) copy-start(bf16[448,1024]{1,0:T(8,128)(2,1)} %copy-done.18) | copy-start | bytes 2752516
  244.3 32.0 %collective-permute-start.28 = (bf16[640,1024]{1,0:T(8,128)(2,1)S(1)}, bf16[640,1024]{1,0:T(8,128)(2,1)S(1)}, u32[]{:S(2)}, u32[]{:S(2)}) collective-permute-start(bf16[640,1024]{1,0:T(8,128)(2,1)S(1)} %get-tuple-element.247.refs_3_), channel_id=1, source_target_pairs={{0,2},{1,3},{2,0},{3,1},{4,6},{5,7},{6,4},{7,5},{8,10},{9,11},{10,... | collective-permute-start | bytes 3932168 | tf_op jit(solution)/shard_map/ppermute | solution.py:25
  260.5 15.8 %copy-start.26 = (f32[640,128]{1,0:T(8,128)S(1)}, f32[640,128]{1,0:T(8,128)}, u32[]{:S(2)}) copy-start(f32[640,128]{1,0:T(8,128)} %copy-done.25) | copy-start | bytes 983044
  281.1 46.1 %all-to-all-start.7 = ((bf16[8,104,1024]{2,1,0:T(8,128)(2,1)}), bf16[8,104,1024]{2,1,0:T(8,128)(2,1)S(1)}, u32[]{:S(2)}, u32[]{:S(2)}) async-start(bf16[8,104,1024]{2,1,0:T(8,128)(2,1)} %bitcast.40), calls=%async_computation.7 | async-start | bytes 3407872 | tf_op jit(solution)/shard_map/all_to_all | solution.py:687
  286.8 2.7 copy-start.36
  286.8 4.4 %collective-permute-start.36 = (bf16[1024,1024]{1,0:T(8,128)(2,1)}, bf16[1024,1024]{1,0:T(8,128)(2,1)S(1)}, u32[]{:S(2)}, u32[]{:S(2)}) collective-permute-start(bf16[1024,1024]{1,0:T(8,128)(2,1)} %copy-done.50), channel_id=1, source_target_pairs={{0,1},{1,0},{2,3},{3,2},{4,5},{5,4},{6,7},{7,6},{8,9},{9,8},{10,11... | collective-permute-start | bytes 6291464 | tf_op jit(solution)/shard_map/ppermute | solution.py:25
  286.9 7.4 %collective-permute-start.37 = (bf16[1024,1024]{1,0:T(8,128)(2,1)}, bf16[1024,1024]{1,0:T(8,128)(2,1)S(1)}, u32[]{:S(2)}, u32[]{:S(2)}) collective-permute-start(bf16[1024,1024]{1,0:T(8,128)(2,1)} %copy-done.47), channel_id=1, source_target_pairs={{0,1},{1,0},{2,3},{3,2},{4,5},{5,4},{6,7},{7,6},{8,9},{9,8},{10,11... | collective-permute-start | bytes 6291464 | tf_op jit(solution)/shard_map/ppermute | solution.py:25
  287.4 25.5 %collective-permute-start.33 = (bf16[1024,1024]{1,0:T(8,128)(2,1)}, bf16[1024,1024]{1,0:T(8,128)(2,1)S(1)}, u32[]{:S(2)}, u32[]{:S(2)}) collective-permute-start(bf16[1024,1024]{1,0:T(8,128)(2,1)} %copy-done.49), channel_id=1, source_target_pairs={{0,1},{1,0},{2,3},{3,2},{4,5},{5,4},{6,7},{7,6},{8,9},{9,8},{10,11... | collective-permute-start | bytes 6291464 | tf_op jit(solution)/shard_map/ppermute | solution.py:25
  287.5 25.5 %collective-permute-start.34 = (bf16[1024,1024]{1,0:T(8,128)(2,1)}, bf16[1024,1024]{1,0:T(8,128)(2,1)S(1)}, u32[]{:S(2)}, u32[]{:S(2)}) collective-permute-start(bf16[1024,1024]{1,0:T(8,128)(2,1)} %copy-done.48), channel_id=1, source_target_pairs={{0,1},{1,0},{2,3},{3,2},{4,5},{5,4},{6,7},{7,6},{8,9},{9,8},{10,11... | collective-permute-start | bytes 6291464 | tf_op jit(solution)/shard_map/ppermute | solution.py:25
  287.9 3.1 collective-permute-start.38
  291.0 15.6 %collective-permute-start.31 = (f32[8,1024]{1,0:T(8,128)S(1)}, f32[8,1024]{1,0:T(8,128)S(1)}, u32[]{:S(2)}, u32[]{:S(2)}) collective-permute-start(f32[8,1024]{1,0:T(8,128)S(1)} %columns_kernel.3.refs_0_), channel_id=1, source_target_pairs={{0,1},{1,0},{2,3},{3,2},{4,5},{5,4},{6,7},{7,6},{8,9},{9,8},{10,11... | collective-permute-start | bytes 98312 | tf_op jit(solution)/shard_map/ppermute | solution.py:25
  291.2 17.0 %copy-start.56 = (bf16[640,1024]{1,0:T(8,128)(2,1)S(1)}, bf16[640,1024]{1,0:T(8,128)(2,1)}, u32[]{:S(2)}) copy-start(bf16[640,1024]{1,0:T(8,128)(2,1)} %refs_2_.2) | copy-start | bytes 3932164
  291.2 17.0 %copy-start.72 = (s32[1,640]{1,0:T(1,128)S(1)}, s32[1,640]{1,0:T(1,128)}, u32[]{:S(2)}) copy-start(s32[1,640]{1,0:T(1,128)} %copy-done.71) | copy-start | bytes 7684
  291.2 3.0 copy-start.65
  291.2 21.7 %collective-permute-start.35 = (f32[1,1024]{1,0:T(1,128)S(1)}, f32[1,1024]{1,0:T(1,128)S(1)}, u32[]{:S(2)}, u32[]{:S(2)}) collective-permute-start(f32[1,1024]{1,0:T(1,128)S(1)} %get-tuple-element.264.refs_10_), channel_id=1, source_target_pairs={{0,1},{1,0},{2,3},{3,2},{4,5},{5,4},{6,7},{7,6},{8,9},{9,8},{10,11... | collective-permute-start | bytes 12296 | tf_op jit(solution)/shard_map/ppermute | solution.py:25
  306.6 19.8 %collective-permute-start.32 = (f32[8,1024]{1,0:T(8,128)S(1)}, f32[8,1024]{1,0:T(8,128)S(1)}, u32[]{:S(2)}, u32[]{:S(2)}) collective-permute-start(f32[8,1024]{1,0:T(8,128)S(1)} %add_kernel.3.refs_1_), channel_id=1, source_target_pairs={{0,2},{1,3},{2,0},{3,1},{4,6},{5,7},{6,4},{7,5},{8,10},{9,11},{10,... | collective-permute-start | bytes 98312 | tf_op jit(solution)/shard_map/ppermute | solution.py:25
  327.2 3.6 %copy-start.52 = (bf16[832,1024]{1,0:T(8,128)(2,1)S(1)}, bf16[832,1024]{1,0:T(8,128)(2,1)}, u32[]{:S(2)}) copy-start(bf16[832,1024]{1,0:T(8,128)(2,1)} %pack_kernel.1.refs_2_) | copy-start | bytes 5111812
  (28 other events, 37.1 us)
